TPU v7x, 32 devices: a whole 2x2x4 slice. The times are simulated.
32 devices in a mesh: group: 2 (over y), dom: 16 (over z, x, core).
Axes of the slice: x: 2, y: 2, z: 4, core: 2. Of those that a mesh axis runs over, the one named last changes fastest.
Arguments:
- prior_basis: bfloat16 [128, 128, 128], P(('group', 'dom'))
- section_state: bfloat16 [128, 128], P(('group', 'dom'))
- source: float32 [128, 128], P(('group', 'dom')), may hold values from -6 to 6
- diag_blocks: bfloat16 [128, 128, 128], P(('group', 'dom'))
- coupling: bfloat16 [128, 4, 128, 128], P(('group', 'dom')), may hold values from -0.125 to 0.125
- neighbour_index: int32 [128, 4], P(('group', 'dom')), may hold values from 0 to 11, as said below
- slot_count: int32 [128], P(('group', 'dom')), may hold values from 2 to 4, as said below
Outputs:
- new_basis: bfloat16 [128, 128, 128], P(('group', 'dom'))
- image_basis: bfloat16 [128, 128, 128], P(('group', 'dom'))
- initial_guess: float32 [128, 128], P(('group', 'dom'))
- start_residual: float32 [128, 128], P(('group', 'dom'))
Inputs may be any that keep to these rules, and one draw needn't show every extreme that they name: `neighbour_index`: an entry of the extended block list of the block's own partition; slot 0 always names a block from the lower neighbour partition and slot 1 one from the upper, and every shared block is named by some slot. Slots from slot_count on are padding and are ignored; the first face block of every partition uses all 4 slots.
All inputs are finite; a program needn't handle non-finite values.
Results may differ from a plain program's by a relative error of at most 0.0052.
Values may be sent and summed in bfloat16 or wider, within the bound.
No kernel may reach another device: no remote copies, remote signals or barrier semaphores. Data moves between devices by JAX's collectives and lax.ppermute only.
A program may use at most 64 MiB of HBM per device.

v0:
```python
import jax
import jax.numpy as jnp
from jax import lax
from jax.sharding import PartitionSpec as P

HALO = 4


section_step = 0.25
highest = lax.Precision.HIGHEST


def padded(array, sides, width):
    for axis, dim in sides:
        devices, length = (lax.axis_size(axis), array.shape[dim])
        up = [(i, (i + 1) % devices) for i in range(devices - 1)]
        down = [(j, i) for i, j in up]
        last = lax.slice_in_dim(array, length - width, length, axis=dim)
        initial = lax.slice_in_dim(array, 0, width, axis=dim)
        before = lax.ppermute(last, axis, up)
        after = lax.ppermute(initial, axis, down)
        array = jnp.concatenate([before, array, after], axis=dim)
    return array


def cholesky_inverse(gram):
    order = gram.shape[0]
    positions = jnp.arange(order, dtype=jnp.int32)

    def factor_step(column, lower):
        row_part = lower[column, :]
        remaining = gram[:, column] - jnp.dot(lower, row_part, precision=highest)
        pivot = jnp.sqrt(remaining[column])
        new_column = jnp.where(positions >= column, remaining / pivot, jnp.zeros_like(remaining))
        return lower.at[:, column].set(new_column)

    lower = lax.fori_loop(0, order, factor_step, jnp.zeros_like(gram))
    identity = (positions[:, None] == positions[None, :]).astype(gram.dtype)

    def solve_step(row, solved):
        row_values = (identity[row] - jnp.dot(lower[row, :], solved, precision=highest)) / lower[
            row, row
        ]
        return solved.at[row].set(row_values)

    lower_inverse = lax.fori_loop(0, order, solve_step, jnp.zeros_like(gram))
    return lower_inverse.T


def slot_apply(extended, local_blocks, diagonal, couple, neighbours, live_count):
    summed = jnp.einsum(
        "nab,nb...->na...", diagonal, local_blocks, preferred_element_type=jnp.float32
    )
    for neighbour_slot in range(couple.shape[1]):
        picked = jnp.take(extended, neighbours[:, neighbour_slot], axis=0)
        alive_mask = (live_count > neighbour_slot).astype(jnp.float32)
        alive_mask = alive_mask.reshape(alive_mask.shape + (1,) * (local_blocks.ndim - 1))
        summed = summed + alive_mask * jnp.einsum(
            "nab,nb...->na...",
            couple[:, neighbour_slot],
            picked,
            preferred_element_type=jnp.float32,
        )
    return summed


def global_sum(values):
    return lax.psum((values[0], values[1]), ("group", "dom"))


def body(prior_basis, section_state, source, diag_blocks, coupling, neighbour_index, slot_count):
    columns = prior_basis.shape[2]
    basis_ext = padded(prior_basis, (("dom", 0),), HALO)
    state_ext = padded(section_state, (("dom", 0),), HALO)
    state_image = slot_apply(
        state_ext, section_state, diag_blocks, coupling, neighbour_index, slot_count
    )
    rhs = section_state.astype(jnp.float32) + section_step * (source - state_image)
    image = slot_apply(
        basis_ext, prior_basis, diag_blocks, coupling, neighbour_index, slot_count
    ).astype(jnp.bfloat16)
    rows_total = float(
        prior_basis.shape[0] * prior_basis.shape[1] * lax.axis_size("group") * lax.axis_size("dom")
    )
    flat_image = image.reshape(-1, columns)
    flat_rhs = rhs.reshape(-1)
    gram_part = lax.dot_general(
        flat_image, flat_image, (((0,), (0,)), ((), ())), preferred_element_type=jnp.float32
    )
    moment_part = jnp.dot(flat_rhs, flat_image.astype(jnp.float32), precision=highest)
    gram_sum, moment = global_sum((gram_part, moment_part))
    inverse = cholesky_inverse(gram_sum / rows_total)
    image_q = jnp.dot(flat_image.astype(jnp.float32), inverse, precision=highest)
    coefficients = jnp.dot(moment, inverse, precision=highest) / rows_total
    basis_q = jnp.dot(
        prior_basis.reshape(-1, columns).astype(jnp.float32), inverse, precision=highest
    )
    initial_guess = jnp.dot(basis_q, coefficients, precision=highest)
    start_residual = flat_rhs - jnp.dot(image_q, coefficients, precision=highest)
    return (
        basis_q.astype(jnp.bfloat16).reshape(prior_basis.shape),
        image_q.astype(jnp.bfloat16).reshape(prior_basis.shape),
        initial_guess.reshape(section_state.shape),
        start_residual.reshape(section_state.shape),
    )


def solution(mesh):
    placed = (
        P(("group", "dom"), None, None),
        P(("group", "dom"), None),
        P(("group", "dom"), None),
        P(("group", "dom"), None, None),
        P(("group", "dom"), None, None, None),
        P(("group", "dom"), None),
        P(("group", "dom")),
    )
    return jax.shard_map(
        body,
        mesh=mesh,
        in_specs=placed,
        out_specs=(
            P(("group", "dom"), None, None),
            P(("group", "dom"), None, None),
            P(("group", "dom"), None),
            P(("group", "dom"), None),
        ),
        check_vma=False,
    )
```

profile of v0, /device:TPU:0, one launch (start us, length us, event | category | flops | bytes accessed | tf_op | source)
XLA Modules:
  0.0 914.6 jit_solution(2797229289684479329)
XLA Ops:
  7.2 2.5 collective-permute-start
  11.0 5.1 collective-permute-start.2
  30.7 43.9 %psum.15 = f32[128]{0:T(128)S(1)} all-reduce(f32[128]{0:T(128)S(1)} %convolution_bitcast_fusion.4), channel_id=1, replica_groups=mesh['group'=2,'dom'=16] {'group','dom'}, use_global_device_ids=true, to_apply=%region_7.10 | all-reduce | flops 128 | bytes 1024 | tf_op jit(solution)/shard_map/psum | solution.py:68
  74.6 78.3 %all-reduce.2.cloned.1.call-done = f32[128,128]{1,0:T(8,128)} async-done(((f32[128,128]{1,0:T(8,128)}), f32[128,128]{1,0:T(8,128)}) %all-reduce.2.cloned.1.call-update) | async-done | bytes 65552 | tf_op jit(solution)/shard_map/psum | solution.py:68
  153.9 392.3 %while.30 = (s32[]{:T(128)}, f32[128,128]{0,1:T(8,128)S(1)}, f32[128,128]{0,1:T(8,128)S(1)}, s32[]{:T(128)}, s32[1]{0:T(128)}, /*index=5*/s32[]{:T(128)}) while((s32[]{:T(128)}, f32[128,128]{0,1:T(8,128)S(1)}, f32[128,128]{0,1:T(8,128)S(1)}, s32[]{:T(128)}, s32[1]{0:T(128)}, /*index=5*/s32[]{:T(128)}) %tuple.94), condition=%wide.region_3.5_spmd.clone, body=%wide.region_1.0_spmd.clone.sunk | while | flops 197261 | bytes 72814 | solution.py:37
  546.9 356.8 %while.29 = (s32[]{:T(128)}, f32[128,128]{1,0:T(8,128)S(1)}, f32[128,128]{1,0:T(8,128)S(1)}, f32[128,128]{1,0:T(8,128)S(1)}, s32[]{:T(128)}, /*index=5*/s32[2]{0:T(128)S(1)}, s32[1]{0:T(128)}, s32[]{:T(128)}) while((s32[]{:T(128)}, f32[128,128]{1,0:T(8,128)S(1)}, f32[128,128]{1,0:T(8,128)S(1)}, f32[128,128]{1,0:T(8,128)S(1)}, s32[]{:T(128)}, ...), condition=%wide.region_6.8_spmd, body=%wide.region_4.7_spmd.sunk | while | flops 197003 | bytes 70774 | solution.py:46
  548.2 1.4 fusion.99
  551.0 1.4 fusion.99
  553.8 1.4 fusion.99
  556.6 1.4 fusion.99
  562.2 1.4 fusion.99
  564.9 1.4 fusion.99
  567.7 1.4 fusion.99
  573.3 1.4 fusion.99
  576.1 1.4 fusion.99
  578.9 1.4 fusion.99
  584.5 1.4 fusion.99
  587.2 1.4 fusion.99
  590.0 1.4 fusion.99
  592.8 1.4 fusion.99
  595.6 1.4 fusion.99
  598.4 1.4 fusion.99
  601.2 1.4 fusion.99
  604.0 1.4 fusion.99
  606.8 1.4 fusion.99
  609.5 1.4 fusion.99
  615.1 1.4 fusion.99
  617.9 1.4 fusion.99
  620.7 1.4 fusion.99
  626.3 1.4 fusion.99
  629.1 1.4 fusion.99
  631.8 1.4 fusion.99
  (1326 shorter events, 637.7 us)
Async XLA Ops:
  7.2 12.1 %copy-start = (bf16[4,128,128]{2,1,0:T(8,128)(2,1)S(1)}, bf16[4,128,128]{2,1,0:T(8,128)(2,1)}, u32[]{:S(2)}) copy-start(bf16[4,128,128]{2,1,0:T(8,128)(2,1)} %param.22) | copy-start | bytes 393220
  7.2 15.3 %copy-start.1 = (bf16[4,4,128,128]{3,2,1,0:T(8,128)(2,1)S(1)}, bf16[4,4,128,128]{3,2,1,0:T(8,128)(2,1)}, u32[]{:S(2)}) copy-start(bf16[4,4,128,128]{3,2,1,0:T(8,128)(2,1)} %param.23) | copy-start | bytes 1572868
  7.2 145.7 %all-reduce.2.cloned.1.call-start = ((), (), s32[]{:S(2)}) async-start(), calls=%async_computation | async-start | bytes 131072 | tf_op jit(solution)/shard_map/psum | solution.py:68
  7.2 18.1 %collective-permute-start = (bf16[4,128,128]{2,1,0:T(8,128)(2,1)}, bf16[4,128,128]{2,1,0:T(8,128)(2,1)S(1)}, u32[]{:S(2)}, u32[]{:S(2)}) collective-permute-start(bf16[4,128,128]{2,1,0:T(8,128)(2,1)} %param.19), channel_id=1, source_target_pairs={{0,1},{1,2},{2,3},{3,4},{4,5},{5,6},{6,7},{7,8},{8,9},{9,10},{10,1... | collective-permute-start | bytes 393224 | tf_op jit(solution)/shard_map/ppermute | solution.py:20
  9.7 16.5 %collective-permute-start.1 = (bf16[4,128,128]{2,1,0:T(8,128)(2,1)}, bf16[4,128,128]{2,1,0:T(8,128)(2,1)S(1)}, u32[]{:S(2)}, u32[]{:S(2)}) collective-permute-start(bf16[4,128,128]{2,1,0:T(8,128)(2,1)} %param.19), channel_id=1, source_target_pairs={{1,0},{2,1},{3,2},{4,3},{5,4},{6,5},{7,6},{8,7},{9,8},{10,9},{11,1... | collective-permute-start | bytes 393224 | tf_op jit(solution)/shard_map/ppermute | solution.py:21
  11.0 10.2 %collective-permute-start.2 = (bf16[4,128]{1,0:T(4,128)(2,1)}, bf16[4,128]{1,0:T(4,128)(2,1)S(1)}, u32[]{:S(2)}, u32[]{:S(2)}) collective-permute-start(bf16[4,128]{1,0:T(4,128)(2,1)} %param.20), channel_id=1, source_target_pairs={{0,1},{1,2},{2,3},{3,4},{4,5},{5,6},{6,7},{7,8},{8,9},{9,10},{10,1... | collective-permute-start | bytes 3080 | tf_op jit(solution)/shard_map/ppermute | solution.py:20
  16.2 5.1 collective-permute-start.3
  20.4 0.7 copy-start.3
  24.6 0.7 copy-start.5
  25.3 0.9 copy-start.2
  546.3 0.7 copy-start.4
Sparse Core Ops, SparseCore 0:
  30.6 122.2 all-reduce.1
where the time goes:
time: 921 us; the launch traced here: 915 us
  other arithmetic  268 us (29%)
  matrix products  212 us (23%)
  local copies, waits for them, and re-layouts  193 us (21%)
  loops' own time  95.1 us (10%)
  waiting for transfers between devices  78.4 us (9%)
  blocking collectives  43.9 us (5%)
  between operations  14.3 us (2%)
  starting transfers between devices  10.3 us (1%)
    another operation x384, other arithmetic  265 us
    dot_general x128, matrix products, solve_step(): jnp.dot(lower[row, :], solved, precision=highest)  185 us
    another operation x1, loops' own time, cholesky_inverse(): lower = lax.fori_loop(0, order, factor_step, jnp.zeros_like(gram))  92.4 us
    psum x1, waiting for transfers between devices, global_sum(): return lax.psum((values[0], values[1]), ('group', 'dom'))  78.3 us
    dynamic_slice x128, local copies, waits for them, and re-layouts, factor_step(): pivot = jnp.sqrt(remaining[column])  77.9 us
    dynamic_slice x128, local copies, waits for them, and re-layouts, solve_step(): lower[row, row]  74.6 us
    psum x1, blocking collectives, global_sum(): return lax.psum((values[0], values[1]), ('group', 'dom'))  43.9 us
    dynamic_slice x128, local copies, waits for them, and re-layouts, factor_step(): row_part = lower[column, :]  22.2 us
  transfers between devices with their start and end apart: 5, of which 1 were waited for; matrix products, arithmetic and copies ran while one was open for 1% of the time, Pallas kernels for 0%

commit v1 on v0

v1 whole, which is shorter than its diff:
```python
import functools

import jax
import jax.numpy as jnp
from jax import lax
from jax.experimental import pallas as pl
from jax.experimental.pallas import tpu as pltpu
from jax.sharding import PartitionSpec as P

HALO = 4
PANEL = 8
section_step = 0.25
AXES = ("group", "dom")
F32 = jnp.float32
BF16 = jnp.bfloat16

NN = (((1,), (0,)), ((), ()))
NT = (((1,), (1,)), ((), ()))
TN = (((0,), (0,)), ((), ()))


def dot(a, b, dims):
    return lax.dot_general(a, b, dims, preferred_element_type=F32)


def split_rows(row, count):
    sub = lax.broadcasted_iota(jnp.int32, (16, row.shape[1]), 0)
    rows = jnp.zeros((16, row.shape[1]), F32)
    rest = row
    for part in range(count):
        piece = rest.astype(BF16).astype(F32)
        rows = jnp.where(sub == part, piece, rows)
        rest = rest - piece
    return rows.astype(BF16)


def operator_kernel(
    index_ref,
    count_ref,
    basis_ref,
    state_ref,
    lower_ref,
    upper_ref,
    source_ref,
    diag_ref,
    coupling_ref,
    image_ref,
    rhs_ref,
    sums_ref,
    ext_ref,
    state_ext_ref,
):
    blocks, block, _ = basis_ref.shape
    slots = coupling_ref.shape[1]
    halo_rows = HALO * block
    ext_ref[:HALO] = lower_ref[:halo_rows].reshape(HALO, block, block)
    ext_ref[HALO : HALO + blocks] = basis_ref[...]
    ext_ref[HALO + blocks :] = upper_ref[:halo_rows].reshape(HALO, block, block)
    state = state_ref[...].astype(F32)
    state_ext_ref[:HALO] = lower_ref[halo_rows:].astype(F32)[:HALO]
    state_ext_ref[HALO : HALO + blocks] = state
    state_ext_ref[HALO + blocks :] = upper_ref[halo_rows:].astype(F32)[:HALO]
    gram = jnp.zeros((block, block), F32)
    moment = jnp.zeros((16, block), F32)
    for b in range(blocks):
        left = [diag_ref[b]]
        right = [basis_ref[b]]
        rows = [jnp.broadcast_to(state[b : b + 1], (16, block))]
        for s in range(slots):
            live = count_ref[b] > s
            pick = index_ref[b, s]
            left.append(coupling_ref[b, s])
            right.append(jnp.where(live, ext_ref[pick], jnp.zeros((block, block), BF16)))
            picked = jnp.where(live, state_ext_ref[pl.ds(pick, 1), :], 0.0)
            rows.append(jnp.broadcast_to(picked, (16, block)))
        left = jnp.concatenate(left, axis=1)
        image = dot(left, jnp.concatenate(right, axis=0), NN).astype(BF16)
        state_image = dot(jnp.concatenate(rows, axis=1).astype(BF16), left, NT)[:1]
        mine = state[b : b + 1]
        rhs = mine + section_step * (source_ref[b : b + 1, :] - state_image)
        image_ref[b] = image
        rhs_ref[b : b + 1, :] = rhs
        gram = gram + dot(image, image, TN)
        moment = moment + dot(split_rows(rhs, 3), image, NN)
    half = block // 2
    top, bottom = gram[:half], gram[half:]
    sub = lax.broadcasted_iota(jnp.int32, (half, block), 0)
    lane = lax.broadcasted_iota(jnp.int32, (half, block), 1)
    sums_ref[:half] = jnp.where(lane < sub, pltpu.roll(bottom, half, 1), top)
    pivots = jnp.sum(jnp.where(lane == sub + half, bottom, 0.0), axis=0, keepdims=True)
    row = lax.broadcasted_iota(jnp.int32, (8, block), 0)
    total = jnp.sum(moment, axis=0, keepdims=True)
    sums_ref[half:] = jnp.where(row == 0, pivots, jnp.where(row == 1, total, 0.0))


def spread(value, shape):
    return jnp.broadcast_to(value, shape)


def eliminate(rows):
    order = rows[0].shape[1]
    panels = len(rows)
    rows = list(rows)
    shape = (PANEL, order)
    lane = lax.broadcasted_iota(jnp.int32, shape, 1)
    sub = lax.broadcasted_iota(jnp.int32, shape, 0)
    done = []
    for p in range(panels):
        c = p * PANEL
        panel = (lane >= c) & (lane < c + PANEL)
        wide = [spread(rows[p][i : i + 1], shape) for i in range(PANEL)]
        a = [
            [spread(wide[i][:, c + j : c + j + 1], shape) if j >= i else None for j in range(PANEL)]
            for i in range(PANEL)
        ]
        wide = [jnp.where(panel, 0.0, row) for row in wide]
        below = {}
        for q in range(p + 1, panels):
            below[q] = [spread(rows[q][:, c + k : c + k + 1], shape) for k in range(PANEL)]
            rows[q] = jnp.where(panel, 0.0, rows[q])
        out = jnp.zeros(shape, F32)
        for k in range(PANEL):
            pivot = a[k][k]
            root = lax.rsqrt(pivot)
            inv = 1.0 / pivot
            unit = jnp.where(lane == c + k, 1.0, wide[k])
            scaled = unit * inv
            factor = [None] * PANEL
            for i in range(k + 1, PANEL):
                factor[i] = a[k][i] * inv
                for j in range(i, PANEL):
                    a[i][j] = a[i][j] - factor[i] * a[k][j]
                wide[i] = wide[i] - factor[i] * unit
            for q in range(p + 1, panels):
                for j in range(k + 1, PANEL):
                    below[q][j] = below[q][j] - below[q][k] * factor[j]
                rows[q] = rows[q] - below[q][k] * scaled
            out = jnp.where(sub == k, unit * root, out)
        done.append(jnp.where(lane <= c + sub, out, 0.0))
    return done


def finish_kernel(*refs, rows_total):
    sum_refs = refs[:-9]
    image_ref, basis_ref, rhs_ref, new_ref, new_image_ref, guess_ref, residual_ref = refs[-9:-2]
    gram_ref, factor_ref = refs[-2:]
    blocks, block, _ = basis_ref.shape
    half = block // 2
    packed = sum_refs[0][...]
    for ref in sum_refs[1:]:
        packed = packed + ref[...]
    packed = packed * (1.0 / rows_total)
    top = packed[:half]
    sub = lax.broadcasted_iota(jnp.int32, (half, block), 0)
    lane = lax.broadcasted_iota(jnp.int32, (half, block), 1)
    upper = jnp.where(lane >= sub, top, 0.0)
    shifted = pltpu.roll(top, half, 1)
    lower = jnp.where((lane >= half) & (lane < sub + half), shifted, 0.0)
    pivots = packed[half : half + 1]
    lower = jnp.where(lane == sub + half, pivots, lower)
    once = jnp.concatenate([upper, lower], axis=0)
    row = lax.broadcasted_iota(jnp.int32, (block, block), 0)
    col = lax.broadcasted_iota(jnp.int32, (block, block), 1)
    gram_ref[...] = once + jnp.where(row == col, 0.0, once.T)
    done = eliminate([gram_ref[p : p + PANEL, :] for p in range(0, block, PANEL)])
    for p, panel in enumerate(done):
        factor_ref[p * PANEL : (p + 1) * PANEL, :] = panel
    factor = factor_ref[...]
    moment = packed[half + 1 : half + 2]
    coefficients = jnp.sum(factor * moment, axis=1, keepdims=True)
    weights = jnp.sum(factor * coefficients, axis=0, keepdims=True)
    weights = split_rows(weights, 3)
    high = factor.astype(BF16)
    low = (factor - high.astype(F32)).astype(BF16)
    both = jnp.concatenate([high, low], axis=1)
    for b in range(blocks):
        image, basis = image_ref[b], basis_ref[b]
        new_image_ref[b] = dot(jnp.concatenate([image, image], axis=1), both, NT).astype(BF16)
        new_ref[b] = dot(jnp.concatenate([basis, basis], axis=1), both, NT).astype(BF16)
        guess = jnp.sum(dot(weights, basis, NT), axis=0, keepdims=True)
        guess_ref[b : b + 1, :] = guess
        fitted = jnp.sum(dot(weights, image, NT), axis=0, keepdims=True)
        residual_ref[b : b + 1, :] = rhs_ref[b : b + 1, :] - fitted


def vmem():
    return pl.BlockSpec(memory_space=pltpu.VMEM)


def smem():
    return pl.BlockSpec(memory_space=pltpu.SMEM)


def halo(array, axis):
    devices = lax.axis_size(axis)
    up = [(i, i + 1) for i in range(devices - 1)]
    down = [(j, i) for i, j in up]
    last, first = array
    return lax.ppermute(last, axis, up), lax.ppermute(first, axis, down)


def exchange_stages(sizes):
    group, dom = sizes
    dom_bits = [1 << i for i in range(dom.bit_length() - 1)]
    group_bits = [dom << i for i in range(group.bit_length() - 1)]
    bits = dom_bits[:2] + group_bits + dom_bits[2:]
    stages = [bits[:1]]
    rest = bits[1:]
    while rest:
        pair, rest = rest[:2], rest[2:]
        stages.append(pair + [sum(pair)] if len(pair) == 2 else pair)
    return stages


def sum_parts(values):
    sizes = [lax.axis_size(axis) for axis in AXES]
    devices = sizes[0] * sizes[1]
    if any(size & (size - 1) for size in sizes):
        return [lax.psum(values, AXES)]
    parts = [values]
    for stage in exchange_stages(sizes):
        total = functools.reduce(jnp.add, parts)
        parts = [total]
        for bit in stage:
            pairs = [(i, i ^ bit) for i in range(devices)]
            parts.append(lax.ppermute(total, AXES, pairs))
    return parts


def body(prior_basis, section_state, source, diag_blocks, coupling, neighbour_index, slot_count):
    blocks, block, columns = prior_basis.shape
    flat = prior_basis.reshape(blocks * block, columns)
    ends = [
        jnp.concatenate([flat[-HALO * block :], section_state[-HALO:], jnp.zeros((16 - HALO, columns), BF16)]),
        jnp.concatenate([flat[: HALO * block], section_state[:HALO], jnp.zeros((16 - HALO, columns), BF16)]),
    ]
    lower, upper = halo(ends, "dom")
    image, rhs, sums = pl.pallas_call(
        operator_kernel,
        out_shape=(
            jax.ShapeDtypeStruct(prior_basis.shape, BF16),
            jax.ShapeDtypeStruct(source.shape, F32),
            jax.ShapeDtypeStruct((block // 2 + 8, columns), F32),
        ),
        in_specs=[smem()] * 2 + [vmem()] * 7,
        out_specs=(vmem(),) * 3,
        scratch_shapes=[
            pltpu.VMEM((blocks + 2 * HALO, block, columns), BF16),
            pltpu.VMEM((blocks + 2 * HALO, columns), F32),
        ],
        name="operator",
    )(
        neighbour_index,
        slot_count,
        prior_basis,
        section_state,
        lower,
        upper,
        source,
        diag_blocks,
        coupling,
    )
    parts = sum_parts(sums)
    rows_total = blocks * block * lax.axis_size("group") * lax.axis_size("dom")
    return pl.pallas_call(
        functools.partial(finish_kernel, rows_total=float(rows_total)),
        out_shape=(
            jax.ShapeDtypeStruct(prior_basis.shape, BF16),
            jax.ShapeDtypeStruct(prior_basis.shape, BF16),
            jax.ShapeDtypeStruct(source.shape, F32),
            jax.ShapeDtypeStruct(source.shape, F32),
        ),
        in_specs=[vmem()] * (len(parts) + 3),
        out_specs=(vmem(),) * 4,
        scratch_shapes=[pltpu.VMEM((block, columns), F32)] * 2,
        name="finish",
    )(*parts, image, prior_basis, rhs)


def solution(mesh):
    rows = P(AXES, None)
    cubes = P(AXES, None, None)
    return jax.shard_map(
        body,
        mesh=mesh,
        in_specs=(cubes, rows, rows, cubes, P(AXES, None, None, None), rows, P(AXES)),
        out_specs=(cubes, cubes, rows, rows),
        check_vma=False,
    )
```

time: 921 us -> 41.8 us (0.05)
  other arithmetic: 268 us -> 1.82 us
  matrix products: 212 us -> 0 us
  local copies, waits for them, and re-layouts: 193 us -> 2.03 us
  loops' own time: 95.1 us -> 0 us
  waiting for transfers between devices: 78.4 us -> 9.83 us
  blocking collectives: 43.9 us -> 0 us
  between operations: 14.3 us -> 0.71 us
  Pallas kernels: 0 us -> 10 us
    another operation x384 -> x0, other arithmetic: 265 us -> none
    dot_general x273 -> x0, matrix products: 212 us -> none  [the longest x128 185 us: solve_step(): jnp.dot(lower[row, :], solved, precision=highest)]
    dynamic_slice x384 -> x0, local copies, waits for them, and re-layouts: 175 us -> none  [the longest x128 77.9 us: factor_step(): pivot = jnp.sqrt(remaining[column])]
    another operation x2 -> x0, loops' own time: 95.1 us -> none  [the longest x1 92.4 us: cholesky_inverse(): lower = lax.fori_loop(0, order, factor_step, jnp.zeros_like(gram))]
    psum x1 -> x0, waiting for transfers between devices: 78.3 us -> none  [global_sum(): return lax.psum((values[0], values[1]), ('group', 'dom'))]
    psum x1 -> x0, blocking collectives: 43.9 us -> none  [global_sum(): return lax.psum((values[0], values[1]), ('group', 'dom'))]
    pallas_call x0 -> x2, Pallas kernels: none -> 10 us  [the longest x1 6.91 us: body(): pl.pallas_call(functools.partial(finish_kernel, rows_total=float(rows_tot...]
    ppermute x4 -> x9, waiting for transfers between devices: 0.03 us -> 9.83 us  [the longest x7 8.88 us: sum_parts(): parts.append(lax.ppermute(total, AXES, pairs))]
  transfers between devices with their start and end apart: 5 -> 9, of which waited for: 1 -> 7; matrix products, arithmetic and copies ran while one was open for 1% -> 0% of each run, Pallas kernels for 0% -> 0%
where the time goes in v1:
time: 41.8 us; the launch traced here: 41.5 us
  starting transfers between devices  17 us (41%)
  Pallas kernels  10 us (24%)
  waiting for transfers between devices  9.83 us (24%)
  local copies, waits for them, and re-layouts  2.03 us (5%)
  other arithmetic  1.82 us (4%)
  between operations  0.71 us (2%)
    ppermute x7, starting transfers between devices, sum_parts(): parts.append(lax.ppermute(total, AXES, pairs))  12.7 us
    ppermute x7, waiting for transfers between devices, sum_parts(): parts.append(lax.ppermute(total, AXES, pairs))  8.88 us
    pallas_call x1, Pallas kernels, body(): pl.pallas_call(functools.partial(finish_kernel, rows_total=float(rows_tot...  6.91 us
    ppermute x2, starting transfers between devices, halo(): return (lax.ppermute(last, axis, up), lax.ppermute(first, axis, down))  4.33 us
    pallas_call x1, Pallas kernels, body(): pl.pallas_call(operator_kernel, out_shape=(jax.ShapeDtypeStruct(prior_bas...  3.12 us
    unnamed x14, local copies, waits for them, and re-layouts  1.95 us
    concatenate x1, other arithmetic, body(): jnp.concatenate([flat[-HALO * block:], section_state[-HALO:], jnp.zeros((...  1.04 us
    ppermute x2, waiting for transfers between devices, halo(): return (lax.ppermute(last, axis, up), lax.ppermute(first, axis, down))  0.95 us
  transfers between devices with their start and end apart: 9, of which 7 were waited for; matrix products, arithmetic and copies ran while one was open for 0% of the time, Pallas kernels for 0%

profile of v1, /device:TPU:0, one launch (start us, length us, event | category | flops | bytes accessed | tf_op | source)
XLA Modules:
  0.0 41.5 jit_solution(8913008981550839366)
XLA Ops:
  0.6 0.1 pad.2.clone
  0.7 0.7 %copy-done.6 = bf16[4,128]{1,0:T(4,128)(2,1)S(1)} copy-done((bf16[4,128]{1,0:T(4,128)(2,1)S(1)}, bf16[4,128]{1,0:T(4,128)(2,1)}, u32[]{:S(2)}) %copy-start.6) | copy-done | bytes 1048
  1.4 1.0 %maximum_maximum_fusion = bf16[528,128]{1,0:T(8,128)(2,1)S(1)} fusion(bf16[4,128]{1,0:T(4,128)(2,1)S(1)} %copy-done.6, bf16[512,128]{1,0:T(8,128)(2,1)} %bitcast.1, bf16[528]{0:T(1024)(128)(2,1)S(1)} %pad.2.clone), kind=kLoop, calls=%fused_computation | loop fusion | flops 405504 | bytes 268320 | tf_op jit(solution)/shard_map/concatenate | solution.py:234
  2.4 1.3 %collective-permute-start.1 = (bf16[528,128]{1,0:T(8,128)(2,1)S(1)}, bf16[528,128]{1,0:T(8,128)(2,1)S(1)}, u32[]{:S(2)}, u32[]{:S(2)}) collective-permute-start(bf16[528,128]{1,0:T(8,128)(2,1)S(1)} %maximum_maximum_fusion), channel_id=1, source_target_pairs={{1,0},{2,1},{3,2},{4,3},{5,4},{6,5},{7,6},{8,7},{9,8},{10,9},{11,1... | collective-permute-start | bytes 405512 | tf_op jit(solution)/shard_map/ppermute | solution.py:199
  3.7 3.0 %collective-permute-start = (bf16[528,128]{1,0:T(8,128)(2,1)S(1)}, bf16[528,128]{1,0:T(8,128)(2,1)S(1)}, u32[]{:S(2)}, u32[]{:S(2)}) collective-permute-start(bf16[528,128]{1,0:T(8,128)(2,1)S(1)} %maximum_maximum_fusion), channel_id=1, source_target_pairs={{0,1},{1,2},{2,3},{3,4},{4,5},{5,6},{6,7},{7,8},{8,9},{9,10},{10,1... | collective-permute-start | bytes 405512 | tf_op jit(solution)/shard_map/ppermute | solution.py:199
  6.8 0.0 collective-permute-done.1.upper_ref
  6.8 0.0 copy-start.1
  6.8 0.9 %collective-permute-done.lower_ref = bf16[528,128]{1,0:T(8,128)(2,1)S(1)} collective-permute-done((bf16[528,128]{1,0:T(8,128)(2,1)S(1)}, bf16[528,128]{1,0:T(8,128)(2,1)S(1)}, u32[]{:S(2)}, u32[]{:S(2)}) %collective-permute-start) | collective-permute-done | bytes 135200 | tf_op jit(solution)/shard_map/ppermute | solution.py:199
  7.8 0.0 copy-done.1
  7.8 0.7 %copy-done.2 = bf16[528,128]{1,0:T(8,128)(2,1)} copy-done((bf16[528,128]{1,0:T(8,128)(2,1)}, bf16[528,128]{1,0:T(8,128)(2,1)S(1)}, u32[]{:S(2)}) %copy-start.2) | copy-done | bytes 135192
  8.4 3.1 %operator.1 = (bf16[4,128,128]{2,1,0:T(8,128)(2,1)}, f32[4,128]{1,0:T(4,128)}, f32[72,128]{1,0:T(8,128)}) custom-call(s32[4,4]{1,0:T(4,128)} %index_ref.1, s32[4]{0:T(128)} %count_ref.1, bf16[4,128,128]{2,1,0:T(8,128)(2,1)} %refs_5_.1, bf16[4,128]{1,0:T(4,128)(2,1)} %state_ref.1, bf16[528,128]{1,0:T(8,128)(2,1)} %copy-done.2, bf16[528,128]{1,0:T(8,128)(2,1)} %copy-done.1, ...), custom_call_target="tpu_custom_call" | custom-call | tf_op jit(solution)/shard_map/operator/pallas_call | solution.py:238
  11.5 4.0 %collective-permute-start.2 = (f32[72,128]{1,0:T(8,128)}, f32[72,128]{1,0:T(8,128)S(1)}, u32[]{:S(2)}, u32[]{:S(2)}) collective-permute-start(f32[72,128]{1,0:T(8,128)} %get-tuple-element.7), channel_id=1, source_target_pairs={{0,1},{1,0},{2,3},{3,2},{4,5},{5,4},{6,7},{7,6},{8,9},{9,8},{10,11... | collective-permute-start | bytes 110600 | tf_op jit(solution)/shard_map/ppermute | solution.py:226
  15.5 1.1 %collective-permute-done.2 = f32[72,128]{1,0:T(8,128)S(1)} collective-permute-done((f32[72,128]{1,0:T(8,128)}, f32[72,128]{1,0:T(8,128)S(1)}, u32[]{:S(2)}, u32[]{:S(2)}) %collective-permute-start.2) | collective-permute-done | bytes 36896 | tf_op jit(solution)/shard_map/ppermute | solution.py:226
  16.6 0.8 %add.12 = f32[72,128]{1,0:T(8,128)S(1)} add(f32[72,128]{1,0:T(8,128)} %get-tuple-element.7, f32[72,128]{1,0:T(8,128)S(1)} %collective-permute-done.2) | non-fusion elementwise | flops 9216 | bytes 110592 | tf_op jit(solution)/shard_map/add | solution.py:222
  17.3 3.7 %collective-permute-start.5 = (f32[72,128]{1,0:T(8,128)S(1)}, f32[72,128]{1,0:T(8,128)S(1)}, u32[]{:S(2)}, u32[]{:S(2)}) collective-permute-start(f32[72,128]{1,0:T(8,128)S(1)} %add.12), channel_id=1, source_target_pairs={{0,18},{1,19},{2,16},{3,17},{4,22},{5,23},{6,20},{7,21},{8,26},{9,... | collective-permute-start | bytes 110600 | tf_op jit(solution)/shard_map/ppermute | solution.py:226
  21.0 0.5 %collective-permute-start.4 = (f32[72,128]{1,0:T(8,128)S(1)}, f32[72,128]{1,0:T(8,128)S(1)}, u32[]{:S(2)}, u32[]{:S(2)}) collective-permute-start(f32[72,128]{1,0:T(8,128)S(1)} %add.12), channel_id=1, source_target_pairs={{0,16},{1,17},{2,18},{3,19},{4,20},{5,21},{6,22},{7,23},{8,24},{9,... | collective-permute-start | bytes 110600 | tf_op jit(solution)/shard_map/ppermute | solution.py:226
  21.5 0.1 collective-permute-start.3
  21.6 1.3 %collective-permute-done.5 = f32[72,128]{1,0:T(8,128)S(1)} collective-permute-done((f32[72,128]{1,0:T(8,128)S(1)}, f32[72,128]{1,0:T(8,128)S(1)}, u32[]{:S(2)}, u32[]{:S(2)}) %collective-permute-start.5) | collective-permute-done | bytes 36896 | tf_op jit(solution)/shard_map/ppermute | solution.py:226
  22.9 2.0 %collective-permute-done.4 = f32[72,128]{1,0:T(8,128)S(1)} collective-permute-done((f32[72,128]{1,0:T(8,128)S(1)}, f32[72,128]{1,0:T(8,128)S(1)}, u32[]{:S(2)}, u32[]{:S(2)}) %collective-permute-start.4) | collective-permute-done | bytes 36896 | tf_op jit(solution)/shard_map/ppermute | solution.py:226
  25.0 0.5 %collective-permute-done.3 = f32[72,128]{1,0:T(8,128)S(1)} collective-permute-done((f32[72,128]{1,0:T(8,128)S(1)}, f32[72,128]{1,0:T(8,128)S(1)}, u32[]{:S(2)}, u32[]{:S(2)}) %collective-permute-start.3) | collective-permute-done | bytes 36896 | tf_op jit(solution)/shard_map/ppermute | solution.py:226
  25.5 0.0 copy-start
  25.5 3.6 %collective-permute-start.8 = (f32[72,128]{1,0:T(8,128)S(1)}, f32[72,128]{1,0:T(8,128)S(1)}, u32[]{:S(2)}, u32[]{:S(2)}) collective-permute-start(f32[72,128]{1,0:T(8,128)S(1)} %add_add_fusion.refs_0_), channel_id=1, source_target_pairs={{0,12},{1,13},{2,14},{3,15},{4,8},{5,9},{6,10},{7,11},{8,4},{9,5},... | collective-permute-start | bytes 110600 | tf_op jit(solution)/shard_map/ppermute | solution.py:226
  29.1 0.0 collective-permute-start.7
  29.1 0.9 %collective-permute-start.6 = (f32[72,128]{1,0:T(8,128)S(1)}, f32[72,128]{1,0:T(8,128)S(1)}, u32[]{:S(2)}, u32[]{:S(2)}) collective-permute-start(f32[72,128]{1,0:T(8,128)S(1)} %add_add_fusion.refs_0_), channel_id=1, source_target_pairs={{0,4},{1,5},{2,6},{3,7},{4,0},{5,1},{6,2},{7,3},{8,12},{9,13},{10,... | collective-permute-start | bytes 110600 | tf_op jit(solution)/shard_map/ppermute | solution.py:226
  30.0 1.4 %collective-permute-done.8.refs_3_ = f32[72,128]{1,0:T(8,128)S(1)} collective-permute-done((f32[72,128]{1,0:T(8,128)S(1)}, f32[72,128]{1,0:T(8,128)S(1)}, u32[]{:S(2)}, u32[]{:S(2)}) %collective-permute-start.8) | collective-permute-done | bytes 36896 | tf_op jit(solution)/shard_map/ppermute | solution.py:226
  31.3 2.6 %collective-permute-done.7.refs_2_ = f32[72,128]{1,0:T(8,128)S(1)} collective-permute-done((f32[72,128]{1,0:T(8,128)S(1)}, f32[72,128]{1,0:T(8,128)S(1)}, u32[]{:S(2)}, u32[]{:S(2)}) %collective-permute-start.7) | collective-permute-done | bytes 36896 | tf_op jit(solution)/shard_map/ppermute | solution.py:226
  33.9 0.0 collective-permute-done.6.refs_1_
  33.9 0.0 copy-done
  33.9 0.0 copy-done.3
  33.9 0.6 %copy-done.4 = f32[72,128]{1,0:T(8,128)} copy-done((f32[72,128]{1,0:T(8,128)}, f32[72,128]{1,0:T(8,128)S(1)}, u32[]{:S(2)}) %copy-start.4) | copy-done | bytes 36888
  34.5 0.0 copy-done.5
  34.5 6.9 %finish.1 = (bf16[4,128,128]{2,1,0:T(8,128)(2,1)}, bf16[4,128,128]{2,1,0:T(8,128)(2,1)}, f32[4,128]{1,0:T(4,128)}, f32[4,128]{1,0:T(4,128)}) custom-call(f32[72,128]{1,0:T(8,128)} %copy-done, f32[72,128]{1,0:T(8,128)} %copy-done.5, f32[72,128]{1,0:T(8,128)} %copy-done.4, f32[72,128]{1,0:T(8,128)} %copy-done.3, ...), custom_call_target="tpu_custom_call" | custom-call | tf_op jit(solution)/shard_map/finish/pallas_call | solution.py:265
  (7 shorter events, 0.0 us)
Async XLA Ops:
  0.7 0.7 %copy-start.6 = (bf16[4,128]{1,0:T(4,128)(2,1)S(1)}, bf16[4,128]{1,0:T(4,128)(2,1)}, u32[]{:S(2)}) copy-start(bf16[4,128]{1,0:T(4,128)(2,1)} %state_ref.1) | copy-start | bytes 3076
  2.4 4.3 %collective-permute-start.1 = (bf16[528,128]{1,0:T(8,128)(2,1)S(1)}, bf16[528,128]{1,0:T(8,128)(2,1)S(1)}, u32[]{:S(2)}, u32[]{:S(2)}) collective-permute-start(bf16[528,128]{1,0:T(8,128)(2,1)S(1)} %maximum_maximum_fusion), channel_id=1, source_target_pairs={{1,0},{2,1},{3,2},{4,3},{5,4},{6,5},{7,6},{8,7},{9,8},{10,9},{11,1... | collective-permute-start | bytes 405512 | tf_op jit(solution)/shard_map/ppermute | solution.py:199
  3.7 4.0 %collective-permute-start = (bf16[528,128]{1,0:T(8,128)(2,1)S(1)}, bf16[528,128]{1,0:T(8,128)(2,1)S(1)}, u32[]{:S(2)}, u32[]{:S(2)}) collective-permute-start(bf16[528,128]{1,0:T(8,128)(2,1)S(1)} %maximum_maximum_fusion), channel_id=1, source_target_pairs={{0,1},{1,2},{2,3},{3,4},{4,5},{5,6},{6,7},{7,8},{8,9},{9,10},{10,1... | collective-permute-start | bytes 405512 | tf_op jit(solution)/shard_map/ppermute | solution.py:199
  6.8 1.0 %copy-start.1 = (bf16[528,128]{1,0:T(8,128)(2,1)}, bf16[528,128]{1,0:T(8,128)(2,1)S(1)}, u32[]{:S(2)}) copy-start(bf16[528,128]{1,0:T(8,128)(2,1)S(1)} %collective-permute-done.1.upper_ref) | copy-start | bytes 405508
  7.8 0.7 %copy-start.2 = (bf16[528,128]{1,0:T(8,128)(2,1)}, bf16[528,128]{1,0:T(8,128)(2,1)S(1)}, u32[]{:S(2)}) copy-start(bf16[528,128]{1,0:T(8,128)(2,1)S(1)} %collective-permute-done.lower_ref) | copy-start | bytes 405508
  11.5 5.0 %collective-permute-start.2 = (f32[72,128]{1,0:T(8,128)}, f32[72,128]{1,0:T(8,128)S(1)}, u32[]{:S(2)}, u32[]{:S(2)}) collective-permute-start(f32[72,128]{1,0:T(8,128)} %get-tuple-element.7), channel_id=1, source_target_pairs={{0,1},{1,0},{2,3},{3,2},{4,5},{5,4},{6,7},{7,6},{8,9},{9,8},{10,11... | collective-permute-start | bytes 110600 | tf_op jit(solution)/shard_map/ppermute | solution.py:226
  17.3 5.6 %collective-permute-start.5 = (f32[72,128]{1,0:T(8,128)S(1)}, f32[72,128]{1,0:T(8,128)S(1)}, u32[]{:S(2)}, u32[]{:S(2)}) collective-permute-start(f32[72,128]{1,0:T(8,128)S(1)} %add.12), channel_id=1, source_target_pairs={{0,18},{1,19},{2,16},{3,17},{4,22},{5,23},{6,20},{7,21},{8,26},{9,... | collective-permute-start | bytes 110600 | tf_op jit(solution)/shard_map/ppermute | solution.py:226
  21.0 4.0 %collective-permute-start.4 = (f32[72,128]{1,0:T(8,128)S(1)}, f32[72,128]{1,0:T(8,128)S(1)}, u32[]{:S(2)}, u32[]{:S(2)}) collective-permute-start(f32[72,128]{1,0:T(8,128)S(1)} %add.12), channel_id=1, source_target_pairs={{0,16},{1,17},{2,18},{3,19},{4,20},{5,21},{6,22},{7,23},{8,24},{9,... | collective-permute-start | bytes 110600 | tf_op jit(solution)/shard_map/ppermute | solution.py:226
  21.5 4.0 %collective-permute-start.3 = (f32[72,128]{1,0:T(8,128)S(1)}, f32[72,128]{1,0:T(8,128)S(1)}, u32[]{:S(2)}, u32[]{:S(2)}) collective-permute-start(f32[72,128]{1,0:T(8,128)S(1)} %add.12), channel_id=1, source_target_pairs={{0,2},{1,3},{2,0},{3,1},{4,6},{5,7},{6,4},{7,5},{8,10},{9,11},{10,... | collective-permute-start | bytes 110600 | tf_op jit(solution)/shard_map/ppermute | solution.py:226
  25.5 8.4 %copy-start = (f32[72,128]{1,0:T(8,128)}, f32[72,128]{1,0:T(8,128)S(1)}, u32[]{:S(2)}) copy-start(f32[72,128]{1,0:T(8,128)S(1)} %add_add_fusion.refs_0_) | copy-start | bytes 110596
  25.5 5.8 %collective-permute-start.8 = (f32[72,128]{1,0:T(8,128)S(1)}, f32[72,128]{1,0:T(8,128)S(1)}, u32[]{:S(2)}, u32[]{:S(2)}) collective-permute-start(f32[72,128]{1,0:T(8,128)S(1)} %add_add_fusion.refs_0_), channel_id=1, source_target_pairs={{0,12},{1,13},{2,14},{3,15},{4,8},{5,9},{6,10},{7,11},{8,4},{9,5},... | collective-permute-start | bytes 110600 | tf_op jit(solution)/shard_map/ppermute | solution.py:226
  29.1 4.9 %collective-permute-start.7 = (f32[72,128]{1,0:T(8,128)S(1)}, f32[72,128]{1,0:T(8,128)S(1)}, u32[]{:S(2)}, u32[]{:S(2)}) collective-permute-start(f32[72,128]{1,0:T(8,128)S(1)} %add_add_fusion.refs_0_), channel_id=1, source_target_pairs={{0,8},{1,9},{2,10},{3,11},{4,12},{5,13},{6,14},{7,15},{8,0},{9,1},... | collective-permute-start | bytes 110600 | tf_op jit(solution)/shard_map/ppermute | solution.py:226
  29.1 4.9 %collective-permute-start.6 = (f32[72,128]{1,0:T(8,128)S(1)}, f32[72,128]{1,0:T(8,128)S(1)}, u32[]{:S(2)}, u32[]{:S(2)}) collective-permute-start(f32[72,128]{1,0:T(8,128)S(1)} %add_add_fusion.refs_0_), channel_id=1, source_target_pairs={{0,4},{1,5},{2,6},{3,7},{4,0},{5,1},{6,2},{7,3},{8,12},{9,13},{10,... | collective-permute-start | bytes 110600 | tf_op jit(solution)/shard_map/ppermute | solution.py:226
  31.3 2.6 %copy-start.3 = (f32[72,128]{1,0:T(8,128)}, f32[72,128]{1,0:T(8,128)S(1)}, u32[]{:S(2)}) copy-start(f32[72,128]{1,0:T(8,128)S(1)} %collective-permute-done.8.refs_3_) | copy-start | bytes 110596
  33.9 0.6 %copy-start.4 = (f32[72,128]{1,0:T(8,128)}, f32[72,128]{1,0:T(8,128)S(1)}, u32[]{:S(2)}) copy-start(f32[72,128]{1,0:T(8,128)S(1)} %collective-permute-done.7.refs_2_) | copy-start | bytes 110596
  33.9 0.6 %copy-start.5 = (f32[72,128]{1,0:T(8,128)}, f32[72,128]{1,0:T(8,128)S(1)}, u32[]{:S(2)}) copy-start(f32[72,128]{1,0:T(8,128)S(1)} %collective-permute-done.6.refs_1_) | copy-start | bytes 110596

commit v2 on v1

--- a/solution.py
+++ b/solution.py
@@ -9,6 +9,7 @@
 
 HALO = 4
 PANEL = 8
+VMEM_LIMIT = 16 << 20
 section_step = 0.25
 AXES = ("group", "dom")
 F32 = jnp.float32
@@ -34,50 +35,129 @@
     return rows.astype(BF16)
 
 
-def operator_kernel(
+def stack_rows(rows):
+    return jnp.concatenate([jnp.broadcast_to(row, (16, row.shape[1])) for row in rows], axis=1).astype(BF16)
+
+
+def pack_kernel(basis_ref, state_ref, packed_ref, rows_ref, sems):
+    rows = basis_ref.shape[0]
+    copy = pltpu.make_async_copy(basis_ref, packed_ref.at[pl.ds(0, rows)], sems.at[0])
+    copy.start()
+    state_copy = pltpu.make_async_copy(state_ref, rows_ref, sems.at[1])
+    state_copy.start()
+    state_copy.wait()
+    state = rows_ref[...].astype(F32)
+    spare = jnp.zeros((packed_ref.shape[0] - rows - state.shape[0], state.shape[1]), F32)
+    packed_ref[rows:] = jnp.concatenate([state, spare], axis=0).astype(BF16)
+    copy.wait()
+
+
+def state_of(packed_ref, rows, count):
+    return packed_ref[rows:].astype(F32)[:count]
+
+
+def block_of(packed_ref, pick, block):
+    return packed_ref[pl.ds(pl.multiple_of(pick * block, block), block)]
+
+
+def local_kernel(
     index_ref,
     count_ref,
-    basis_ref,
-    state_ref,
-    lower_ref,
-    upper_ref,
+    packed_ref,
     source_ref,
     diag_ref,
     coupling_ref,
+    partial_ref,
+    base_ref,
+    near_coupling_ref,
+    near_index_ref,
+    near_count_ref,
+    sem,
+):
+    copy = pltpu.make_async_copy(coupling_ref, near_coupling_ref, sem)
+    copy.start()
+    blocks, block, _ = diag_ref.shape
+    slots = coupling_ref.shape[1]
+    for b in range(blocks):
+        near_count_ref[b] = count_ref[b]
+        for s in range(slots):
+            near_index_ref[b, s] = index_ref[b, s]
+    state = state_of(packed_ref, blocks * block, blocks)
+    state_rows = [state[b : b + 1] for b in range(blocks)]
+    copy.wait()
+    for b in range(blocks):
+        left, right, rows = [diag_ref[b]], [block_of(packed_ref, b, block)], [state_rows[b]]
+        for s in range(2, slots):
+            pick = index_ref[b, s] - HALO
+            live = (count_ref[b] > s) & (pick >= 0) & (pick < blocks)
+            pick = jnp.clip(pick, 0, blocks - 1)
+            left.append(near_coupling_ref[b, s])
+            right.append(jnp.where(live, block_of(packed_ref, pick, block), jnp.zeros((block, block), BF16)))
+            row = state_rows[0]
+            for i in range(1, blocks):
+                row = jnp.where(pick == i, state_rows[i], row)
+            rows.append(jnp.where(live, row, 0.0))
+        left = jnp.concatenate(left, axis=1)
+        partial_ref[b] = dot(left, jnp.concatenate(right, axis=0), NN)
+        state_image = dot(stack_rows(rows), left, NT)[:1]
+        base_ref[b : b + 1, :] = state_rows[b] + section_step * (source_ref[b : b + 1, :] - state_image)
+
+
+def shared_kernel(
+    index_ref,
+    count_ref,
+    inner_ref,
+    outer_ref,
+    coupling_ref,
+    _partial_in_ref,
+    _base_in_ref,
+    partial_ref,
+    rhs_ref,
     image_ref,
-    rhs_ref,
     sums_ref,
-    ext_ref,
-    state_ext_ref,
 ):
-    blocks, block, _ = basis_ref.shape
-    slots = coupling_ref.shape[1]
-    halo_rows = HALO * block
-    ext_ref[:HALO] = lower_ref[:halo_rows].reshape(HALO, block, block)
-    ext_ref[HALO : HALO + blocks] = basis_ref[...]
-    ext_ref[HALO + blocks :] = upper_ref[:halo_rows].reshape(HALO, block, block)
-    state = state_ref[...].astype(F32)
-    state_ext_ref[:HALO] = lower_ref[halo_rows:].astype(F32)[:HALO]
-    state_ext_ref[HALO : HALO + blocks] = state
-    state_ext_ref[HALO + blocks :] = upper_ref[halo_rows:].astype(F32)[:HALO]
+    blocks, block, _ = image_ref.shape
+    odd = lax.axis_index("dom") % 2 == 1
+    inner_state = state_of(inner_ref, HALO * block, HALO)
+    outer_state = state_of(outer_ref, HALO * block, HALO)
+    lower_state = jnp.where(odd, inner_state, outer_state)
+    upper_state = jnp.where(odd, outer_state, inner_state)
+
+    def lower(pick):
+        return jnp.where(odd, block_of(inner_ref, pick, block), block_of(outer_ref, pick, block))
+
+    def upper(pick):
+        return jnp.where(odd, block_of(outer_ref, pick, block), block_of(inner_ref, pick, block))
+
+    def chosen(rows, pick):
+        row = rows[:1]
+        for i in range(1, HALO):
+            row = jnp.where(pick == i, rows[i : i + 1], row)
+        return row
+
+    for b in range(blocks):
+        for s in range(2, coupling_ref.shape[1]):
+            pick = index_ref[b, s]
+            above = pick - HALO - blocks
+
+            @pl.when((count_ref[b] > s) & ((pick < HALO) | (above >= 0)))
+            def _(b=b, s=s, pick=pick, above=above):
+                at = jnp.where(above >= 0, above, pick)
+                picked = jnp.where(above >= 0, upper(at), lower(at))
+                row = jnp.where(above >= 0, chosen(upper_state, at), chosen(lower_state, at))
+                left = coupling_ref[b, s]
+                partial_ref[b] += dot(left, picked, NN)
+                rhs_ref[b : b + 1, :] -= section_step * dot(stack_rows([row]), left, NT)[:1]
+
     gram = jnp.zeros((block, block), F32)
     moment = jnp.zeros((16, block), F32)
     for b in range(blocks):
-        left = [diag_ref[b]]
-        right = [basis_ref[b]]
-        rows = [jnp.broadcast_to(state[b : b + 1], (16, block))]
-        for s in range(slots):
-            live = count_ref[b] > s
-            pick = index_ref[b, s]
-            left.append(coupling_ref[b, s])
-            right.append(jnp.where(live, ext_ref[pick], jnp.zeros((block, block), BF16)))
-            picked = jnp.where(live, state_ext_ref[pl.ds(pick, 1), :], 0.0)
-            rows.append(jnp.broadcast_to(picked, (16, block)))
-        left = jnp.concatenate(left, axis=1)
-        image = dot(left, jnp.concatenate(right, axis=0), NN).astype(BF16)
-        state_image = dot(jnp.concatenate(rows, axis=1).astype(BF16), left, NT)[:1]
-        mine = state[b : b + 1]
-        rhs = mine + section_step * (source_ref[b : b + 1, :] - state_image)
+        below, above = index_ref[b, 0], index_ref[b, 1] - HALO - blocks
+        left = jnp.concatenate([coupling_ref[b, 0], coupling_ref[b, 1]], axis=1)
+        right = jnp.concatenate([lower(below), upper(above)], axis=0)
+        image = (partial_ref[b] + dot(left, right, NN)).astype(BF16)
+        rows = stack_rows([chosen(lower_state, below), chosen(upper_state, above)])
+        rhs = rhs_ref[b : b + 1, :] - section_step * dot(rows, left, NT)[:1]
         image_ref[b] = image
         rhs_ref[b : b + 1, :] = rhs
         gram = gram + dot(image, image, TN)
@@ -142,9 +222,9 @@
 
 def finish_kernel(*refs, rows_total):
     sum_refs = refs[:-9]
-    image_ref, basis_ref, rhs_ref, new_ref, new_image_ref, guess_ref, residual_ref = refs[-9:-2]
+    image_ref, packed_ref, rhs_ref, new_ref, new_image_ref, guess_ref, residual_ref = refs[-9:-2]
     gram_ref, factor_ref = refs[-2:]
-    blocks, block, _ = basis_ref.shape
+    blocks, block, _ = image_ref.shape
     half = block // 2
     packed = sum_refs[0][...]
     for ref in sum_refs[1:]:
@@ -174,7 +254,7 @@
     low = (factor - high.astype(F32)).astype(BF16)
     both = jnp.concatenate([high, low], axis=1)
     for b in range(blocks):
-        image, basis = image_ref[b], basis_ref[b]
+        image, basis = image_ref[b], block_of(packed_ref, b, block)
         new_image_ref[b] = dot(jnp.concatenate([image, image], axis=1), both, NT).astype(BF16)
         new_ref[b] = dot(jnp.concatenate([basis, basis], axis=1), both, NT).astype(BF16)
         guess = jnp.sum(dot(weights, basis, NT), axis=0, keepdims=True)
@@ -183,6 +263,14 @@
         residual_ref[b : b + 1, :] = rhs_ref[b : b + 1, :] - fitted
 
 
+def near(*arrays):
+    return [pltpu.with_memory_space_constraint(array, pltpu.VMEM) for array in arrays]
+
+
+def far(*arrays):
+    return [pltpu.with_memory_space_constraint(array, pltpu.HBM) for array in arrays]
+
+
 def vmem():
     return pl.BlockSpec(memory_space=pltpu.VMEM)
 
@@ -191,12 +279,32 @@
     return pl.BlockSpec(memory_space=pltpu.SMEM)
 
 
-def halo(array, axis):
-    devices = lax.axis_size(axis)
-    up = [(i, i + 1) for i in range(devices - 1)]
-    down = [(j, i) for i, j in up]
-    last, first = array
-    return lax.ppermute(last, axis, up), lax.ppermute(first, axis, down)
+def pack(basis, state):
+    blocks, block, columns = basis.shape
+    rows = blocks * block
+    return pl.pallas_call(
+        pack_kernel,
+        out_shape=pltpu.VMEM((rows + 16 * pl.cdiv(blocks, 16), columns), BF16),
+        in_specs=[pl.BlockSpec(memory_space=pl.ANY)] * 2,
+        out_specs=vmem(),
+        scratch_shapes=[pltpu.VMEM(state.shape, BF16), pltpu.SemaphoreType.DMA((2,))],
+        compiler_params=pltpu.CompilerParams(vmem_limit_bytes=VMEM_LIMIT),
+        name="pack",
+    )(*far(basis.reshape(rows, columns), state))
+
+
+def halo(packed, basis, state):
+    devices = lax.axis_size("dom")
+    odd = lax.axis_index("dom") % 2
+    got = []
+    for parity in (1, 0):
+        pairs = [(i, i + 1) for i in range(parity, devices - 1, 2)]
+        sent = packed
+        if basis.shape[0] > HALO:
+            up = odd == parity
+            sent = pack(*(jnp.where(up, whole[-HALO:], whole[:HALO]) for whole in (basis, state)))
+        got.append(lax.ppermute(sent, "dom", pairs + [(j, i) for i, j in pairs]))
+    return got
 
 
 def exchange_stages(sizes):
@@ -229,36 +337,39 @@
 
 def body(prior_basis, section_state, source, diag_blocks, coupling, neighbour_index, slot_count):
     blocks, block, columns = prior_basis.shape
-    flat = prior_basis.reshape(blocks * block, columns)
-    ends = [
-        jnp.concatenate([flat[-HALO * block :], section_state[-HALO:], jnp.zeros((16 - HALO, columns), BF16)]),
-        jnp.concatenate([flat[: HALO * block], section_state[:HALO], jnp.zeros((16 - HALO, columns), BF16)]),
-    ]
-    lower, upper = halo(ends, "dom")
-    image, rhs, sums = pl.pallas_call(
-        operator_kernel,
+    packed = pack(prior_basis, section_state)
+    outer, inner = halo(packed, prior_basis, section_state)
+    partial, base, near_coupling, near_index, near_count = pl.pallas_call(
+        local_kernel,
         out_shape=(
-            jax.ShapeDtypeStruct(prior_basis.shape, BF16),
-            jax.ShapeDtypeStruct(source.shape, F32),
-            jax.ShapeDtypeStruct((block // 2 + 8, columns), F32),
+            pltpu.VMEM(prior_basis.shape, F32),
+            pltpu.VMEM(source.shape, F32),
+            pltpu.VMEM(coupling.shape, BF16),
+            pltpu.SMEM(neighbour_index.shape, jnp.int32),
+            pltpu.SMEM(slot_count.shape, jnp.int32),
         ),
-        in_specs=[smem()] * 2 + [vmem()] * 7,
-        out_specs=(vmem(),) * 3,
-        scratch_shapes=[
-            pltpu.VMEM((blocks + 2 * HALO, block, columns), BF16),
-            pltpu.VMEM((blocks + 2 * HALO, columns), F32),
-        ],
-        name="operator",
+        in_specs=[smem()] * 2 + [vmem()] * 3 + [pl.BlockSpec(memory_space=pl.ANY)],
+        out_specs=(vmem(),) * 3 + (smem(),) * 2,
+        scratch_shapes=[pltpu.SemaphoreType.DMA],
+        compiler_params=pltpu.CompilerParams(vmem_limit_bytes=VMEM_LIMIT),
+        name="local_part",
+    )(*far(neighbour_index, slot_count), *near(packed), *far(source, diag_blocks, coupling))
+    _, rhs, image, sums = pl.pallas_call(
+        shared_kernel,
+        out_shape=(
+            pltpu.VMEM(prior_basis.shape, F32),
+            pltpu.VMEM(source.shape, F32),
+            pltpu.VMEM(prior_basis.shape, BF16),
+            pltpu.VMEM((block // 2 + 8, columns), F32),
+        ),
+        in_specs=[smem()] * 2 + [vmem()] * 5,
+        out_specs=(vmem(),) * 4,
+        input_output_aliases={5: 0, 6: 1},
+        compiler_params=pltpu.CompilerParams(vmem_limit_bytes=VMEM_LIMIT),
+        name="shared_part",
     )(
-        neighbour_index,
-        slot_count,
-        prior_basis,
-        section_state,
-        lower,
-        upper,
-        source,
-        diag_blocks,
-        coupling,
+        *(pltpu.with_memory_space_constraint(array, pltpu.SMEM) for array in (near_index, near_count)),
+        *near(inner, outer, near_coupling, partial, base),
     )
     parts = sum_parts(sums)
     rows_total = blocks * block * lax.axis_size("group") * lax.axis_size("dom")
@@ -273,8 +384,9 @@
         in_specs=[vmem()] * (len(parts) + 3),
         out_specs=(vmem(),) * 4,
         scratch_shapes=[pltpu.VMEM((block, columns), F32)] * 2,
+        compiler_params=pltpu.CompilerParams(vmem_limit_bytes=VMEM_LIMIT),
         name="finish",
-    )(*parts, image, prior_basis, rhs)
+    )(*near(*parts, image, packed, rhs))
 
 
 def solution(mesh):

time: 41.8 us -> 33.4 us (0.80)
  starting transfers between devices: 17 us -> 14.7 us
  waiting for transfers between devices: 9.83 us -> 7.7 us
  local copies, waits for them, and re-layouts: 2.03 us -> 0 us
  other arithmetic: 1.82 us -> 0.02 us
    ppermute x7, starting transfers between devices: 12.7 us -> 9.67 us  [sum_parts(): parts.append(lax.ppermute(total, AXES, pairs))]
    unnamed x14 -> x0, local copies, waits for them, and re-layouts: 1.95 us -> none
    ppermute x7, waiting for transfers between devices: 8.88 us -> 7.69 us  [sum_parts(): parts.append(lax.ppermute(total, AXES, pairs))]
    pallas_call x1 -> x3, Pallas kernels: 3.12 us -> 4.26 us  [the longest x1 2.36 us: body(): pl.pallas_call(local_kernel, out_shape=(pltpu.VMEM(prior_basis.shape, F32...]
    pallas_call x1, Pallas kernels: 6.91 us -> 5.86 us  [body(): pl.pallas_call(functools.partial(finish_kernel, rows_total=float(rows_tot...]
    concatenate x1 -> x0, other arithmetic: 1.04 us -> none  [body(): jnp.concatenate([flat[-HALO * block:], section_state[-HALO:], jnp.zeros((...]
    ppermute x2, waiting for transfers between devices: 0.95 us -> 0.01 us  [halo(): got.append(lax.ppermute(sent, 'dom', pairs + [(j, i) for i, j in pairs]))]
    add x2, other arithmetic: 0.79 us -> 0.02 us  [sum_parts(): total = functools.reduce(jnp.add, parts)]
  transfers between devices with their start and end apart: 9 -> 9, of which waited for: 7 -> 7; matrix products, arithmetic and copies ran while one was open for 0% -> 0% of each run, Pallas kernels for 0% -> 7%
where the time goes in v2:
time: 33.4 us; the launch traced here: 33.2 us
  starting transfers between devices  14.7 us (44%)
  Pallas kernels  10.1 us (30%)
  waiting for transfers between devices  7.7 us (23%)
  between operations  0.68 us (2%)
    ppermute x7, starting transfers between devices, sum_parts(): parts.append(lax.ppermute(total, AXES, pairs))  9.67 us
    ppermute x7, waiting for transfers between devices, sum_parts(): parts.append(lax.ppermute(total, AXES, pairs))  7.69 us
    pallas_call x1, Pallas kernels, body(): pl.pallas_call(functools.partial(finish_kernel, rows_total=float(rows_tot...  5.86 us
    ppermute x2, starting transfers between devices, halo(): got.append(lax.ppermute(sent, 'dom', pairs + [(j, i) for i, j in pairs]))  5.03 us
    pallas_call x1, Pallas kernels, body(): pl.pallas_call(local_kernel, out_shape=(pltpu.VMEM(prior_basis.shape, F32...  2.36 us
    pallas_call x1, Pallas kernels, body(): pl.pallas_call(shared_kernel, out_shape=(pltpu.VMEM(prior_basis.shape, F3...  0.98 us
    pallas_call x1, Pallas kernels, pack(): pl.pallas_call(pack_kernel, out_shape=pltpu.VMEM((rows + 16 * pl.cdiv(blo...  0.92 us
  transfers between devices with their start and end apart: 9, of which 7 were waited for; matrix products, arithmetic and copies ran while one was open for 0% of the time, Pallas kernels for 7%

profile of v2, /device:TPU:0, one launch (start us, length us, event | category | flops | bytes accessed | tf_op | source)
XLA Modules:
  0.0 33.2 jit_solution(15613573608505396013)
XLA Ops:
  0.6 0.9 %pack.1.packed_ref.refs_5_ = bf16[528,128]{1,0:T(8,128)(2,1)S(1)} custom-call(bf16[512,128]{1,0:T(8,128)(2,1)} %bitcast.1, bf16[4,128]{1,0:T(4,128)(2,1)} %state_ref.1), custom_call_target="tpu_custom_call" | custom-call | tf_op jit(solution)/shard_map/pack/pallas_call | solution.py:285
  1.6 0.7 %collective-permute-start.1 = (bf16[528,128]{1,0:T(8,128)(2,1)S(1)}, bf16[528,128]{1,0:T(8,128)(2,1)S(1)}, u32[]{:S(2)}, u32[]{:S(2)}) collective-permute-start(bf16[528,128]{1,0:T(8,128)(2,1)S(1)} %pack.1.packed_ref.refs_5_), channel_id=1, source_target_pairs={{1,2},{3,4},{5,6},{7,8},{9,10},{11,12},{13,14},{2,1},{4,3},{6,5},{... | collective-permute-start | bytes 405512 | tf_op jit(solution)/shard_map/ppermute | solution.py:306
  2.2 4.4 %collective-permute-start = (bf16[528,128]{1,0:T(8,128)(2,1)S(1)}, bf16[528,128]{1,0:T(8,128)(2,1)S(1)}, u32[]{:S(2)}, u32[]{:S(2)}) collective-permute-start(bf16[528,128]{1,0:T(8,128)(2,1)S(1)} %pack.1.packed_ref.refs_5_), channel_id=1, source_target_pairs={{0,1},{2,3},{4,5},{6,7},{8,9},{10,11},{12,13},{14,15},{1,0},{3,2},... | collective-permute-start | bytes 405512 | tf_op jit(solution)/shard_map/ppermute | solution.py:306
  6.6 2.4 %local_part.1 = (f32[4,128,128]{2,1,0:T(8,128)S(1)}, f32[4,128]{1,0:T(4,128)S(1)}, bf16[4,4,128,128]{3,2,1,0:T(8,128)(2,1)S(1)}, s32[4,4]{1,0:T(4,128)S(4)}, s32[4]{0:T(128)S(4)}) custom-call(s32[4,4]{1,0:T(4,128)} %index_ref.1, s32[4]{0:T(128)} %count_ref.1, bf16[528,128]{1,0:T(8,128)(2,1)S(1)} %pack.1.packed_ref.refs_5_, f32[4,128]{1,0:T(4,128)} %source_ref.1, ...), custom_call_target="tpu_custom_call" | custom-call | tf_op jit(solution)/shard_map/local_part/pallas_call | solution.py:342
  9.0 0.0 collective-permute-done.1.outer_ref
  9.0 0.0 collective-permute-done.inner_ref
  9.0 1.0 %shared_part.1 = (f32[4,128,128]{2,1,0:T(8,128)S(1)}, f32[4,128]{1,0:T(4,128)S(1)}, bf16[4,128,128]{2,1,0:T(8,128)(2,1)S(1)}, f32[72,128]{1,0:T(8,128)S(1)}) custom-call(s32[4,4]{1,0:T(4,128)S(4)} %get-tuple-element.12.index_ref, s32[4]{0:T(128)S(4)} %get-tuple-element.13.count_ref, ...), custom_call_target="tpu_custom_call", output_to_operand_aliasing={{0}: (5, {}), {1}: (6, {})} | custom-call | tf_op jit(solution)/shard_map/shared_part/pallas_call | solution.py:357
  10.0 0.9 %collective-permute-start.2 = (f32[72,128]{1,0:T(8,128)S(1)}, f32[72,128]{1,0:T(8,128)S(1)}, u32[]{:S(2)}, u32[]{:S(2)}) collective-permute-start(f32[72,128]{1,0:T(8,128)S(1)} %get-tuple-element.17), channel_id=1, source_target_pairs={{0,1},{1,0},{2,3},{3,2},{4,5},{5,4},{6,7},{7,6},{8,9},{9,8},{10,11... | collective-permute-start | bytes 110600 | tf_op jit(solution)/shard_map/ppermute | solution.py:334
  10.9 0.9 %collective-permute-done.2 = f32[72,128]{1,0:T(8,128)S(1)} collective-permute-done((f32[72,128]{1,0:T(8,128)S(1)}, f32[72,128]{1,0:T(8,128)S(1)}, u32[]{:S(2)}, u32[]{:S(2)}) %collective-permute-start.2) | collective-permute-done | bytes 36896 | tf_op jit(solution)/shard_map/ppermute | solution.py:334
  11.7 3.7 %collective-permute-start.5 = (f32[72,128]{1,0:T(8,128)S(1)}, f32[72,128]{1,0:T(8,128)S(1)}, u32[]{:S(2)}, u32[]{:S(2)}) collective-permute-start(f32[72,128]{1,0:T(8,128)S(1)} %add.12), channel_id=1, source_target_pairs={{0,18},{1,19},{2,16},{3,17},{4,22},{5,23},{6,20},{7,21},{8,26},{9,... | collective-permute-start | bytes 110600 | tf_op jit(solution)/shard_map/ppermute | solution.py:334
  15.4 0.5 %collective-permute-start.4 = (f32[72,128]{1,0:T(8,128)S(1)}, f32[72,128]{1,0:T(8,128)S(1)}, u32[]{:S(2)}, u32[]{:S(2)}) collective-permute-start(f32[72,128]{1,0:T(8,128)S(1)} %add.12), channel_id=1, source_target_pairs={{0,16},{1,17},{2,18},{3,19},{4,20},{5,21},{6,22},{7,23},{8,24},{9,... | collective-permute-start | bytes 110600 | tf_op jit(solution)/shard_map/ppermute | solution.py:334
  15.9 0.1 collective-permute-start.3
  16.1 1.3 %collective-permute-done.5 = f32[72,128]{1,0:T(8,128)S(1)} collective-permute-done((f32[72,128]{1,0:T(8,128)S(1)}, f32[72,128]{1,0:T(8,128)S(1)}, u32[]{:S(2)}, u32[]{:S(2)}) %collective-permute-start.5) | collective-permute-done | bytes 36896 | tf_op jit(solution)/shard_map/ppermute | solution.py:334
  17.4 2.0 %collective-permute-done.4 = f32[72,128]{1,0:T(8,128)S(1)} collective-permute-done((f32[72,128]{1,0:T(8,128)S(1)}, f32[72,128]{1,0:T(8,128)S(1)}, u32[]{:S(2)}, u32[]{:S(2)}) %collective-permute-start.4) | collective-permute-done | bytes 36896 | tf_op jit(solution)/shard_map/ppermute | solution.py:334
  19.4 0.5 %collective-permute-done.3 = f32[72,128]{1,0:T(8,128)S(1)} collective-permute-done((f32[72,128]{1,0:T(8,128)S(1)}, f32[72,128]{1,0:T(8,128)S(1)}, u32[]{:S(2)}, u32[]{:S(2)}) %collective-permute-start.3) | collective-permute-done | bytes 36896 | tf_op jit(solution)/shard_map/ppermute | solution.py:334
  19.9 2.2 %collective-permute-start.8 = (f32[72,128]{1,0:T(8,128)S(1)}, f32[72,128]{1,0:T(8,128)S(1)}, u32[]{:S(2)}, u32[]{:S(2)}) collective-permute-start(f32[72,128]{1,0:T(8,128)S(1)} %add_add_fusion.refs_0_), channel_id=1, source_target_pairs={{0,12},{1,13},{2,14},{3,15},{4,8},{5,9},{6,10},{7,11},{8,4},{9,5},... | collective-permute-start | bytes 110600 | tf_op jit(solution)/shard_map/ppermute | solution.py:334
  22.1 0.9 %collective-permute-start.7 = (f32[72,128]{1,0:T(8,128)S(1)}, f32[72,128]{1,0:T(8,128)S(1)}, u32[]{:S(2)}, u32[]{:S(2)}) collective-permute-start(f32[72,128]{1,0:T(8,128)S(1)} %add_add_fusion.refs_0_), channel_id=1, source_target_pairs={{0,8},{1,9},{2,10},{3,11},{4,12},{5,13},{6,14},{7,15},{8,0},{9,1},... | collective-permute-start | bytes 110600 | tf_op jit(solution)/shard_map/ppermute | solution.py:334
  23.0 1.3 %collective-permute-start.6 = (f32[72,128]{1,0:T(8,128)S(1)}, f32[72,128]{1,0:T(8,128)S(1)}, u32[]{:S(2)}, u32[]{:S(2)}) collective-permute-start(f32[72,128]{1,0:T(8,128)S(1)} %add_add_fusion.refs_0_), channel_id=1, source_target_pairs={{0,4},{1,5},{2,6},{3,7},{4,0},{5,1},{6,2},{7,3},{8,12},{9,13},{10,... | collective-permute-start | bytes 110600 | tf_op jit(solution)/shard_map/ppermute | solution.py:334
  24.4 1.5 %collective-permute-done.8.refs_3_ = f32[72,128]{1,0:T(8,128)S(1)} collective-permute-done((f32[72,128]{1,0:T(8,128)S(1)}, f32[72,128]{1,0:T(8,128)S(1)}, u32[]{:S(2)}, u32[]{:S(2)}) %collective-permute-start.8) | collective-permute-done | bytes 36896 | tf_op jit(solution)/shard_map/ppermute | solution.py:334
  25.8 1.2 %collective-permute-done.7.refs_2_ = f32[72,128]{1,0:T(8,128)S(1)} collective-permute-done((f32[72,128]{1,0:T(8,128)S(1)}, f32[72,128]{1,0:T(8,128)S(1)}, u32[]{:S(2)}, u32[]{:S(2)}) %collective-permute-start.7) | collective-permute-done | bytes 36896 | tf_op jit(solution)/shard_map/ppermute | solution.py:334
  27.1 0.3 collective-permute-done.6.refs_1_
  27.4 5.9 %finish.1 = (bf16[4,128,128]{2,1,0:T(8,128)(2,1)}, bf16[4,128,128]{2,1,0:T(8,128)(2,1)}, f32[4,128]{1,0:T(4,128)}, f32[4,128]{1,0:T(4,128)}) custom-call(f32[72,128]{1,0:T(8,128)S(1)} %add_add_fusion.refs_0_, f32[72,128]{1,0:T(8,128)S(1)} %collective-permute-done.6.refs_1_, f32[72,128]{1,0:T(8,128)S(1)} %collective-permute-done.7.refs_2_, ...), custom_call_target="tpu_custom_call" | custom-call | tf_op jit(solution)/shard_map/finish/pallas_call | solution.py:376
  (2 shorter events, 0.0 us)
Async XLA Ops:
  1.6 7.4 %collective-permute-start.1 = (bf16[528,128]{1,0:T(8,128)(2,1)S(1)}, bf16[528,128]{1,0:T(8,128)(2,1)S(1)}, u32[]{:S(2)}, u32[]{:S(2)}) collective-permute-start(bf16[528,128]{1,0:T(8,128)(2,1)S(1)} %pack.1.packed_ref.refs_5_), channel_id=1, source_target_pairs={{1,2},{3,4},{5,6},{7,8},{9,10},{11,12},{13,14},{2,1},{4,3},{6,5},{... | collective-permute-start | bytes 405512 | tf_op jit(solution)/shard_map/ppermute | solution.py:306
  2.2 6.7 %collective-permute-start = (bf16[528,128]{1,0:T(8,128)(2,1)S(1)}, bf16[528,128]{1,0:T(8,128)(2,1)S(1)}, u32[]{:S(2)}, u32[]{:S(2)}) collective-permute-start(bf16[528,128]{1,0:T(8,128)(2,1)S(1)} %pack.1.packed_ref.refs_5_), channel_id=1, source_target_pairs={{0,1},{2,3},{4,5},{6,7},{8,9},{10,11},{12,13},{14,15},{1,0},{3,2},... | collective-permute-start | bytes 405512 | tf_op jit(solution)/shard_map/ppermute | solution.py:306
  10.0 1.8 %collective-permute-start.2 = (f32[72,128]{1,0:T(8,128)S(1)}, f32[72,128]{1,0:T(8,128)S(1)}, u32[]{:S(2)}, u32[]{:S(2)}) collective-permute-start(f32[72,128]{1,0:T(8,128)S(1)} %get-tuple-element.17), channel_id=1, source_target_pairs={{0,1},{1,0},{2,3},{3,2},{4,5},{5,4},{6,7},{7,6},{8,9},{9,8},{10,11... | collective-permute-start | bytes 110600 | tf_op jit(solution)/shard_map/ppermute | solution.py:334
  11.7 5.6 %collective-permute-start.5 = (f32[72,128]{1,0:T(8,128)S(1)}, f32[72,128]{1,0:T(8,128)S(1)}, u32[]{:S(2)}, u32[]{:S(2)}) collective-permute-start(f32[72,128]{1,0:T(8,128)S(1)} %add.12), channel_id=1, source_target_pairs={{0,18},{1,19},{2,16},{3,17},{4,22},{5,23},{6,20},{7,21},{8,26},{9,... | collective-permute-start | bytes 110600 | tf_op jit(solution)/shard_map/ppermute | solution.py:334
  15.4 4.0 %collective-permute-start.4 = (f32[72,128]{1,0:T(8,128)S(1)}, f32[72,128]{1,0:T(8,128)S(1)}, u32[]{:S(2)}, u32[]{:S(2)}) collective-permute-start(f32[72,128]{1,0:T(8,128)S(1)} %add.12), channel_id=1, source_target_pairs={{0,16},{1,17},{2,18},{3,19},{4,20},{5,21},{6,22},{7,23},{8,24},{9,... | collective-permute-start | bytes 110600 | tf_op jit(solution)/shard_map/ppermute | solution.py:334
  15.9 4.0 %collective-permute-start.3 = (f32[72,128]{1,0:T(8,128)S(1)}, f32[72,128]{1,0:T(8,128)S(1)}, u32[]{:S(2)}, u32[]{:S(2)}) collective-permute-start(f32[72,128]{1,0:T(8,128)S(1)} %add.12), channel_id=1, source_target_pairs={{0,2},{1,3},{2,0},{3,1},{4,6},{5,7},{6,4},{7,5},{8,10},{9,11},{10,... | collective-permute-start | bytes 110600 | tf_op jit(solution)/shard_map/ppermute | solution.py:334
  19.9 6.0 %collective-permute-start.8 = (f32[72,128]{1,0:T(8,128)S(1)}, f32[72,128]{1,0:T(8,128)S(1)}, u32[]{:S(2)}, u32[]{:S(2)}) collective-permute-start(f32[72,128]{1,0:T(8,128)S(1)} %add_add_fusion.refs_0_), channel_id=1, source_target_pairs={{0,12},{1,13},{2,14},{3,15},{4,8},{5,9},{6,10},{7,11},{8,4},{9,5},... | collective-permute-start | bytes 110600 | tf_op jit(solution)/shard_map/ppermute | solution.py:334
  22.1 5.0 %collective-permute-start.7 = (f32[72,128]{1,0:T(8,128)S(1)}, f32[72,128]{1,0:T(8,128)S(1)}, u32[]{:S(2)}, u32[]{:S(2)}) collective-permute-start(f32[72,128]{1,0:T(8,128)S(1)} %add_add_fusion.refs_0_), channel_id=1, source_target_pairs={{0,8},{1,9},{2,10},{3,11},{4,12},{5,13},{6,14},{7,15},{8,0},{9,1},... | collective-permute-start | bytes 110600 | tf_op jit(solution)/shard_map/ppermute | solution.py:334
  23.0 4.4 %collective-permute-start.6 = (f32[72,128]{1,0:T(8,128)S(1)}, f32[72,128]{1,0:T(8,128)S(1)}, u32[]{:S(2)}, u32[]{:S(2)}) collective-permute-start(f32[72,128]{1,0:T(8,128)S(1)} %add_add_fusion.refs_0_), channel_id=1, source_target_pairs={{0,4},{1,5},{2,6},{3,7},{4,0},{5,1},{6,2},{7,3},{8,12},{9,13},{10,... | collective-permute-start | bytes 110600 | tf_op jit(solution)/shard_map/ppermute | solution.py:334

commit v3 on v2

--- a/solution.py
+++ b/solution.py
@@ -117,17 +117,22 @@
     sums_ref,
 ):
     blocks, block, _ = image_ref.shape
-    odd = lax.axis_index("dom") % 2 == 1
+    here = lax.axis_index("dom")
+    odd = here % 2 == 1
+    first, last = here == 0, here == lax.axis_size("dom") - 1
     inner_state = state_of(inner_ref, HALO * block, HALO)
     outer_state = state_of(outer_ref, HALO * block, HALO)
-    lower_state = jnp.where(odd, inner_state, outer_state)
-    upper_state = jnp.where(odd, outer_state, inner_state)
+    lower_state = jnp.where(first, 0.0, jnp.where(odd, inner_state, outer_state))
+    upper_state = jnp.where(last, 0.0, jnp.where(odd, outer_state, inner_state))
+    nothing = jnp.zeros((block, block), BF16)
 
     def lower(pick):
-        return jnp.where(odd, block_of(inner_ref, pick, block), block_of(outer_ref, pick, block))
+        picked = jnp.where(odd, block_of(inner_ref, pick, block), block_of(outer_ref, pick, block))
+        return jnp.where(first, nothing, picked)
 
     def upper(pick):
-        return jnp.where(odd, block_of(outer_ref, pick, block), block_of(inner_ref, pick, block))
+        picked = jnp.where(odd, block_of(outer_ref, pick, block), block_of(inner_ref, pick, block))
+        return jnp.where(last, nothing, picked)
 
     def chosen(rows, pick):
         row = rows[:1]
@@ -293,17 +298,29 @@
     )(*far(basis.reshape(rows, columns), state))
 
 
+def swap_pairs(parity, groups, devices):
+    pairs = []
+    for group in range(groups):
+        for device in range(devices):
+            other = device + 1 if device % 2 == parity else device - 1
+            if 0 <= other < devices:
+                pairs.append((group * devices + device, group * devices + other))
+            else:
+                twin = group ^ 1 if group ^ 1 < groups else group
+                pairs.append((group * devices + device, twin * devices + device))
+    return pairs
+
+
 def halo(packed, basis, state):
-    devices = lax.axis_size("dom")
+    groups, devices = (lax.axis_size(axis) for axis in AXES)
     odd = lax.axis_index("dom") % 2
     got = []
     for parity in (1, 0):
-        pairs = [(i, i + 1) for i in range(parity, devices - 1, 2)]
         sent = packed
         if basis.shape[0] > HALO:
             up = odd == parity
             sent = pack(*(jnp.where(up, whole[-HALO:], whole[:HALO]) for whole in (basis, state)))
-        got.append(lax.ppermute(sent, "dom", pairs + [(j, i) for i, j in pairs]))
+        got.append(lax.ppermute(sent, AXES, swap_pairs(parity, groups, devices)))
     return got
 
 
@@ -311,13 +328,12 @@
     group, dom = sizes
     dom_bits = [1 << i for i in range(dom.bit_length() - 1)]
     group_bits = [dom << i for i in range(group.bit_length() - 1)]
-    bits = dom_bits[:2] + group_bits + dom_bits[2:]
-    stages = [bits[:1]]
-    rest = bits[1:]
-    while rest:
-        pair, rest = rest[:2], rest[2:]
-        stages.append(pair + [sum(pair)] if len(pair) == 2 else pair)
-    return stages
+    bits = dom_bits[1:2] + group_bits + dom_bits[2:]
+    stages = [dom_bits[:1]]
+    while bits:
+        pair, bits = bits[:2], bits[2:]
+        stages.append([pair[-1], pair[0], sum(pair)] if len(pair) == 2 else pair)
+    return stages[:1] + [[bit | 1 for bit in stage] for stage in stages[1:]]
 
 
 def sum_parts(values):

time: 33.4 us -> 30.9 us (0.925)
  starting transfers between devices: 14.7 us -> 11.8 us
  waiting for transfers between devices: 7.7 us -> 8.07 us
    ppermute x2, starting transfers between devices: 5.03 us -> 3.12 us  [halo(): got.append(lax.ppermute(sent, AXES, swap_pairs(parity, groups, devices)))]
    ppermute x7, starting transfers between devices: 9.67 us -> 8.72 us  [sum_parts(): parts.append(lax.ppermute(total, AXES, pairs))]
    ppermute x2, waiting for transfers between devices: 0.01 us -> 0.53 us  [halo(): got.append(lax.ppermute(sent, AXES, swap_pairs(parity, groups, devices)))]
  transfers between devices with their start and end apart: 9 -> 9, of which waited for: 7 -> 7; matrix products, arithmetic and copies ran while one was open for 0% -> 0% of each run, Pallas kernels for 7% -> 8%
where the time goes in v3:
time: 30.9 us; the launch traced here: 30.7 us
  starting transfers between devices  11.8 us (38%)
  Pallas kernels  10.1 us (33%)
  waiting for transfers between devices  8.07 us (26%)
  between operations  0.66 us (2%)
    ppermute x7, starting transfers between devices, sum_parts(): parts.append(lax.ppermute(total, AXES, pairs))  8.72 us
    ppermute x7, waiting for transfers between devices, sum_parts(): parts.append(lax.ppermute(total, AXES, pairs))  7.54 us
    pallas_call x1, Pallas kernels, body(): pl.pallas_call(functools.partial(finish_kernel, rows_total=float(rows_tot...  5.87 us
    ppermute x2, starting transfers between devices, halo(): got.append(lax.ppermute(sent, AXES, swap_pairs(parity, groups, devices)))  3.12 us
    pallas_call x1, Pallas kernels, body(): pl.pallas_call(local_kernel, out_shape=(pltpu.VMEM(prior_basis.shape, F32...  2.37 us
    pallas_call x1, Pallas kernels, body(): pl.pallas_call(shared_kernel, out_shape=(pltpu.VMEM(prior_basis.shape, F3...  0.96 us
    pallas_call x1, Pallas kernels, pack(): pl.pallas_call(pack_kernel, out_shape=pltpu.VMEM((rows + 16 * pl.cdiv(blo...  0.92 us
  transfers between devices with their start and end apart: 9, of which 7 were waited for; matrix products, arithmetic and copies ran while one was open for 0% of the time, Pallas kernels for 8%

profile of v3, /device:TPU:0, one launch (start us, length us, event | category | flops | bytes accessed | tf_op | source)
XLA Modules:
  0.0 30.7 jit_solution(2509095549092763559)
XLA Ops:
  0.6 0.9 %pack.1.packed_ref.refs_5_ = bf16[528,128]{1,0:T(8,128)(2,1)S(1)} custom-call(bf16[512,128]{1,0:T(8,128)(2,1)} %bitcast.1, bf16[4,128]{1,0:T(4,128)(2,1)} %state_ref.1), custom_call_target="tpu_custom_call" | custom-call | tf_op jit(solution)/shard_map/pack/pallas_call | solution.py:290
  1.6 3.0 %collective-permute-start.1 = (bf16[528,128]{1,0:T(8,128)(2,1)S(1)}, bf16[528,128]{1,0:T(8,128)(2,1)S(1)}, u32[]{:S(2)}, u32[]{:S(2)}) collective-permute-start(bf16[528,128]{1,0:T(8,128)(2,1)S(1)} %pack.1.packed_ref.refs_5_), channel_id=1, source_target_pairs={{0,16},{1,2},{2,1},{3,4},{4,3},{5,6},{6,5},{7,8},{8,7},{9,10},{10,... | collective-permute-start | bytes 405512 | tf_op jit(solution)/shard_map/ppermute | solution.py:323
  4.6 0.1 collective-permute-start
  4.7 2.4 %local_part.1 = (f32[4,128,128]{2,1,0:T(8,128)S(1)}, f32[4,128]{1,0:T(4,128)S(1)}, bf16[4,4,128,128]{3,2,1,0:T(8,128)(2,1)S(1)}, s32[4,4]{1,0:T(4,128)S(4)}, s32[4]{0:T(128)S(4)}) custom-call(s32[4,4]{1,0:T(4,128)} %index_ref.1, s32[4]{0:T(128)} %count_ref.1, bf16[528,128]{1,0:T(8,128)(2,1)S(1)} %pack.1.packed_ref.refs_5_, f32[4,128]{1,0:T(4,128)} %source_ref.1, ...), custom_call_target="tpu_custom_call" | custom-call | tf_op jit(solution)/shard_map/local_part/pallas_call | solution.py:358
  7.1 0.5 %collective-permute-done.1.outer_ref = bf16[528,128]{1,0:T(8,128)(2,1)S(1)} collective-permute-done((bf16[528,128]{1,0:T(8,128)(2,1)S(1)}, bf16[528,128]{1,0:T(8,128)(2,1)S(1)}, u32[]{:S(2)}, u32[]{:S(2)}) %collective-permute-start.1) | collective-permute-done | bytes 135200 | tf_op jit(solution)/shard_map/ppermute | solution.py:323
  7.6 0.0 collective-permute-done.inner_ref
  7.6 1.0 %shared_part.1 = (f32[4,128,128]{2,1,0:T(8,128)S(1)}, f32[4,128]{1,0:T(4,128)S(1)}, bf16[4,128,128]{2,1,0:T(8,128)(2,1)S(1)}, f32[72,128]{1,0:T(8,128)S(1)}) custom-call(s32[4,4]{1,0:T(4,128)S(4)} %get-tuple-element.12.index_ref, s32[4]{0:T(128)S(4)} %get-tuple-element.13.count_ref, ...), custom_call_target="tpu_custom_call", output_to_operand_aliasing={{0}: (5, {}), {1}: (6, {})} | custom-call | tf_op jit(solution)/shard_map/shared_part/pallas_call | solution.py:373
  8.5 0.6 %collective-permute-start.2 = (f32[72,128]{1,0:T(8,128)S(1)}, f32[72,128]{1,0:T(8,128)S(1)}, u32[]{:S(2)}, u32[]{:S(2)}) collective-permute-start(f32[72,128]{1,0:T(8,128)S(1)} %get-tuple-element.17), channel_id=1, source_target_pairs={{0,1},{1,0},{2,3},{3,2},{4,5},{5,4},{6,7},{7,6},{8,9},{9,8},{10,11... | collective-permute-start | bytes 110600 | tf_op jit(solution)/shard_map/ppermute | solution.py:350
  9.1 0.9 %collective-permute-done.2 = f32[72,128]{1,0:T(8,128)S(1)} collective-permute-done((f32[72,128]{1,0:T(8,128)S(1)}, f32[72,128]{1,0:T(8,128)S(1)}, u32[]{:S(2)}, u32[]{:S(2)}) %collective-permute-start.2) | collective-permute-done | bytes 36896 | tf_op jit(solution)/shard_map/ppermute | solution.py:350
  10.0 3.4 %collective-permute-start.5 = (f32[72,128]{1,0:T(8,128)S(1)}, f32[72,128]{1,0:T(8,128)S(1)}, u32[]{:S(2)}, u32[]{:S(2)}) collective-permute-start(f32[72,128]{1,0:T(8,128)S(1)} %add.12), channel_id=1, source_target_pairs={{0,19},{1,18},{2,17},{3,16},{4,23},{5,22},{6,21},{7,20},{8,27},{9,... | collective-permute-start | bytes 110600 | tf_op jit(solution)/shard_map/ppermute | solution.py:350
  13.4 0.0 collective-permute-start.4
  13.4 0.6 %collective-permute-start.3 = (f32[72,128]{1,0:T(8,128)S(1)}, f32[72,128]{1,0:T(8,128)S(1)}, u32[]{:S(2)}, u32[]{:S(2)}) collective-permute-start(f32[72,128]{1,0:T(8,128)S(1)} %add.12), channel_id=1, source_target_pairs={{0,17},{1,16},{2,19},{3,18},{4,21},{5,20},{6,23},{7,22},{8,25},{9,... | collective-permute-start | bytes 110600 | tf_op jit(solution)/shard_map/ppermute | solution.py:350
  14.0 1.3 %collective-permute-done.5 = f32[72,128]{1,0:T(8,128)S(1)} collective-permute-done((f32[72,128]{1,0:T(8,128)S(1)}, f32[72,128]{1,0:T(8,128)S(1)}, u32[]{:S(2)}, u32[]{:S(2)}) %collective-permute-start.5) | collective-permute-done | bytes 36896 | tf_op jit(solution)/shard_map/ppermute | solution.py:350
  15.3 1.5 %collective-permute-done.4 = f32[72,128]{1,0:T(8,128)S(1)} collective-permute-done((f32[72,128]{1,0:T(8,128)S(1)}, f32[72,128]{1,0:T(8,128)S(1)}, u32[]{:S(2)}, u32[]{:S(2)}) %collective-permute-start.4) | collective-permute-done | bytes 36896 | tf_op jit(solution)/shard_map/ppermute | solution.py:350
  16.8 0.0 collective-permute-done.3
  16.8 3.6 %collective-permute-start.8 = (f32[72,128]{1,0:T(8,128)S(1)}, f32[72,128]{1,0:T(8,128)S(1)}, u32[]{:S(2)}, u32[]{:S(2)}) collective-permute-start(f32[72,128]{1,0:T(8,128)S(1)} %add_add_fusion.refs_0_), channel_id=1, source_target_pairs={{0,13},{1,12},{2,15},{3,14},{4,9},{5,8},{6,11},{7,10},{8,5},{9,4},... | collective-permute-start | bytes 110600 | tf_op jit(solution)/shard_map/ppermute | solution.py:350
  20.4 0.0 collective-permute-start.7
  20.5 0.5 %collective-permute-start.6 = (f32[72,128]{1,0:T(8,128)S(1)}, f32[72,128]{1,0:T(8,128)S(1)}, u32[]{:S(2)}, u32[]{:S(2)}) collective-permute-start(f32[72,128]{1,0:T(8,128)S(1)} %add_add_fusion.refs_0_), channel_id=1, source_target_pairs={{0,9},{1,8},{2,11},{3,10},{4,13},{5,12},{6,15},{7,14},{8,1},{9,0},... | collective-permute-start | bytes 110600 | tf_op jit(solution)/shard_map/ppermute | solution.py:350
  21.0 1.3 %collective-permute-done.8.refs_3_ = f32[72,128]{1,0:T(8,128)S(1)} collective-permute-done((f32[72,128]{1,0:T(8,128)S(1)}, f32[72,128]{1,0:T(8,128)S(1)}, u32[]{:S(2)}, u32[]{:S(2)}) %collective-permute-start.8) | collective-permute-done | bytes 36896 | tf_op jit(solution)/shard_map/ppermute | solution.py:350
  22.2 1.7 %collective-permute-done.7.refs_2_ = f32[72,128]{1,0:T(8,128)S(1)} collective-permute-done((f32[72,128]{1,0:T(8,128)S(1)}, f32[72,128]{1,0:T(8,128)S(1)}, u32[]{:S(2)}, u32[]{:S(2)}) %collective-permute-start.7) | collective-permute-done | bytes 36896 | tf_op jit(solution)/shard_map/ppermute | solution.py:350
  23.9 0.9 %collective-permute-done.6.refs_1_ = f32[72,128]{1,0:T(8,128)S(1)} collective-permute-done((f32[72,128]{1,0:T(8,128)S(1)}, f32[72,128]{1,0:T(8,128)S(1)}, u32[]{:S(2)}, u32[]{:S(2)}) %collective-permute-start.6) | collective-permute-done | bytes 36896 | tf_op jit(solution)/shard_map/ppermute | solution.py:350
  24.8 5.9 %finish.1 = (bf16[4,128,128]{2,1,0:T(8,128)(2,1)}, bf16[4,128,128]{2,1,0:T(8,128)(2,1)}, f32[4,128]{1,0:T(4,128)}, f32[4,128]{1,0:T(4,128)}) custom-call(f32[72,128]{1,0:T(8,128)S(1)} %add_add_fusion.refs_0_, f32[72,128]{1,0:T(8,128)S(1)} %collective-permute-done.6.refs_1_, f32[72,128]{1,0:T(8,128)S(1)} %collective-permute-done.7.refs_2_, ...), custom_call_target="tpu_custom_call" | custom-call | tf_op jit(solution)/shard_map/finish/pallas_call | solution.py:392
  (2 shorter events, 0.0 us)
Async XLA Ops:
  1.6 6.0 %collective-permute-start.1 = (bf16[528,128]{1,0:T(8,128)(2,1)S(1)}, bf16[528,128]{1,0:T(8,128)(2,1)S(1)}, u32[]{:S(2)}, u32[]{:S(2)}) collective-permute-start(bf16[528,128]{1,0:T(8,128)(2,1)S(1)} %pack.1.packed_ref.refs_5_), channel_id=1, source_target_pairs={{0,16},{1,2},{2,1},{3,4},{4,3},{5,6},{6,5},{7,8},{8,7},{9,10},{10,... | collective-permute-start | bytes 405512 | tf_op jit(solution)/shard_map/ppermute | solution.py:323
  4.6 3.0 %collective-permute-start = (bf16[528,128]{1,0:T(8,128)(2,1)S(1)}, bf16[528,128]{1,0:T(8,128)(2,1)S(1)}, u32[]{:S(2)}, u32[]{:S(2)}) collective-permute-start(bf16[528,128]{1,0:T(8,128)(2,1)S(1)} %pack.1.packed_ref.refs_5_), channel_id=1, source_target_pairs={{0,1},{1,0},{2,3},{3,2},{4,5},{5,4},{6,7},{7,6},{8,9},{9,8},{10,11... | collective-permute-start | bytes 405512 | tf_op jit(solution)/shard_map/ppermute | solution.py:323
  8.5 1.4 %collective-permute-start.2 = (f32[72,128]{1,0:T(8,128)S(1)}, f32[72,128]{1,0:T(8,128)S(1)}, u32[]{:S(2)}, u32[]{:S(2)}) collective-permute-start(f32[72,128]{1,0:T(8,128)S(1)} %get-tuple-element.17), channel_id=1, source_target_pairs={{0,1},{1,0},{2,3},{3,2},{4,5},{5,4},{6,7},{7,6},{8,9},{9,8},{10,11... | collective-permute-start | bytes 110600 | tf_op jit(solution)/shard_map/ppermute | solution.py:350
  10.0 5.3 %collective-permute-start.5 = (f32[72,128]{1,0:T(8,128)S(1)}, f32[72,128]{1,0:T(8,128)S(1)}, u32[]{:S(2)}, u32[]{:S(2)}) collective-permute-start(f32[72,128]{1,0:T(8,128)S(1)} %add.12), channel_id=1, source_target_pairs={{0,19},{1,18},{2,17},{3,16},{4,23},{5,22},{6,21},{7,20},{8,27},{9,... | collective-permute-start | bytes 110600 | tf_op jit(solution)/shard_map/ppermute | solution.py:350
  13.4 3.4 %collective-permute-start.4 = (f32[72,128]{1,0:T(8,128)S(1)}, f32[72,128]{1,0:T(8,128)S(1)}, u32[]{:S(2)}, u32[]{:S(2)}) collective-permute-start(f32[72,128]{1,0:T(8,128)S(1)} %add.12), channel_id=1, source_target_pairs={{0,3},{1,2},{2,1},{3,0},{4,7},{5,6},{6,5},{7,4},{8,11},{9,10},{10,... | collective-permute-start | bytes 110600 | tf_op jit(solution)/shard_map/ppermute | solution.py:350
  13.4 3.4 %collective-permute-start.3 = (f32[72,128]{1,0:T(8,128)S(1)}, f32[72,128]{1,0:T(8,128)S(1)}, u32[]{:S(2)}, u32[]{:S(2)}) collective-permute-start(f32[72,128]{1,0:T(8,128)S(1)} %add.12), channel_id=1, source_target_pairs={{0,17},{1,16},{2,19},{3,18},{4,21},{5,20},{6,23},{7,22},{8,25},{9,... | collective-permute-start | bytes 110600 | tf_op jit(solution)/shard_map/ppermute | solution.py:350
  16.8 5.4 %collective-permute-start.8 = (f32[72,128]{1,0:T(8,128)S(1)}, f32[72,128]{1,0:T(8,128)S(1)}, u32[]{:S(2)}, u32[]{:S(2)}) collective-permute-start(f32[72,128]{1,0:T(8,128)S(1)} %add_add_fusion.refs_0_), channel_id=1, source_target_pairs={{0,13},{1,12},{2,15},{3,14},{4,9},{5,8},{6,11},{7,10},{8,5},{9,4},... | collective-permute-start | bytes 110600 | tf_op jit(solution)/shard_map/ppermute | solution.py:350
  20.4 3.5 %collective-permute-start.7 = (f32[72,128]{1,0:T(8,128)S(1)}, f32[72,128]{1,0:T(8,128)S(1)}, u32[]{:S(2)}, u32[]{:S(2)}) collective-permute-start(f32[72,128]{1,0:T(8,128)S(1)} %add_add_fusion.refs_0_), channel_id=1, source_target_pairs={{0,5},{1,4},{2,7},{3,6},{4,1},{5,0},{6,3},{7,2},{8,13},{9,12},{10,... | collective-permute-start | bytes 110600 | tf_op jit(solution)/shard_map/ppermute | solution.py:350
  20.5 4.4 %collective-permute-start.6 = (f32[72,128]{1,0:T(8,128)S(1)}, f32[72,128]{1,0:T(8,128)S(1)}, u32[]{:S(2)}, u32[]{:S(2)}) collective-permute-start(f32[72,128]{1,0:T(8,128)S(1)} %add_add_fusion.refs_0_), channel_id=1, source_target_pairs={{0,9},{1,8},{2,11},{3,10},{4,13},{5,12},{6,15},{7,14},{8,1},{9,0},... | collective-permute-start | bytes 110600 | tf_op jit(solution)/shard_map/ppermute | solution.py:350

commit v4 on v3

--- a/solution.py
+++ b/solution.py
@@ -182,53 +182,81 @@
     return jnp.broadcast_to(value, shape)
 
 
-def eliminate(rows):
+def eliminate(rows, wide_ref, pair_ref):
     order = rows[0].shape[1]
     panels = len(rows)
     rows = list(rows)
     shape = (PANEL, order)
     lane = lax.broadcasted_iota(jnp.int32, shape, 1)
     sub = lax.broadcasted_iota(jnp.int32, shape, 0)
+
+    def update(q, c, solved):
+        terms = [spread(rows[q][:, c + k : c + k + 1], shape) * solved[k] for k in range(PANEL)]
+        while len(terms) > 1:
+            terms = [x + y for x, y in zip(terms[::2], terms[1::2])]
+        rows[q] = jnp.where((lane >= c) & (lane < c + PANEL), 0.0, rows[q]) - terms[0]
+
     done = []
+    waiting = []
     for p in range(panels):
         c = p * PANEL
         panel = (lane >= c) & (lane < c + PANEL)
-        wide = [spread(rows[p][i : i + 1], shape) for i in range(PANEL)]
+        columns = [spread(rows[p][:, c + j : c + j + 1], shape) for j in range(PANEL)]
+        at = p % 2 * PANEL
+        wide_ref[at : at + PANEL, :] = jnp.where(panel, 0.0, rows[p])
+        for j in range(PANEL):
+            base = (at + j) * PANEL
+            pair_ref[base : base + PANEL, :] = columns[j]
+        wide = [spread(wide_ref[at + i : at + i + 1, :], shape) for i in range(PANEL)]
         a = [
-            [spread(wide[i][:, c + j : c + j + 1], shape) if j >= i else None for j in range(PANEL)]
+            [
+                spread(pair_ref[(at + j) * PANEL + i : (at + j) * PANEL + i + 1, :], shape) if j >= i else None
+                for j in range(PANEL)
+            ]
             for i in range(PANEL)
         ]
-        wide = [jnp.where(panel, 0.0, row) for row in wide]
-        below = {}
-        for q in range(p + 1, panels):
-            below[q] = [spread(rows[q][:, c + k : c + k + 1], shape) for k in range(PANEL)]
-            rows[q] = jnp.where(panel, 0.0, rows[q])
         out = jnp.zeros(shape, F32)
+        solved = [None] * PANEL
         for k in range(PANEL):
             pivot = a[k][k]
             root = lax.rsqrt(pivot)
-            inv = 1.0 / pivot
+            if k % 2 == 0:
+                inv = pl.reciprocal(pivot, approx=True)
+                minor = pivot * a[k + 1][k + 1] - a[k][k + 1] * a[k][k + 1]
+                next_inv = pivot * pl.reciprocal(minor, approx=True)
+            else:
+                inv = next_inv
             unit = jnp.where(lane == c + k, 1.0, wide[k])
-            scaled = unit * inv
+            out = jnp.where(sub == k, unit * root, out)
+            solved[k] = unit * inv
             factor = [None] * PANEL
+            for j in range(k + 1, PANEL):
+                factor[j] = a[k][j] * inv
             for i in range(k + 1, PANEL):
-                factor[i] = a[k][i] * inv
                 for j in range(i, PANEL):
                     a[i][j] = a[i][j] - factor[i] * a[k][j]
                 wide[i] = wide[i] - factor[i] * unit
-            for q in range(p + 1, panels):
+            for i in range(k):
                 for j in range(k + 1, PANEL):
-                    below[q][j] = below[q][j] - below[q][k] * factor[j]
-                rows[q] = rows[q] - below[q][k] * scaled
-            out = jnp.where(sub == k, unit * root, out)
+                    a[i][j] = a[i][j] - a[i][k] * factor[j]
+                solved[i] = solved[i] - a[i][k] * solved[k]
+            for j in range(k + 1, PANEL):
+                a[k][j] = factor[j]
+            share = pl.cdiv(len(waiting), PANEL - k)
+            for job in waiting[:share]:
+                update(*job)
+            waiting = waiting[share:]
+        if p + 1 < panels:
+            update(p + 1, c, solved)
+        waiting = [(q, c, solved) for q in range(p + 2, panels)]
         done.append(jnp.where(lane <= c + sub, out, 0.0))
     return done
 
 
 def finish_kernel(*refs, rows_total):
-    sum_refs = refs[:-9]
-    image_ref, packed_ref, rhs_ref, new_ref, new_image_ref, guess_ref, residual_ref = refs[-9:-2]
-    gram_ref, factor_ref = refs[-2:]
+    sum_refs = refs[:-11]
+    image_ref, packed_ref, rhs_ref, new_ref, new_image_ref, guess_ref, residual_ref = refs[-11:-4]
+    gram_ref, factor_ref, wide_ref, pair_ref = refs[-4:]
     blocks, block, _ = image_ref.shape
     half = block // 2
     packed = sum_refs[0][...]
@@ -247,7 +275,7 @@
     row = lax.broadcasted_iota(jnp.int32, (block, block), 0)
     col = lax.broadcasted_iota(jnp.int32, (block, block), 1)
     gram_ref[...] = once + jnp.where(row == col, 0.0, once.T)
-    done = eliminate([gram_ref[p : p + PANEL, :] for p in range(0, block, PANEL)])
+    done = eliminate([gram_ref[p : p + PANEL, :] for p in range(0, block, PANEL)], wide_ref, pair_ref)
     for p, panel in enumerate(done):
         factor_ref[p * PANEL : (p + 1) * PANEL, :] = panel
     factor = factor_ref[...]
@@ -349,6 +377,24 @@
             pairs = [(i, i ^ bit) for i in range(devices)]
             parts.append(lax.ppermute(total, AXES, pairs))
     return parts
+
+
+def finish(parts, image, packed, rhs, rows_total):
+    blocks, block, columns = image.shape
+    return pl.pallas_call(
+        functools.partial(finish_kernel, rows_total=rows_total),
+        out_shape=(
+            jax.ShapeDtypeStruct(image.shape, BF16),
+            jax.ShapeDtypeStruct(image.shape, BF16),
+            jax.ShapeDtypeStruct(rhs.shape, F32),
+            jax.ShapeDtypeStruct(rhs.shape, F32),
+        ),
+        in_specs=[vmem()] * (len(parts) + 3),
+        out_specs=(vmem(),) * 4,
+        scratch_shapes=[pltpu.VMEM((block, columns), F32)] * 2 + [pltpu.VMEM((2 * PANEL, columns), F32), pltpu.VMEM((2 * PANEL * PANEL, columns), F32)],
+        compiler_params=pltpu.CompilerParams(vmem_limit_bytes=VMEM_LIMIT),
+        name="finish",
+    )(*near(*parts, image, packed, rhs))
 
 
 def body(prior_basis, section_state, source, diag_blocks, coupling, neighbour_index, slot_count):
@@ -389,20 +435,7 @@
     )
     parts = sum_parts(sums)
     rows_total = blocks * block * lax.axis_size("group") * lax.axis_size("dom")
-    return pl.pallas_call(
-        functools.partial(finish_kernel, rows_total=float(rows_total)),
-        out_shape=(
-            jax.ShapeDtypeStruct(prior_basis.shape, BF16),
-            jax.ShapeDtypeStruct(prior_basis.shape, BF16),
-            jax.ShapeDtypeStruct(source.shape, F32),
-            jax.ShapeDtypeStruct(source.shape, F32),
-        ),
-        in_specs=[vmem()] * (len(parts) + 3),
-        out_specs=(vmem(),) * 4,
-        scratch_shapes=[pltpu.VMEM((block, columns), F32)] * 2,
-        compiler_params=pltpu.CompilerParams(vmem_limit_bytes=VMEM_LIMIT),
-        name="finish",
-    )(*near(*parts, image, packed, rhs))
+    return finish(parts, image, packed, rhs, float(rows_total))
 
 
 def solution(mesh):

time: 30.9 us -> 29.4 us (0.951)
  Pallas kernels: 10.1 us -> 8.65 us
    pallas_call x1, Pallas kernels: 5.87 us -> 4.41 us  [finish(): pl.pallas_call(functools.partial(finish_kernel, rows_total=rows_total), o...]
where the time goes in v4:
time: 29.4 us; the launch traced here: 29.2 us
  starting transfers between devices  11.8 us (40%)
  Pallas kernels  8.65 us (29%)
  waiting for transfers between devices  8.07 us (27%)
  between operations  0.66 us (2%)
    ppermute x7, starting transfers between devices, sum_parts(): parts.append(lax.ppermute(total, AXES, pairs))  8.72 us
    ppermute x7, waiting for transfers between devices, sum_parts(): parts.append(lax.ppermute(total, AXES, pairs))  7.54 us
    pallas_call x1, Pallas kernels, finish(): pl.pallas_call(functools.partial(finish_kernel, rows_total=rows_total), o...  4.41 us
    ppermute x2, starting transfers between devices, halo(): got.append(lax.ppermute(sent, AXES, swap_pairs(parity, groups, devices)))  3.12 us
    pallas_call x1, Pallas kernels, body(): pl.pallas_call(local_kernel, out_shape=(pltpu.VMEM(prior_basis.shape, F32...  2.37 us
    pallas_call x1, Pallas kernels, body(): pl.pallas_call(shared_kernel, out_shape=(pltpu.VMEM(prior_basis.shape, F3...  0.96 us
    pallas_call x1, Pallas kernels, pack(): pl.pallas_call(pack_kernel, out_shape=pltpu.VMEM((rows + 16 * pl.cdiv(blo...  0.92 us
  transfers between devices with their start and end apart: 9, of which 7 were waited for; matrix products, arithmetic and copies ran while one was open for 0% of the time, Pallas kernels for 8%

profile of v4, /device:TPU:0, one launch (start us, length us, event | category | flops | bytes accessed | tf_op | source)
XLA Modules:
  0.0 29.2 jit_solution(16835940522597686366)
XLA Ops:
  0.6 0.9 %pack.1.packed_ref.refs_5_ = bf16[528,128]{1,0:T(8,128)(2,1)S(1)} custom-call(bf16[512,128]{1,0:T(8,128)(2,1)} %bitcast.1, bf16[4,128]{1,0:T(4,128)(2,1)} %state_ref.1), custom_call_target="tpu_custom_call" | custom-call | tf_op jit(solution)/shard_map/pack/pallas_call | solution.py:318
  1.6 3.0 %collective-permute-start.1 = (bf16[528,128]{1,0:T(8,128)(2,1)S(1)}, bf16[528,128]{1,0:T(8,128)(2,1)S(1)}, u32[]{:S(2)}, u32[]{:S(2)}) collective-permute-start(bf16[528,128]{1,0:T(8,128)(2,1)S(1)} %pack.1.packed_ref.refs_5_), channel_id=1, source_target_pairs={{0,16},{1,2},{2,1},{3,4},{4,3},{5,6},{6,5},{7,8},{8,7},{9,10},{10,... | collective-permute-start | bytes 405512 | tf_op jit(solution)/shard_map/ppermute | solution.py:351
  4.6 0.1 collective-permute-start
  4.7 2.4 %local_part.1 = (f32[4,128,128]{2,1,0:T(8,128)S(1)}, f32[4,128]{1,0:T(4,128)S(1)}, bf16[4,4,128,128]{3,2,1,0:T(8,128)(2,1)S(1)}, s32[4,4]{1,0:T(4,128)S(4)}, s32[4]{0:T(128)S(4)}) custom-call(s32[4,4]{1,0:T(4,128)} %index_ref.1, s32[4]{0:T(128)} %count_ref.1, bf16[528,128]{1,0:T(8,128)(2,1)S(1)} %pack.1.packed_ref.refs_5_, f32[4,128]{1,0:T(4,128)} %source_ref.1, ...), custom_call_target="tpu_custom_call" | custom-call | tf_op jit(solution)/shard_map/local_part/pallas_call | solution.py:404
  7.1 0.5 %collective-permute-done.1.outer_ref = bf16[528,128]{1,0:T(8,128)(2,1)S(1)} collective-permute-done((bf16[528,128]{1,0:T(8,128)(2,1)S(1)}, bf16[528,128]{1,0:T(8,128)(2,1)S(1)}, u32[]{:S(2)}, u32[]{:S(2)}) %collective-permute-start.1) | collective-permute-done | bytes 135200 | tf_op jit(solution)/shard_map/ppermute | solution.py:351
  7.6 0.0 collective-permute-done.inner_ref
  7.6 1.0 %shared_part.1 = (f32[4,128,128]{2,1,0:T(8,128)S(1)}, f32[4,128]{1,0:T(4,128)S(1)}, bf16[4,128,128]{2,1,0:T(8,128)(2,1)S(1)}, f32[72,128]{1,0:T(8,128)S(1)}) custom-call(s32[4,4]{1,0:T(4,128)S(4)} %get-tuple-element.12.index_ref, s32[4]{0:T(128)S(4)} %get-tuple-element.13.count_ref, ...), custom_call_target="tpu_custom_call", output_to_operand_aliasing={{0}: (5, {}), {1}: (6, {})} | custom-call | tf_op jit(solution)/shard_map/shared_part/pallas_call | solution.py:419
  8.5 0.6 %collective-permute-start.2 = (f32[72,128]{1,0:T(8,128)S(1)}, f32[72,128]{1,0:T(8,128)S(1)}, u32[]{:S(2)}, u32[]{:S(2)}) collective-permute-start(f32[72,128]{1,0:T(8,128)S(1)} %get-tuple-element.17), channel_id=1, source_target_pairs={{0,1},{1,0},{2,3},{3,2},{4,5},{5,4},{6,7},{7,6},{8,9},{9,8},{10,11... | collective-permute-start | bytes 110600 | tf_op jit(solution)/shard_map/ppermute | solution.py:378
  9.1 0.9 %collective-permute-done.2 = f32[72,128]{1,0:T(8,128)S(1)} collective-permute-done((f32[72,128]{1,0:T(8,128)S(1)}, f32[72,128]{1,0:T(8,128)S(1)}, u32[]{:S(2)}, u32[]{:S(2)}) %collective-permute-start.2) | collective-permute-done | bytes 36896 | tf_op jit(solution)/shard_map/ppermute | solution.py:378
  10.0 3.4 %collective-permute-start.5 = (f32[72,128]{1,0:T(8,128)S(1)}, f32[72,128]{1,0:T(8,128)S(1)}, u32[]{:S(2)}, u32[]{:S(2)}) collective-permute-start(f32[72,128]{1,0:T(8,128)S(1)} %add.12), channel_id=1, source_target_pairs={{0,19},{1,18},{2,17},{3,16},{4,23},{5,22},{6,21},{7,20},{8,27},{9,... | collective-permute-start | bytes 110600 | tf_op jit(solution)/shard_map/ppermute | solution.py:378
  13.4 0.0 collective-permute-start.4
  13.4 0.6 %collective-permute-start.3 = (f32[72,128]{1,0:T(8,128)S(1)}, f32[72,128]{1,0:T(8,128)S(1)}, u32[]{:S(2)}, u32[]{:S(2)}) collective-permute-start(f32[72,128]{1,0:T(8,128)S(1)} %add.12), channel_id=1, source_target_pairs={{0,17},{1,16},{2,19},{3,18},{4,21},{5,20},{6,23},{7,22},{8,25},{9,... | collective-permute-start | bytes 110600 | tf_op jit(solution)/shard_map/ppermute | solution.py:378
  14.0 1.3 %collective-permute-done.5 = f32[72,128]{1,0:T(8,128)S(1)} collective-permute-done((f32[72,128]{1,0:T(8,128)S(1)}, f32[72,128]{1,0:T(8,128)S(1)}, u32[]{:S(2)}, u32[]{:S(2)}) %collective-permute-start.5) | collective-permute-done | bytes 36896 | tf_op jit(solution)/shard_map/ppermute | solution.py:378
  15.3 1.5 %collective-permute-done.4 = f32[72,128]{1,0:T(8,128)S(1)} collective-permute-done((f32[72,128]{1,0:T(8,128)S(1)}, f32[72,128]{1,0:T(8,128)S(1)}, u32[]{:S(2)}, u32[]{:S(2)}) %collective-permute-start.4) | collective-permute-done | bytes 36896 | tf_op jit(solution)/shard_map/ppermute | solution.py:378
  16.8 0.0 collective-permute-done.3
  16.8 3.6 %collective-permute-start.8 = (f32[72,128]{1,0:T(8,128)S(1)}, f32[72,128]{1,0:T(8,128)S(1)}, u32[]{:S(2)}, u32[]{:S(2)}) collective-permute-start(f32[72,128]{1,0:T(8,128)S(1)} %add_add_fusion.refs_0_), channel_id=1, source_target_pairs={{0,13},{1,12},{2,15},{3,14},{4,9},{5,8},{6,11},{7,10},{8,5},{9,4},... | collective-permute-start | bytes 110600 | tf_op jit(solution)/shard_map/ppermute | solution.py:378
  20.4 0.0 collective-permute-start.7
  20.5 0.5 %collective-permute-start.6 = (f32[72,128]{1,0:T(8,128)S(1)}, f32[72,128]{1,0:T(8,128)S(1)}, u32[]{:S(2)}, u32[]{:S(2)}) collective-permute-start(f32[72,128]{1,0:T(8,128)S(1)} %add_add_fusion.refs_0_), channel_id=1, source_target_pairs={{0,9},{1,8},{2,11},{3,10},{4,13},{5,12},{6,15},{7,14},{8,1},{9,0},... | collective-permute-start | bytes 110600 | tf_op jit(solution)/shard_map/ppermute | solution.py:378
  21.0 1.3 %collective-permute-done.8.refs_3_ = f32[72,128]{1,0:T(8,128)S(1)} collective-permute-done((f32[72,128]{1,0:T(8,128)S(1)}, f32[72,128]{1,0:T(8,128)S(1)}, u32[]{:S(2)}, u32[]{:S(2)}) %collective-permute-start.8) | collective-permute-done | bytes 36896 | tf_op jit(solution)/shard_map/ppermute | solution.py:378
  22.2 1.7 %collective-permute-done.7.refs_2_ = f32[72,128]{1,0:T(8,128)S(1)} collective-permute-done((f32[72,128]{1,0:T(8,128)S(1)}, f32[72,128]{1,0:T(8,128)S(1)}, u32[]{:S(2)}, u32[]{:S(2)}) %collective-permute-start.7) | collective-permute-done | bytes 36896 | tf_op jit(solution)/shard_map/ppermute | solution.py:378
  23.9 0.9 %collective-permute-done.6.refs_1_ = f32[72,128]{1,0:T(8,128)S(1)} collective-permute-done((f32[72,128]{1,0:T(8,128)S(1)}, f32[72,128]{1,0:T(8,128)S(1)}, u32[]{:S(2)}, u32[]{:S(2)}) %collective-permute-start.6) | collective-permute-done | bytes 36896 | tf_op jit(solution)/shard_map/ppermute | solution.py:378
  24.8 4.4 %finish.1 = (bf16[4,128,128]{2,1,0:T(8,128)(2,1)}, bf16[4,128,128]{2,1,0:T(8,128)(2,1)}, f32[4,128]{1,0:T(4,128)}, f32[4,128]{1,0:T(4,128)}) custom-call(f32[72,128]{1,0:T(8,128)S(1)} %add_add_fusion.refs_0_, f32[72,128]{1,0:T(8,128)S(1)} %collective-permute-done.6.refs_1_, f32[72,128]{1,0:T(8,128)S(1)} %collective-permute-done.7.refs_2_, ...), custom_call_target="tpu_custom_call" | custom-call | tf_op jit(solution)/shard_map/finish/pallas_call | solution.py:384
  (2 shorter events, 0.0 us)
Async XLA Ops:
  1.6 6.0 %collective-permute-start.1 = (bf16[528,128]{1,0:T(8,128)(2,1)S(1)}, bf16[528,128]{1,0:T(8,128)(2,1)S(1)}, u32[]{:S(2)}, u32[]{:S(2)}) collective-permute-start(bf16[528,128]{1,0:T(8,128)(2,1)S(1)} %pack.1.packed_ref.refs_5_), channel_id=1, source_target_pairs={{0,16},{1,2},{2,1},{3,4},{4,3},{5,6},{6,5},{7,8},{8,7},{9,10},{10,... | collective-permute-start | bytes 405512 | tf_op jit(solution)/shard_map/ppermute | solution.py:351
  4.6 3.0 %collective-permute-start = (bf16[528,128]{1,0:T(8,128)(2,1)S(1)}, bf16[528,128]{1,0:T(8,128)(2,1)S(1)}, u32[]{:S(2)}, u32[]{:S(2)}) collective-permute-start(bf16[528,128]{1,0:T(8,128)(2,1)S(1)} %pack.1.packed_ref.refs_5_), channel_id=1, source_target_pairs={{0,1},{1,0},{2,3},{3,2},{4,5},{5,4},{6,7},{7,6},{8,9},{9,8},{10,11... | collective-permute-start | bytes 405512 | tf_op jit(solution)/shard_map/ppermute | solution.py:351
  8.5 1.4 %collective-permute-start.2 = (f32[72,128]{1,0:T(8,128)S(1)}, f32[72,128]{1,0:T(8,128)S(1)}, u32[]{:S(2)}, u32[]{:S(2)}) collective-permute-start(f32[72,128]{1,0:T(8,128)S(1)} %get-tuple-element.17), channel_id=1, source_target_pairs={{0,1},{1,0},{2,3},{3,2},{4,5},{5,4},{6,7},{7,6},{8,9},{9,8},{10,11... | collective-permute-start | bytes 110600 | tf_op jit(solution)/shard_map/ppermute | solution.py:378
  10.0 5.3 %collective-permute-start.5 = (f32[72,128]{1,0:T(8,128)S(1)}, f32[72,128]{1,0:T(8,128)S(1)}, u32[]{:S(2)}, u32[]{:S(2)}) collective-permute-start(f32[72,128]{1,0:T(8,128)S(1)} %add.12), channel_id=1, source_target_pairs={{0,19},{1,18},{2,17},{3,16},{4,23},{5,22},{6,21},{7,20},{8,27},{9,... | collective-permute-start | bytes 110600 | tf_op jit(solution)/shard_map/ppermute | solution.py:378
  13.4 3.4 %collective-permute-start.4 = (f32[72,128]{1,0:T(8,128)S(1)}, f32[72,128]{1,0:T(8,128)S(1)}, u32[]{:S(2)}, u32[]{:S(2)}) collective-permute-start(f32[72,128]{1,0:T(8,128)S(1)} %add.12), channel_id=1, source_target_pairs={{0,3},{1,2},{2,1},{3,0},{4,7},{5,6},{6,5},{7,4},{8,11},{9,10},{10,... | collective-permute-start | bytes 110600 | tf_op jit(solution)/shard_map/ppermute | solution.py:378
  13.4 3.4 %collective-permute-start.3 = (f32[72,128]{1,0:T(8,128)S(1)}, f32[72,128]{1,0:T(8,128)S(1)}, u32[]{:S(2)}, u32[]{:S(2)}) collective-permute-start(f32[72,128]{1,0:T(8,128)S(1)} %add.12), channel_id=1, source_target_pairs={{0,17},{1,16},{2,19},{3,18},{4,21},{5,20},{6,23},{7,22},{8,25},{9,... | collective-permute-start | bytes 110600 | tf_op jit(solution)/shard_map/ppermute | solution.py:378
  16.8 5.4 %collective-permute-start.8 = (f32[72,128]{1,0:T(8,128)S(1)}, f32[72,128]{1,0:T(8,128)S(1)}, u32[]{:S(2)}, u32[]{:S(2)}) collective-permute-start(f32[72,128]{1,0:T(8,128)S(1)} %add_add_fusion.refs_0_), channel_id=1, source_target_pairs={{0,13},{1,12},{2,15},{3,14},{4,9},{5,8},{6,11},{7,10},{8,5},{9,4},... | collective-permute-start | bytes 110600 | tf_op jit(solution)/shard_map/ppermute | solution.py:378
  20.4 3.5 %collective-permute-start.7 = (f32[72,128]{1,0:T(8,128)S(1)}, f32[72,128]{1,0:T(8,128)S(1)}, u32[]{:S(2)}, u32[]{:S(2)}) collective-permute-start(f32[72,128]{1,0:T(8,128)S(1)} %add_add_fusion.refs_0_), channel_id=1, source_target_pairs={{0,5},{1,4},{2,7},{3,6},{4,1},{5,0},{6,3},{7,2},{8,13},{9,12},{10,... | collective-permute-start | bytes 110600 | tf_op jit(solution)/shard_map/ppermute | solution.py:378
  20.5 4.4 %collective-permute-start.6 = (f32[72,128]{1,0:T(8,128)S(1)}, f32[72,128]{1,0:T(8,128)S(1)}, u32[]{:S(2)}, u32[]{:S(2)}) collective-permute-start(f32[72,128]{1,0:T(8,128)S(1)} %add_add_fusion.refs_0_), channel_id=1, source_target_pairs={{0,9},{1,8},{2,11},{3,10},{4,13},{5,12},{6,15},{7,14},{8,1},{9,0},... | collective-permute-start | bytes 110600 | tf_op jit(solution)/shard_map/ppermute | solution.py:378

commit v5 on v4

--- a/solution.py
+++ b/solution.py
@@ -172,7 +172,8 @@
     sub = lax.broadcasted_iota(jnp.int32, (half, block), 0)
     lane = lax.broadcasted_iota(jnp.int32, (half, block), 1)
     sums_ref[:half] = jnp.where(lane < sub, pltpu.roll(bottom, half, 1), top)
-    pivots = jnp.sum(jnp.where(lane == sub + half, bottom, 0.0), axis=0, keepdims=True)
+    pivots = jnp.where(lane == sub, top, jnp.where(lane == sub + half, bottom, 0.0))
+    pivots = jnp.sum(pivots, axis=0, keepdims=True)
     row = lax.broadcasted_iota(jnp.int32, (8, block), 0)
     total = jnp.sum(moment, axis=0, keepdims=True)
     sums_ref[half:] = jnp.where(row == 0, pivots, jnp.where(row == 1, total, 0.0))
@@ -262,24 +263,23 @@
     packed = sum_refs[0][...]
     for ref in sum_refs[1:]:
         packed = packed + ref[...]
-    packed = packed * (1.0 / rows_total)
-    top = packed[:half]
+    top, pivots = packed[:half], packed[half : half + 1]
     sub = lax.broadcasted_iota(jnp.int32, (half, block), 0)
     lane = lax.broadcasted_iota(jnp.int32, (half, block), 1)
     upper = jnp.where(lane >= sub, top, 0.0)
-    shifted = pltpu.roll(top, half, 1)
-    lower = jnp.where((lane >= half) & (lane < sub + half), shifted, 0.0)
-    pivots = packed[half : half + 1]
+    lower = jnp.where((lane >= half) & (lane < sub + half), pltpu.roll(top, half, 1), 0.0)
     lower = jnp.where(lane == sub + half, pivots, lower)
     once = jnp.concatenate([upper, lower], axis=0)
     row = lax.broadcasted_iota(jnp.int32, (block, block), 0)
     col = lax.broadcasted_iota(jnp.int32, (block, block), 1)
-    gram_ref[...] = once + jnp.where(row == col, 0.0, once.T)
+    across = lax.rsqrt(pivots)
+    half_scaled = (once * across).T * across
+    gram_ref[...] = half_scaled + jnp.where(row == col, 0.0, half_scaled.T)
     done = eliminate([gram_ref[p : p + PANEL, :] for p in range(0, block, PANEL)], wide_ref, pair_ref)
     for p, panel in enumerate(done):
         factor_ref[p * PANEL : (p + 1) * PANEL, :] = panel
-    factor = factor_ref[...]
-    moment = packed[half + 1 : half + 2]
+    factor = factor_ref[...] * (across * rows_total**0.5)
+    moment = packed[half + 1 : half + 2] * (1.0 / rows_total)
     coefficients = jnp.sum(factor * moment, axis=1, keepdims=True)
     weights = jnp.sum(factor * coefficients, axis=0, keepdims=True)
     weights = split_rows(weights, 3)
@@ -356,11 +356,10 @@
     group, dom = sizes
     dom_bits = [1 << i for i in range(dom.bit_length() - 1)]
     group_bits = [dom << i for i in range(group.bit_length() - 1)]
-    bits = dom_bits[1:2] + group_bits + dom_bits[2:]
-    stages = [dom_bits[:1]]
-    while bits:
-        pair, bits = bits[:2], bits[2:]
-        stages.append([pair[-1], pair[0], sum(pair)] if len(pair) == 2 else pair)
+    bits = group_bits[:1] + dom_bits[1:2] + dom_bits[2:] + group_bits[1:]
+    stages = [dom_bits[:1], bits[:2] + [sum(bits[:2])], *([bit] for bit in bits[2:])]
+    if len(dom_bits) < 2 or not group_bits:
+        stages = [dom_bits[:1], *([bit] for bit in bits)]
     return stages[:1] + [[bit | 1 for bit in stage] for stage in stages[1:]]
 
 

time: 29.4 us -> 29.1 us (0.990)
    ppermute x7 -> x6, waiting for transfers between devices: 7.54 us -> 7.25 us  [sum_parts(): parts.append(lax.ppermute(total, AXES, pairs))]
    ppermute x7 -> x6, starting transfers between devices: 8.72 us -> 8.73 us  [sum_parts(): parts.append(lax.ppermute(total, AXES, pairs))]
  transfers between devices with their start and end apart: 9 -> 8, of which waited for: 7 -> 6; matrix products, arithmetic and copies ran while one was open for 0% -> 0% of each run, Pallas kernels for 8% -> 8%
where the time goes in v5:
time: 29.1 us; the launch traced here: 28.9 us
  starting transfers between devices  11.9 us (41%)
  Pallas kernels  8.63 us (30%)
  waiting for transfers between devices  7.78 us (27%)
  between operations  0.66 us (2%)
    ppermute x6, starting transfers between devices, sum_parts(): parts.append(lax.ppermute(total, AXES, pairs))  8.73 us
    ppermute x6, waiting for transfers between devices, sum_parts(): parts.append(lax.ppermute(total, AXES, pairs))  7.25 us
    pallas_call x1, Pallas kernels, finish(): pl.pallas_call(functools.partial(finish_kernel, rows_total=rows_total), o...  4.38 us
    ppermute x2, starting transfers between devices, halo(): got.append(lax.ppermute(sent, AXES, swap_pairs(parity, groups, devices)))  3.12 us
    pallas_call x1, Pallas kernels, body(): pl.pallas_call(local_kernel, out_shape=(pltpu.VMEM(prior_basis.shape, F32...  2.37 us
    pallas_call x1, Pallas kernels, body(): pl.pallas_call(shared_kernel, out_shape=(pltpu.VMEM(prior_basis.shape, F3...  0.96 us
    pallas_call x1, Pallas kernels, pack(): pl.pallas_call(pack_kernel, out_shape=pltpu.VMEM((rows + 16 * pl.cdiv(blo...  0.92 us
  transfers between devices with their start and end apart: 8, of which 6 were waited for; matrix products, arithmetic and copies ran while one was open for 0% of the time, Pallas kernels for 8%

profile of v5, /device:TPU:0, one launch (start us, length us, event | category | flops | bytes accessed | tf_op | source)
XLA Modules:
  0.0 28.9 jit_solution(15277209517704649875)
XLA Ops:
  0.6 0.9 %pack.1.packed_ref.refs_3_ = bf16[528,128]{1,0:T(8,128)(2,1)S(1)} custom-call(bf16[512,128]{1,0:T(8,128)(2,1)} %bitcast.1, bf16[4,128]{1,0:T(4,128)(2,1)} %state_ref.1), custom_call_target="tpu_custom_call" | custom-call | tf_op jit(solution)/shard_map/pack/pallas_call | solution.py:318
  1.6 3.0 %collective-permute-start.1 = (bf16[528,128]{1,0:T(8,128)(2,1)S(1)}, bf16[528,128]{1,0:T(8,128)(2,1)S(1)}, u32[]{:S(2)}, u32[]{:S(2)}) collective-permute-start(bf16[528,128]{1,0:T(8,128)(2,1)S(1)} %pack.1.packed_ref.refs_3_), channel_id=1, source_target_pairs={{0,16},{1,2},{2,1},{3,4},{4,3},{5,6},{6,5},{7,8},{8,7},{9,10},{10,... | collective-permute-start | bytes 405512 | tf_op jit(solution)/shard_map/ppermute | solution.py:351
  4.6 0.1 collective-permute-start
  4.7 2.4 %local_part.1 = (f32[4,128,128]{2,1,0:T(8,128)S(1)}, f32[4,128]{1,0:T(4,128)S(1)}, bf16[4,4,128,128]{3,2,1,0:T(8,128)(2,1)S(1)}, s32[4,4]{1,0:T(4,128)S(4)}, s32[4]{0:T(128)S(4)}) custom-call(s32[4,4]{1,0:T(4,128)} %index_ref.1, s32[4]{0:T(128)} %count_ref.1, bf16[528,128]{1,0:T(8,128)(2,1)S(1)} %pack.1.packed_ref.refs_3_, f32[4,128]{1,0:T(4,128)} %source_ref.1, ...), custom_call_target="tpu_custom_call" | custom-call | tf_op jit(solution)/shard_map/local_part/pallas_call | solution.py:403
  7.1 0.5 %collective-permute-done.1.outer_ref = bf16[528,128]{1,0:T(8,128)(2,1)S(1)} collective-permute-done((bf16[528,128]{1,0:T(8,128)(2,1)S(1)}, bf16[528,128]{1,0:T(8,128)(2,1)S(1)}, u32[]{:S(2)}, u32[]{:S(2)}) %collective-permute-start.1) | collective-permute-done | bytes 135200 | tf_op jit(solution)/shard_map/ppermute | solution.py:351
  7.6 0.0 collective-permute-done.inner_ref
  7.6 1.0 %shared_part.1 = (f32[4,128,128]{2,1,0:T(8,128)S(1)}, f32[4,128]{1,0:T(4,128)S(1)}, bf16[4,128,128]{2,1,0:T(8,128)(2,1)S(1)}, f32[72,128]{1,0:T(8,128)S(1)}) custom-call(s32[4,4]{1,0:T(4,128)S(4)} %get-tuple-element.12.index_ref, s32[4]{0:T(128)S(4)} %get-tuple-element.13.count_ref, ...), custom_call_target="tpu_custom_call", output_to_operand_aliasing={{0}: (5, {}), {1}: (6, {})} | custom-call | tf_op jit(solution)/shard_map/shared_part/pallas_call | solution.py:418
  8.5 0.6 %collective-permute-start.2 = (f32[72,128]{1,0:T(8,128)S(1)}, f32[72,128]{1,0:T(8,128)S(1)}, u32[]{:S(2)}, u32[]{:S(2)}) collective-permute-start(f32[72,128]{1,0:T(8,128)S(1)} %get-tuple-element.17), channel_id=1, source_target_pairs={{0,1},{1,0},{2,3},{3,2},{4,5},{5,4},{6,7},{7,6},{8,9},{9,8},{10,11... | collective-permute-start | bytes 110600 | tf_op jit(solution)/shard_map/ppermute | solution.py:377
  9.1 0.9 %collective-permute-done.2 = f32[72,128]{1,0:T(8,128)S(1)} collective-permute-done((f32[72,128]{1,0:T(8,128)S(1)}, f32[72,128]{1,0:T(8,128)S(1)}, u32[]{:S(2)}, u32[]{:S(2)}) %collective-permute-start.2) | collective-permute-done | bytes 36896 | tf_op jit(solution)/shard_map/ppermute | solution.py:377
  10.0 3.4 %collective-permute-start.5 = (f32[72,128]{1,0:T(8,128)S(1)}, f32[72,128]{1,0:T(8,128)S(1)}, u32[]{:S(2)}, u32[]{:S(2)}) collective-permute-start(f32[72,128]{1,0:T(8,128)S(1)} %add.15), channel_id=1, source_target_pairs={{0,19},{1,18},{2,17},{3,16},{4,23},{5,22},{6,21},{7,20},{8,27},{9,... | collective-permute-start | bytes 110600 | tf_op jit(solution)/shard_map/ppermute | solution.py:377
  13.4 0.0 collective-permute-start.4
  13.4 0.6 %collective-permute-start.3 = (f32[72,128]{1,0:T(8,128)S(1)}, f32[72,128]{1,0:T(8,128)S(1)}, u32[]{:S(2)}, u32[]{:S(2)}) collective-permute-start(f32[72,128]{1,0:T(8,128)S(1)} %add.15), channel_id=1, source_target_pairs={{0,17},{1,16},{2,19},{3,18},{4,21},{5,20},{6,23},{7,22},{8,25},{9,... | collective-permute-start | bytes 110600 | tf_op jit(solution)/shard_map/ppermute | solution.py:377
  14.0 1.3 %collective-permute-done.5 = f32[72,128]{1,0:T(8,128)S(1)} collective-permute-done((f32[72,128]{1,0:T(8,128)S(1)}, f32[72,128]{1,0:T(8,128)S(1)}, u32[]{:S(2)}, u32[]{:S(2)}) %collective-permute-start.5) | collective-permute-done | bytes 36896 | tf_op jit(solution)/shard_map/ppermute | solution.py:377
  15.3 1.5 %collective-permute-done.4 = f32[72,128]{1,0:T(8,128)S(1)} collective-permute-done((f32[72,128]{1,0:T(8,128)S(1)}, f32[72,128]{1,0:T(8,128)S(1)}, u32[]{:S(2)}, u32[]{:S(2)}) %collective-permute-start.4) | collective-permute-done | bytes 36896 | tf_op jit(solution)/shard_map/ppermute | solution.py:377
  16.8 0.0 collective-permute-done.3
  16.8 1.6 %collective-permute-start.6 = (f32[72,128]{1,0:T(8,128)S(1)}, f32[72,128]{1,0:T(8,128)S(1)}, u32[]{:S(2)}, u32[]{:S(2)}) collective-permute-start(f32[72,128]{1,0:T(8,128)S(1)} %add_add_fusion), channel_id=1, source_target_pairs={{0,5},{1,4},{2,7},{3,6},{4,1},{5,0},{6,3},{7,2},{8,13},{9,12},{10,... | collective-permute-start | bytes 110600 | tf_op jit(solution)/shard_map/ppermute | solution.py:377
  18.4 1.9 %collective-permute-done.6 = f32[72,128]{1,0:T(8,128)S(1)} collective-permute-done((f32[72,128]{1,0:T(8,128)S(1)}, f32[72,128]{1,0:T(8,128)S(1)}, u32[]{:S(2)}, u32[]{:S(2)}) %collective-permute-start.6) | collective-permute-done | bytes 36896 | tf_op jit(solution)/shard_map/ppermute | solution.py:377
  20.3 2.5 %collective-permute-start.7 = (f32[72,128]{1,0:T(8,128)S(1)}, f32[72,128]{1,0:T(8,128)S(1)}, u32[]{:S(2)}, u32[]{:S(2)}) collective-permute-start(f32[72,128]{1,0:T(8,128)S(1)} %add.19.refs_0_), channel_id=1, source_target_pairs={{0,9},{1,8},{2,11},{3,10},{4,13},{5,12},{6,15},{7,14},{8,1},{9,0},... | collective-permute-start | bytes 110600 | tf_op jit(solution)/shard_map/ppermute | solution.py:377
  22.8 1.7 %collective-permute-done.7.refs_1_ = f32[72,128]{1,0:T(8,128)S(1)} collective-permute-done((f32[72,128]{1,0:T(8,128)S(1)}, f32[72,128]{1,0:T(8,128)S(1)}, u32[]{:S(2)}, u32[]{:S(2)}) %collective-permute-start.7) | collective-permute-done | bytes 36896 | tf_op jit(solution)/shard_map/ppermute | solution.py:377
  24.6 4.4 %finish.1 = (bf16[4,128,128]{2,1,0:T(8,128)(2,1)}, bf16[4,128,128]{2,1,0:T(8,128)(2,1)}, f32[4,128]{1,0:T(4,128)}, f32[4,128]{1,0:T(4,128)}) custom-call(f32[72,128]{1,0:T(8,128)S(1)} %add.19.refs_0_, f32[72,128]{1,0:T(8,128)S(1)} %collective-permute-done.7.refs_1_, bf16[4,128,128]{2,1,0:T(8,128)(2,1)S(1)} %get-tuple-element.18.refs_2_, ...), custom_call_target="tpu_custom_call" | custom-call | tf_op jit(solution)/shard_map/finish/pallas_call | solution.py:383
  (3 shorter events, 0.0 us)
Async XLA Ops:
  1.6 6.0 %collective-permute-start.1 = (bf16[528,128]{1,0:T(8,128)(2,1)S(1)}, bf16[528,128]{1,0:T(8,128)(2,1)S(1)}, u32[]{:S(2)}, u32[]{:S(2)}) collective-permute-start(bf16[528,128]{1,0:T(8,128)(2,1)S(1)} %pack.1.packed_ref.refs_3_), channel_id=1, source_target_pairs={{0,16},{1,2},{2,1},{3,4},{4,3},{5,6},{6,5},{7,8},{8,7},{9,10},{10,... | collective-permute-start | bytes 405512 | tf_op jit(solution)/shard_map/ppermute | solution.py:351
  4.6 3.0 %collective-permute-start = (bf16[528,128]{1,0:T(8,128)(2,1)S(1)}, bf16[528,128]{1,0:T(8,128)(2,1)S(1)}, u32[]{:S(2)}, u32[]{:S(2)}) collective-permute-start(bf16[528,128]{1,0:T(8,128)(2,1)S(1)} %pack.1.packed_ref.refs_3_), channel_id=1, source_target_pairs={{0,1},{1,0},{2,3},{3,2},{4,5},{5,4},{6,7},{7,6},{8,9},{9,8},{10,11... | collective-permute-start | bytes 405512 | tf_op jit(solution)/shard_map/ppermute | solution.py:351
  8.5 1.4 %collective-permute-start.2 = (f32[72,128]{1,0:T(8,128)S(1)}, f32[72,128]{1,0:T(8,128)S(1)}, u32[]{:S(2)}, u32[]{:S(2)}) collective-permute-start(f32[72,128]{1,0:T(8,128)S(1)} %get-tuple-element.17), channel_id=1, source_target_pairs={{0,1},{1,0},{2,3},{3,2},{4,5},{5,4},{6,7},{7,6},{8,9},{9,8},{10,11... | collective-permute-start | bytes 110600 | tf_op jit(solution)/shard_map/ppermute | solution.py:377
  10.0 5.3 %collective-permute-start.5 = (f32[72,128]{1,0:T(8,128)S(1)}, f32[72,128]{1,0:T(8,128)S(1)}, u32[]{:S(2)}, u32[]{:S(2)}) collective-permute-start(f32[72,128]{1,0:T(8,128)S(1)} %add.15), channel_id=1, source_target_pairs={{0,19},{1,18},{2,17},{3,16},{4,23},{5,22},{6,21},{7,20},{8,27},{9,... | collective-permute-start | bytes 110600 | tf_op jit(solution)/shard_map/ppermute | solution.py:377
  13.4 3.4 %collective-permute-start.4 = (f32[72,128]{1,0:T(8,128)S(1)}, f32[72,128]{1,0:T(8,128)S(1)}, u32[]{:S(2)}, u32[]{:S(2)}) collective-permute-start(f32[72,128]{1,0:T(8,128)S(1)} %add.15), channel_id=1, source_target_pairs={{0,3},{1,2},{2,1},{3,0},{4,7},{5,6},{6,5},{7,4},{8,11},{9,10},{10,... | collective-permute-start | bytes 110600 | tf_op jit(solution)/shard_map/ppermute | solution.py:377
  13.4 3.4 %collective-permute-start.3 = (f32[72,128]{1,0:T(8,128)S(1)}, f32[72,128]{1,0:T(8,128)S(1)}, u32[]{:S(2)}, u32[]{:S(2)}) collective-permute-start(f32[72,128]{1,0:T(8,128)S(1)} %add.15), channel_id=1, source_target_pairs={{0,17},{1,16},{2,19},{3,18},{4,21},{5,20},{6,23},{7,22},{8,25},{9,... | collective-permute-start | bytes 110600 | tf_op jit(solution)/shard_map/ppermute | solution.py:377
  16.8 3.4 %collective-permute-start.6 = (f32[72,128]{1,0:T(8,128)S(1)}, f32[72,128]{1,0:T(8,128)S(1)}, u32[]{:S(2)}, u32[]{:S(2)}) collective-permute-start(f32[72,128]{1,0:T(8,128)S(1)} %add_add_fusion), channel_id=1, source_target_pairs={{0,5},{1,4},{2,7},{3,6},{4,1},{5,0},{6,3},{7,2},{8,13},{9,12},{10,... | collective-permute-start | bytes 110600 | tf_op jit(solution)/shard_map/ppermute | solution.py:377
  20.3 4.3 %collective-permute-start.7 = (f32[72,128]{1,0:T(8,128)S(1)}, f32[72,128]{1,0:T(8,128)S(1)}, u32[]{:S(2)}, u32[]{:S(2)}) collective-permute-start(f32[72,128]{1,0:T(8,128)S(1)} %add.19.refs_0_), channel_id=1, source_target_pairs={{0,9},{1,8},{2,11},{3,10},{4,13},{5,12},{6,15},{7,14},{8,1},{9,0},... | collective-permute-start | bytes 110600 | tf_op jit(solution)/shard_map/ppermute | solution.py:377

commit v6 on v5

--- a/solution.py
+++ b/solution.py
@@ -72,16 +72,26 @@
     near_coupling_ref,
     near_index_ref,
     near_count_ref,
+    facts_ref,
     sem,
 ):
     copy = pltpu.make_async_copy(coupling_ref, near_coupling_ref, sem)
     copy.start()
     blocks, block, _ = diag_ref.shape
     slots = coupling_ref.shape[1]
+    here = lax.axis_index("dom")
+    facts_ref[0] = here % 2
+    facts_ref[1] = (here == 0).astype(jnp.int32)
+    facts_ref[2] = (here == lax.axis_size("dom") - 1).astype(jnp.int32)
+    shared = jnp.int32(0)
     for b in range(blocks):
         near_count_ref[b] = count_ref[b]
         for s in range(slots):
             near_index_ref[b, s] = index_ref[b, s]
+        for s in range(2, slots):
+            outside = (index_ref[b, s] < HALO) | (index_ref[b, s] >= HALO + blocks)
+            shared += ((count_ref[b] > s) & outside).astype(jnp.int32)
+    facts_ref[3] = shared
     state = state_of(packed_ref, blocks * block, blocks)
     state_rows = [state[b : b + 1] for b in range(blocks)]
     copy.wait()
@@ -106,6 +116,7 @@
 def shared_kernel(
     index_ref,
     count_ref,
+    facts_ref,
     inner_ref,
     outer_ref,
     coupling_ref,
@@ -117,9 +128,7 @@
     sums_ref,
 ):
     blocks, block, _ = image_ref.shape
-    here = lax.axis_index("dom")
-    odd = here % 2 == 1
-    first, last = here == 0, here == lax.axis_size("dom") - 1
+    odd, first, last = (facts_ref[i] == 1 for i in range(3))
     inner_state = state_of(inner_ref, HALO * block, HALO)
     outer_state = state_of(outer_ref, HALO * block, HALO)
     lower_state = jnp.where(first, 0.0, jnp.where(odd, inner_state, outer_state))
@@ -140,22 +149,23 @@
             row = jnp.where(pick == i, rows[i : i + 1], row)
         return row
 
-    for b in range(blocks):
-        for s in range(2, coupling_ref.shape[1]):
-            pick = index_ref[b, s]
-            above = pick - HALO - blocks
-
-            @pl.when((count_ref[b] > s) & ((pick < HALO) | (above >= 0)))
-            def _(b=b, s=s, pick=pick, above=above):
-                at = jnp.where(above >= 0, above, pick)
-                picked = jnp.where(above >= 0, upper(at), lower(at))
-                row = jnp.where(above >= 0, chosen(upper_state, at), chosen(lower_state, at))
-                left = coupling_ref[b, s]
-                partial_ref[b] += dot(left, picked, NN)
-                rhs_ref[b : b + 1, :] -= section_step * dot(stack_rows([row]), left, NT)[:1]
-
-    gram = jnp.zeros((block, block), F32)
-    moment = jnp.zeros((16, block), F32)
+    @pl.when(facts_ref[3] > 0)
+    def _():
+        for b in range(blocks):
+            for s in range(2, coupling_ref.shape[1]):
+                pick = index_ref[b, s]
+                above = pick - HALO - blocks
+
+                @pl.when((count_ref[b] > s) & ((pick < HALO) | (above >= 0)))
+                def _(b=b, s=s, pick=pick, above=above):
+                    at = jnp.where(above >= 0, above, pick)
+                    picked = jnp.where(above >= 0, upper(at), lower(at))
+                    row = jnp.where(above >= 0, chosen(upper_state, at), chosen(lower_state, at))
+                    left = coupling_ref[b, s]
+                    partial_ref[b] += dot(left, picked, NN)
+                    rhs_ref[b : b + 1, :] -= section_step * dot(stack_rows([row]), left, NT)[:1]
+
+    images, rows_of = [], []
     for b in range(blocks):
         below, above = index_ref[b, 0], index_ref[b, 1] - HALO - blocks
         left = jnp.concatenate([coupling_ref[b, 0], coupling_ref[b, 1]], axis=1)
@@ -165,8 +175,11 @@
         rhs = rhs_ref[b : b + 1, :] - section_step * dot(rows, left, NT)[:1]
         image_ref[b] = image
         rhs_ref[b : b + 1, :] = rhs
-        gram = gram + dot(image, image, TN)
-        moment = moment + dot(split_rows(rhs, 3), image, NN)
+        images.append(image)
+        rows_of.append(split_rows(rhs, 3))
+    image = jnp.concatenate(images, axis=0)
+    gram = dot(image, image, TN)
+    moment = dot(jnp.concatenate(rows_of, axis=1), image, NN)
     half = block // 2
     top, bottom = gram[:half], gram[half:]
     sub = lax.broadcasted_iota(jnp.int32, (half, block), 0)
@@ -286,14 +299,18 @@
     high = factor.astype(BF16)
     low = (factor - high.astype(F32)).astype(BF16)
     both = jnp.concatenate([high, low], axis=1)
+    image = image_ref[...].reshape(blocks * block, block)
+    basis = packed_ref[: blocks * block]
+    new_image = dot(jnp.concatenate([image, image], axis=1), both, NT)
+    new_image_ref[...] = new_image.astype(BF16).reshape(new_image_ref.shape)
+    new_basis = dot(jnp.concatenate([basis, basis], axis=1), both, NT)
+    new_ref[...] = new_basis.astype(BF16).reshape(new_ref.shape)
+    guess = jnp.sum(dot(weights, basis, NT), axis=0, keepdims=True)
+    fitted = jnp.sum(dot(weights, image, NT), axis=0, keepdims=True)
     for b in range(blocks):
-        image, basis = image_ref[b], block_of(packed_ref, b, block)
-        new_image_ref[b] = dot(jnp.concatenate([image, image], axis=1), both, NT).astype(BF16)
-        new_ref[b] = dot(jnp.concatenate([basis, basis], axis=1), both, NT).astype(BF16)
-        guess = jnp.sum(dot(weights, basis, NT), axis=0, keepdims=True)
-        guess_ref[b : b + 1, :] = guess
-        fitted = jnp.sum(dot(weights, image, NT), axis=0, keepdims=True)
-        residual_ref[b : b + 1, :] = rhs_ref[b : b + 1, :] - fitted
+        part = slice(b * block, (b + 1) * block)
+        guess_ref[b : b + 1, :] = guess[:, part]
+        residual_ref[b : b + 1, :] = rhs_ref[b : b + 1, :] - fitted[:, part]
 
 
 def near(*arrays):
@@ -400,7 +417,7 @@
     blocks, block, columns = prior_basis.shape
     packed = pack(prior_basis, section_state)
     outer, inner = halo(packed, prior_basis, section_state)
-    partial, base, near_coupling, near_index, near_count = pl.pallas_call(
+    partial, base, near_coupling, *near_scalars = pl.pallas_call(
         local_kernel,
         out_shape=(
             pltpu.VMEM(prior_basis.shape, F32),
@@ -408,9 +425,10 @@
             pltpu.VMEM(coupling.shape, BF16),
             pltpu.SMEM(neighbour_index.shape, jnp.int32),
             pltpu.SMEM(slot_count.shape, jnp.int32),
+            pltpu.SMEM((4,), jnp.int32),
         ),
         in_specs=[smem()] * 2 + [vmem()] * 3 + [pl.BlockSpec(memory_space=pl.ANY)],
-        out_specs=(vmem(),) * 3 + (smem(),) * 2,
+        out_specs=(vmem(),) * 3 + (smem(),) * 3,
         scratch_shapes=[pltpu.SemaphoreType.DMA],
         compiler_params=pltpu.CompilerParams(vmem_limit_bytes=VMEM_LIMIT),
         name="local_part",
@@ -423,13 +441,13 @@
             pltpu.VMEM(prior_basis.shape, BF16),
             pltpu.VMEM((block // 2 + 8, columns), F32),
         ),
-        in_specs=[smem()] * 2 + [vmem()] * 5,
+        in_specs=[smem()] * 3 + [vmem()] * 5,
         out_specs=(vmem(),) * 4,
-        input_output_aliases={5: 0, 6: 1},
+        input_output_aliases={6: 0, 7: 1},
         compiler_params=pltpu.CompilerParams(vmem_limit_bytes=VMEM_LIMIT),
         name="shared_part",
     )(
-        *(pltpu.with_memory_space_constraint(array, pltpu.SMEM) for array in (near_index, near_count)),
+        *(pltpu.with_memory_space_constraint(array, pltpu.SMEM) for array in near_scalars),
         *near(inner, outer, near_coupling, partial, base),
     )
     parts = sum_parts(sums)

time: 29.1 us -> 28.7 us (0.986)
  Pallas kernels: 8.63 us -> 8.18 us
    pallas_call x1, Pallas kernels: 0.96 us -> 0.56 us  [body(): pl.pallas_call(shared_kernel, out_shape=(pltpu.VMEM(prior_basis.shape, F3...]
where the time goes in v6:
time: 28.7 us; the launch traced here: 28.5 us
  starting transfers between devices  11.9 us (41%)
  Pallas kernels  8.18 us (29%)
  waiting for transfers between devices  7.78 us (27%)
  between operations  0.66 us (2%)
    ppermute x6, starting transfers between devices, sum_parts(): parts.append(lax.ppermute(total, AXES, pairs))  8.73 us
    ppermute x6, waiting for transfers between devices, sum_parts(): parts.append(lax.ppermute(total, AXES, pairs))  7.25 us
    pallas_call x1, Pallas kernels, finish(): pl.pallas_call(functools.partial(finish_kernel, rows_total=rows_total), o...  4.33 us
    ppermute x2, starting transfers between devices, halo(): got.append(lax.ppermute(sent, AXES, swap_pairs(parity, groups, devices)))  3.12 us
    pallas_call x1, Pallas kernels, body(): pl.pallas_call(local_kernel, out_shape=(pltpu.VMEM(prior_basis.shape, F32...  2.37 us
    pallas_call x1, Pallas kernels, pack(): pl.pallas_call(pack_kernel, out_shape=pltpu.VMEM((rows + 16 * pl.cdiv(blo...  0.92 us
  transfers between devices with their start and end apart: 8, of which 6 were waited for; matrix products, arithmetic and copies ran while one was open for 0% of the time, Pallas kernels for 8%

profile of v6, /device:TPU:0, one launch (start us, length us, event | category | flops | bytes accessed | tf_op | source)
XLA Modules:
  0.0 28.5 jit_solution(18096094608889798177)
XLA Ops:
  0.6 0.9 %pack.1.packed_ref.refs_3_ = bf16[528,128]{1,0:T(8,128)(2,1)S(1)} custom-call(bf16[512,128]{1,0:T(8,128)(2,1)} %bitcast.1, bf16[4,128]{1,0:T(4,128)(2,1)} %state_ref.1), custom_call_target="tpu_custom_call" | custom-call | tf_op jit(solution)/shard_map/pack/pallas_call | solution.py:335
  1.6 3.0 %collective-permute-start.1 = (bf16[528,128]{1,0:T(8,128)(2,1)S(1)}, bf16[528,128]{1,0:T(8,128)(2,1)S(1)}, u32[]{:S(2)}, u32[]{:S(2)}) collective-permute-start(bf16[528,128]{1,0:T(8,128)(2,1)S(1)} %pack.1.packed_ref.refs_3_), channel_id=1, source_target_pairs={{0,16},{1,2},{2,1},{3,4},{4,3},{5,6},{6,5},{7,8},{8,7},{9,10},{10,... | collective-permute-start | bytes 405512 | tf_op jit(solution)/shard_map/ppermute | solution.py:368
  4.6 0.1 collective-permute-start
  4.7 2.4 %local_part.1 = (f32[4,128,128]{2,1,0:T(8,128)S(1)}, f32[4,128]{1,0:T(4,128)S(1)}, bf16[4,4,128,128]{3,2,1,0:T(8,128)(2,1)S(1)}, s32[4,4]{1,0:T(4,128)S(4)}, s32[4]{0:T(128)S(4)}, /*index=5*/s32[4]{0:T(128)S(4)}) custom-call(s32[4,4]{1,0:T(4,128)} %index_ref.1, s32[4]{0:T(128)} %count_ref.1, bf16[528,128]{1,0:T(8,128)(2,1)S(1)} %pack.1.packed_ref.refs_3_, ...), custom_call_target="tpu_custom_call" | custom-call | tf_op jit(solution)/shard_map/local_part/pallas_call | solution.py:420
  7.1 0.5 %collective-permute-done.1.outer_ref = bf16[528,128]{1,0:T(8,128)(2,1)S(1)} collective-permute-done((bf16[528,128]{1,0:T(8,128)(2,1)S(1)}, bf16[528,128]{1,0:T(8,128)(2,1)S(1)}, u32[]{:S(2)}, u32[]{:S(2)}) %collective-permute-start.1) | collective-permute-done | bytes 135200 | tf_op jit(solution)/shard_map/ppermute | solution.py:368
  7.6 0.0 collective-permute-done.inner_ref
  7.6 0.6 %shared_part.1 = (f32[4,128,128]{2,1,0:T(8,128)S(1)}, f32[4,128]{1,0:T(4,128)S(1)}, bf16[4,128,128]{2,1,0:T(8,128)(2,1)S(1)}, f32[72,128]{1,0:T(8,128)S(1)}) custom-call(s32[4,4]{1,0:T(4,128)S(4)} %get-tuple-element.13.index_ref, s32[4]{0:T(128)S(4)} %get-tuple-element.14.count_ref, ...), custom_call_target="tpu_custom_call", output_to_operand_aliasing={{0}: (6, {}), {1}: (7, {})} | custom-call | tf_op jit(solution)/shard_map/shared_part/pallas_call | solution.py:436
  8.2 0.6 %collective-permute-start.2 = (f32[72,128]{1,0:T(8,128)S(1)}, f32[72,128]{1,0:T(8,128)S(1)}, u32[]{:S(2)}, u32[]{:S(2)}) collective-permute-start(f32[72,128]{1,0:T(8,128)S(1)} %get-tuple-element.19), channel_id=1, source_target_pairs={{0,1},{1,0},{2,3},{3,2},{4,5},{5,4},{6,7},{7,6},{8,9},{9,8},{10,11... | collective-permute-start | bytes 110600 | tf_op jit(solution)/shard_map/ppermute | solution.py:394
  8.7 0.9 %collective-permute-done.2 = f32[72,128]{1,0:T(8,128)S(1)} collective-permute-done((f32[72,128]{1,0:T(8,128)S(1)}, f32[72,128]{1,0:T(8,128)S(1)}, u32[]{:S(2)}, u32[]{:S(2)}) %collective-permute-start.2) | collective-permute-done | bytes 36896 | tf_op jit(solution)/shard_map/ppermute | solution.py:394
  9.6 3.4 %collective-permute-start.5 = (f32[72,128]{1,0:T(8,128)S(1)}, f32[72,128]{1,0:T(8,128)S(1)}, u32[]{:S(2)}, u32[]{:S(2)}) collective-permute-start(f32[72,128]{1,0:T(8,128)S(1)} %add.15), channel_id=1, source_target_pairs={{0,19},{1,18},{2,17},{3,16},{4,23},{5,22},{6,21},{7,20},{8,27},{9,... | collective-permute-start | bytes 110600 | tf_op jit(solution)/shard_map/ppermute | solution.py:394
  13.0 0.0 collective-permute-start.4
  13.0 0.6 %collective-permute-start.3 = (f32[72,128]{1,0:T(8,128)S(1)}, f32[72,128]{1,0:T(8,128)S(1)}, u32[]{:S(2)}, u32[]{:S(2)}) collective-permute-start(f32[72,128]{1,0:T(8,128)S(1)} %add.15), channel_id=1, source_target_pairs={{0,17},{1,16},{2,19},{3,18},{4,21},{5,20},{6,23},{7,22},{8,25},{9,... | collective-permute-start | bytes 110600 | tf_op jit(solution)/shard_map/ppermute | solution.py:394
  13.6 1.3 %collective-permute-done.5 = f32[72,128]{1,0:T(8,128)S(1)} collective-permute-done((f32[72,128]{1,0:T(8,128)S(1)}, f32[72,128]{1,0:T(8,128)S(1)}, u32[]{:S(2)}, u32[]{:S(2)}) %collective-permute-start.5) | collective-permute-done | bytes 36896 | tf_op jit(solution)/shard_map/ppermute | solution.py:394
  14.9 1.5 %collective-permute-done.4 = f32[72,128]{1,0:T(8,128)S(1)} collective-permute-done((f32[72,128]{1,0:T(8,128)S(1)}, f32[72,128]{1,0:T(8,128)S(1)}, u32[]{:S(2)}, u32[]{:S(2)}) %collective-permute-start.4) | collective-permute-done | bytes 36896 | tf_op jit(solution)/shard_map/ppermute | solution.py:394
  16.4 0.0 collective-permute-done.3
  16.4 1.6 %collective-permute-start.6 = (f32[72,128]{1,0:T(8,128)S(1)}, f32[72,128]{1,0:T(8,128)S(1)}, u32[]{:S(2)}, u32[]{:S(2)}) collective-permute-start(f32[72,128]{1,0:T(8,128)S(1)} %add_add_fusion), channel_id=1, source_target_pairs={{0,5},{1,4},{2,7},{3,6},{4,1},{5,0},{6,3},{7,2},{8,13},{9,12},{10,... | collective-permute-start | bytes 110600 | tf_op jit(solution)/shard_map/ppermute | solution.py:394
  18.0 1.9 %collective-permute-done.6 = f32[72,128]{1,0:T(8,128)S(1)} collective-permute-done((f32[72,128]{1,0:T(8,128)S(1)}, f32[72,128]{1,0:T(8,128)S(1)}, u32[]{:S(2)}, u32[]{:S(2)}) %collective-permute-start.6) | collective-permute-done | bytes 36896 | tf_op jit(solution)/shard_map/ppermute | solution.py:394
  19.9 2.5 %collective-permute-start.7 = (f32[72,128]{1,0:T(8,128)S(1)}, f32[72,128]{1,0:T(8,128)S(1)}, u32[]{:S(2)}, u32[]{:S(2)}) collective-permute-start(f32[72,128]{1,0:T(8,128)S(1)} %add.19.refs_0_), channel_id=1, source_target_pairs={{0,9},{1,8},{2,11},{3,10},{4,13},{5,12},{6,15},{7,14},{8,1},{9,0},... | collective-permute-start | bytes 110600 | tf_op jit(solution)/shard_map/ppermute | solution.py:394
  22.4 1.7 %collective-permute-done.7.refs_1_ = f32[72,128]{1,0:T(8,128)S(1)} collective-permute-done((f32[72,128]{1,0:T(8,128)S(1)}, f32[72,128]{1,0:T(8,128)S(1)}, u32[]{:S(2)}, u32[]{:S(2)}) %collective-permute-start.7) | collective-permute-done | bytes 36896 | tf_op jit(solution)/shard_map/ppermute | solution.py:394
  24.2 4.3 %finish.1 = (bf16[4,128,128]{2,1,0:T(8,128)(2,1)}, bf16[4,128,128]{2,1,0:T(8,128)(2,1)}, f32[4,128]{1,0:T(4,128)}, f32[4,128]{1,0:T(4,128)}) custom-call(f32[72,128]{1,0:T(8,128)S(1)} %add.19.refs_0_, f32[72,128]{1,0:T(8,128)S(1)} %collective-permute-done.7.refs_1_, bf16[4,128,128]{2,1,0:T(8,128)(2,1)S(1)} %get-tuple-element.20.refs_2_, ...), custom_call_target="tpu_custom_call" | custom-call | tf_op jit(solution)/shard_map/finish/pallas_call | solution.py:400
  (3 shorter events, 0.0 us)
Async XLA Ops:
  1.6 6.0 %collective-permute-start.1 = (bf16[528,128]{1,0:T(8,128)(2,1)S(1)}, bf16[528,128]{1,0:T(8,128)(2,1)S(1)}, u32[]{:S(2)}, u32[]{:S(2)}) collective-permute-start(bf16[528,128]{1,0:T(8,128)(2,1)S(1)} %pack.1.packed_ref.refs_3_), channel_id=1, source_target_pairs={{0,16},{1,2},{2,1},{3,4},{4,3},{5,6},{6,5},{7,8},{8,7},{9,10},{10,... | collective-permute-start | bytes 405512 | tf_op jit(solution)/shard_map/ppermute | solution.py:368
  4.6 3.0 %collective-permute-start = (bf16[528,128]{1,0:T(8,128)(2,1)S(1)}, bf16[528,128]{1,0:T(8,128)(2,1)S(1)}, u32[]{:S(2)}, u32[]{:S(2)}) collective-permute-start(bf16[528,128]{1,0:T(8,128)(2,1)S(1)} %pack.1.packed_ref.refs_3_), channel_id=1, source_target_pairs={{0,1},{1,0},{2,3},{3,2},{4,5},{5,4},{6,7},{7,6},{8,9},{9,8},{10,11... | collective-permute-start | bytes 405512 | tf_op jit(solution)/shard_map/ppermute | solution.py:368
  8.2 1.4 %collective-permute-start.2 = (f32[72,128]{1,0:T(8,128)S(1)}, f32[72,128]{1,0:T(8,128)S(1)}, u32[]{:S(2)}, u32[]{:S(2)}) collective-permute-start(f32[72,128]{1,0:T(8,128)S(1)} %get-tuple-element.19), channel_id=1, source_target_pairs={{0,1},{1,0},{2,3},{3,2},{4,5},{5,4},{6,7},{7,6},{8,9},{9,8},{10,11... | collective-permute-start | bytes 110600 | tf_op jit(solution)/shard_map/ppermute | solution.py:394
  9.6 5.3 %collective-permute-start.5 = (f32[72,128]{1,0:T(8,128)S(1)}, f32[72,128]{1,0:T(8,128)S(1)}, u32[]{:S(2)}, u32[]{:S(2)}) collective-permute-start(f32[72,128]{1,0:T(8,128)S(1)} %add.15), channel_id=1, source_target_pairs={{0,19},{1,18},{2,17},{3,16},{4,23},{5,22},{6,21},{7,20},{8,27},{9,... | collective-permute-start | bytes 110600 | tf_op jit(solution)/shard_map/ppermute | solution.py:394
  13.0 3.4 %collective-permute-start.4 = (f32[72,128]{1,0:T(8,128)S(1)}, f32[72,128]{1,0:T(8,128)S(1)}, u32[]{:S(2)}, u32[]{:S(2)}) collective-permute-start(f32[72,128]{1,0:T(8,128)S(1)} %add.15), channel_id=1, source_target_pairs={{0,3},{1,2},{2,1},{3,0},{4,7},{5,6},{6,5},{7,4},{8,11},{9,10},{10,... | collective-permute-start | bytes 110600 | tf_op jit(solution)/shard_map/ppermute | solution.py:394
  13.0 3.4 %collective-permute-start.3 = (f32[72,128]{1,0:T(8,128)S(1)}, f32[72,128]{1,0:T(8,128)S(1)}, u32[]{:S(2)}, u32[]{:S(2)}) collective-permute-start(f32[72,128]{1,0:T(8,128)S(1)} %add.15), channel_id=1, source_target_pairs={{0,17},{1,16},{2,19},{3,18},{4,21},{5,20},{6,23},{7,22},{8,25},{9,... | collective-permute-start | bytes 110600 | tf_op jit(solution)/shard_map/ppermute | solution.py:394
  16.4 3.4 %collective-permute-start.6 = (f32[72,128]{1,0:T(8,128)S(1)}, f32[72,128]{1,0:T(8,128)S(1)}, u32[]{:S(2)}, u32[]{:S(2)}) collective-permute-start(f32[72,128]{1,0:T(8,128)S(1)} %add_add_fusion), channel_id=1, source_target_pairs={{0,5},{1,4},{2,7},{3,6},{4,1},{5,0},{6,3},{7,2},{8,13},{9,12},{10,... | collective-permute-start | bytes 110600 | tf_op jit(solution)/shard_map/ppermute | solution.py:394
  19.9 4.3 %collective-permute-start.7 = (f32[72,128]{1,0:T(8,128)S(1)}, f32[72,128]{1,0:T(8,128)S(1)}, u32[]{:S(2)}, u32[]{:S(2)}) collective-permute-start(f32[72,128]{1,0:T(8,128)S(1)} %add.19.refs_0_), channel_id=1, source_target_pairs={{0,9},{1,8},{2,11},{3,10},{4,13},{5,12},{6,15},{7,14},{8,1},{9,0},... | collective-permute-start | bytes 110600 | tf_op jit(solution)/shard_map/ppermute | solution.py:394

commit v7 on v6

--- a/solution.py
+++ b/solution.py
@@ -9,6 +9,7 @@
 
 HALO = 4
 PANEL = 8
+PACK_COPIES = 4
 VMEM_LIMIT = 16 << 20
 section_step = 0.25
 AXES = ("group", "dom")
@@ -41,15 +42,20 @@
 
 def pack_kernel(basis_ref, state_ref, packed_ref, rows_ref, sems):
     rows = basis_ref.shape[0]
-    copy = pltpu.make_async_copy(basis_ref, packed_ref.at[pl.ds(0, rows)], sems.at[0])
-    copy.start()
-    state_copy = pltpu.make_async_copy(state_ref, rows_ref, sems.at[1])
+    state_copy = pltpu.make_async_copy(state_ref, rows_ref, sems.at[0])
     state_copy.start()
+    share = rows // PACK_COPIES
+    copies = []
+    for part in range(PACK_COPIES):
+        at = pl.ds(part * share, share)
+        copies.append(pltpu.make_async_copy(basis_ref.at[at], packed_ref.at[at], sems.at[part + 1]))
+        copies[-1].start()
     state_copy.wait()
     state = rows_ref[...].astype(F32)
     spare = jnp.zeros((packed_ref.shape[0] - rows - state.shape[0], state.shape[1]), F32)
     packed_ref[rows:] = jnp.concatenate([state, spare], axis=0).astype(BF16)
-    copy.wait()
+    for copy in copies:
+        copy.wait()
 
 
 def state_of(packed_ref, rows, count):
@@ -337,7 +343,7 @@
         out_shape=pltpu.VMEM((rows + 16 * pl.cdiv(blocks, 16), columns), BF16),
         in_specs=[pl.BlockSpec(memory_space=pl.ANY)] * 2,
         out_specs=vmem(),
-        scratch_shapes=[pltpu.VMEM(state.shape, BF16), pltpu.SemaphoreType.DMA((2,))],
+        scratch_shapes=[pltpu.VMEM(state.shape, BF16), pltpu.SemaphoreType.DMA((PACK_COPIES + 1,))],
         compiler_params=pltpu.CompilerParams(vmem_limit_bytes=VMEM_LIMIT),
         name="pack",
     )(*far(basis.reshape(rows, columns), state))

time: 28.7 us -> 28.7 us (level)
  no operation moved by 1% of the time
where the time goes in v7:
time: 28.7 us; the launch traced here: 28.4 us
  starting transfers between devices  11.9 us (41%)
  Pallas kernels  8.12 us (28%)
  waiting for transfers between devices  7.78 us (27%)
  between operations  0.66 us (2%)
    ppermute x6, starting transfers between devices, sum_parts(): parts.append(lax.ppermute(total, AXES, pairs))  8.73 us
    ppermute x6, waiting for transfers between devices, sum_parts(): parts.append(lax.ppermute(total, AXES, pairs))  7.25 us
    pallas_call x1, Pallas kernels, finish(): pl.pallas_call(functools.partial(finish_kernel, rows_total=rows_total), o...  4.33 us
    ppermute x2, starting transfers between devices, halo(): got.append(lax.ppermute(sent, AXES, swap_pairs(parity, groups, devices)))  3.12 us
    pallas_call x1, Pallas kernels, body(): pl.pallas_call(local_kernel, out_shape=(pltpu.VMEM(prior_basis.shape, F32...  2.37 us
    pallas_call x1, Pallas kernels, pack(): pl.pallas_call(pack_kernel, out_shape=pltpu.VMEM((rows + 16 * pl.cdiv(blo...  0.87 us
  transfers between devices with their start and end apart: 8, of which 6 were waited for; matrix products, arithmetic and copies ran while one was open for 0% of the time, Pallas kernels for 8%

profile of v7, /device:TPU:0, one launch (start us, length us, event | category | flops | bytes accessed | tf_op | source)
XLA Modules:
  0.0 28.4 jit_solution(15800242011273801820)
XLA Ops:
  0.6 0.9 %pack.1.packed_ref.refs_3_ = bf16[528,128]{1,0:T(8,128)(2,1)S(1)} custom-call(bf16[512,128]{1,0:T(8,128)(2,1)} %bitcast.1, bf16[4,128]{1,0:T(4,128)(2,1)} %state_ref.1), custom_call_target="tpu_custom_call" | custom-call | tf_op jit(solution)/shard_map/pack/pallas_call | solution.py:341
  1.5 3.0 %collective-permute-start.1 = (bf16[528,128]{1,0:T(8,128)(2,1)S(1)}, bf16[528,128]{1,0:T(8,128)(2,1)S(1)}, u32[]{:S(2)}, u32[]{:S(2)}) collective-permute-start(bf16[528,128]{1,0:T(8,128)(2,1)S(1)} %pack.1.packed_ref.refs_3_), channel_id=1, source_target_pairs={{0,16},{1,2},{2,1},{3,4},{4,3},{5,6},{6,5},{7,8},{8,7},{9,10},{10,... | collective-permute-start | bytes 405512 | tf_op jit(solution)/shard_map/ppermute | solution.py:374
  4.5 0.1 collective-permute-start
  4.6 2.4 %local_part.1 = (f32[4,128,128]{2,1,0:T(8,128)S(1)}, f32[4,128]{1,0:T(4,128)S(1)}, bf16[4,4,128,128]{3,2,1,0:T(8,128)(2,1)S(1)}, s32[4,4]{1,0:T(4,128)S(4)}, s32[4]{0:T(128)S(4)}, /*index=5*/s32[4]{0:T(128)S(4)}) custom-call(s32[4,4]{1,0:T(4,128)} %index_ref.1, s32[4]{0:T(128)} %count_ref.1, bf16[528,128]{1,0:T(8,128)(2,1)S(1)} %pack.1.packed_ref.refs_3_, ...), custom_call_target="tpu_custom_call" | custom-call | tf_op jit(solution)/shard_map/local_part/pallas_call | solution.py:426
  7.0 0.5 %collective-permute-done.1.outer_ref = bf16[528,128]{1,0:T(8,128)(2,1)S(1)} collective-permute-done((bf16[528,128]{1,0:T(8,128)(2,1)S(1)}, bf16[528,128]{1,0:T(8,128)(2,1)S(1)}, u32[]{:S(2)}, u32[]{:S(2)}) %collective-permute-start.1) | collective-permute-done | bytes 135200 | tf_op jit(solution)/shard_map/ppermute | solution.py:374
  7.5 0.0 collective-permute-done.inner_ref
  7.5 0.6 %shared_part.1 = (f32[4,128,128]{2,1,0:T(8,128)S(1)}, f32[4,128]{1,0:T(4,128)S(1)}, bf16[4,128,128]{2,1,0:T(8,128)(2,1)S(1)}, f32[72,128]{1,0:T(8,128)S(1)}) custom-call(s32[4,4]{1,0:T(4,128)S(4)} %get-tuple-element.13.index_ref, s32[4]{0:T(128)S(4)} %get-tuple-element.14.count_ref, ...), custom_call_target="tpu_custom_call", output_to_operand_aliasing={{0}: (6, {}), {1}: (7, {})} | custom-call | tf_op jit(solution)/shard_map/shared_part/pallas_call | solution.py:442
  8.1 0.6 %collective-permute-start.2 = (f32[72,128]{1,0:T(8,128)S(1)}, f32[72,128]{1,0:T(8,128)S(1)}, u32[]{:S(2)}, u32[]{:S(2)}) collective-permute-start(f32[72,128]{1,0:T(8,128)S(1)} %get-tuple-element.19), channel_id=1, source_target_pairs={{0,1},{1,0},{2,3},{3,2},{4,5},{5,4},{6,7},{7,6},{8,9},{9,8},{10,11... | collective-permute-start | bytes 110600 | tf_op jit(solution)/shard_map/ppermute | solution.py:400
  8.7 0.9 %collective-permute-done.2 = f32[72,128]{1,0:T(8,128)S(1)} collective-permute-done((f32[72,128]{1,0:T(8,128)S(1)}, f32[72,128]{1,0:T(8,128)S(1)}, u32[]{:S(2)}, u32[]{:S(2)}) %collective-permute-start.2) | collective-permute-done | bytes 36896 | tf_op jit(solution)/shard_map/ppermute | solution.py:400
  9.5 3.4 %collective-permute-start.5 = (f32[72,128]{1,0:T(8,128)S(1)}, f32[72,128]{1,0:T(8,128)S(1)}, u32[]{:S(2)}, u32[]{:S(2)}) collective-permute-start(f32[72,128]{1,0:T(8,128)S(1)} %add.15), channel_id=1, source_target_pairs={{0,19},{1,18},{2,17},{3,16},{4,23},{5,22},{6,21},{7,20},{8,27},{9,... | collective-permute-start | bytes 110600 | tf_op jit(solution)/shard_map/ppermute | solution.py:400
  13.0 0.0 collective-permute-start.4
  13.0 0.6 %collective-permute-start.3 = (f32[72,128]{1,0:T(8,128)S(1)}, f32[72,128]{1,0:T(8,128)S(1)}, u32[]{:S(2)}, u32[]{:S(2)}) collective-permute-start(f32[72,128]{1,0:T(8,128)S(1)} %add.15), channel_id=1, source_target_pairs={{0,17},{1,16},{2,19},{3,18},{4,21},{5,20},{6,23},{7,22},{8,25},{9,... | collective-permute-start | bytes 110600 | tf_op jit(solution)/shard_map/ppermute | solution.py:400
  13.6 1.3 %collective-permute-done.5 = f32[72,128]{1,0:T(8,128)S(1)} collective-permute-done((f32[72,128]{1,0:T(8,128)S(1)}, f32[72,128]{1,0:T(8,128)S(1)}, u32[]{:S(2)}, u32[]{:S(2)}) %collective-permute-start.5) | collective-permute-done | bytes 36896 | tf_op jit(solution)/shard_map/ppermute | solution.py:400
  14.8 1.5 %collective-permute-done.4 = f32[72,128]{1,0:T(8,128)S(1)} collective-permute-done((f32[72,128]{1,0:T(8,128)S(1)}, f32[72,128]{1,0:T(8,128)S(1)}, u32[]{:S(2)}, u32[]{:S(2)}) %collective-permute-start.4) | collective-permute-done | bytes 36896 | tf_op jit(solution)/shard_map/ppermute | solution.py:400
  16.4 0.0 collective-permute-done.3
  16.4 1.6 %collective-permute-start.6 = (f32[72,128]{1,0:T(8,128)S(1)}, f32[72,128]{1,0:T(8,128)S(1)}, u32[]{:S(2)}, u32[]{:S(2)}) collective-permute-start(f32[72,128]{1,0:T(8,128)S(1)} %add_add_fusion), channel_id=1, source_target_pairs={{0,5},{1,4},{2,7},{3,6},{4,1},{5,0},{6,3},{7,2},{8,13},{9,12},{10,... | collective-permute-start | bytes 110600 | tf_op jit(solution)/shard_map/ppermute | solution.py:400
  18.0 1.9 %collective-permute-done.6 = f32[72,128]{1,0:T(8,128)S(1)} collective-permute-done((f32[72,128]{1,0:T(8,128)S(1)}, f32[72,128]{1,0:T(8,128)S(1)}, u32[]{:S(2)}, u32[]{:S(2)}) %collective-permute-start.6) | collective-permute-done | bytes 36896 | tf_op jit(solution)/shard_map/ppermute | solution.py:400
  19.8 2.5 %collective-permute-start.7 = (f32[72,128]{1,0:T(8,128)S(1)}, f32[72,128]{1,0:T(8,128)S(1)}, u32[]{:S(2)}, u32[]{:S(2)}) collective-permute-start(f32[72,128]{1,0:T(8,128)S(1)} %add.19.refs_0_), channel_id=1, source_target_pairs={{0,9},{1,8},{2,11},{3,10},{4,13},{5,12},{6,15},{7,14},{8,1},{9,0},... | collective-permute-start | bytes 110600 | tf_op jit(solution)/shard_map/ppermute | solution.py:400
  22.4 1.7 %collective-permute-done.7.refs_1_ = f32[72,128]{1,0:T(8,128)S(1)} collective-permute-done((f32[72,128]{1,0:T(8,128)S(1)}, f32[72,128]{1,0:T(8,128)S(1)}, u32[]{:S(2)}, u32[]{:S(2)}) %collective-permute-start.7) | collective-permute-done | bytes 36896 | tf_op jit(solution)/shard_map/ppermute | solution.py:400
  24.1 4.3 %finish.1 = (bf16[4,128,128]{2,1,0:T(8,128)(2,1)}, bf16[4,128,128]{2,1,0:T(8,128)(2,1)}, f32[4,128]{1,0:T(4,128)}, f32[4,128]{1,0:T(4,128)}) custom-call(f32[72,128]{1,0:T(8,128)S(1)} %add.19.refs_0_, f32[72,128]{1,0:T(8,128)S(1)} %collective-permute-done.7.refs_1_, bf16[4,128,128]{2,1,0:T(8,128)(2,1)S(1)} %get-tuple-element.20.refs_2_, ...), custom_call_target="tpu_custom_call" | custom-call | tf_op jit(solution)/shard_map/finish/pallas_call | solution.py:406
  (3 shorter events, 0.0 us)
Async XLA Ops:
  1.5 6.0 %collective-permute-start.1 = (bf16[528,128]{1,0:T(8,128)(2,1)S(1)}, bf16[528,128]{1,0:T(8,128)(2,1)S(1)}, u32[]{:S(2)}, u32[]{:S(2)}) collective-permute-start(bf16[528,128]{1,0:T(8,128)(2,1)S(1)} %pack.1.packed_ref.refs_3_), channel_id=1, source_target_pairs={{0,16},{1,2},{2,1},{3,4},{4,3},{5,6},{6,5},{7,8},{8,7},{9,10},{10,... | collective-permute-start | bytes 405512 | tf_op jit(solution)/shard_map/ppermute | solution.py:374
  4.5 3.0 %collective-permute-start = (bf16[528,128]{1,0:T(8,128)(2,1)S(1)}, bf16[528,128]{1,0:T(8,128)(2,1)S(1)}, u32[]{:S(2)}, u32[]{:S(2)}) collective-permute-start(bf16[528,128]{1,0:T(8,128)(2,1)S(1)} %pack.1.packed_ref.refs_3_), channel_id=1, source_target_pairs={{0,1},{1,0},{2,3},{3,2},{4,5},{5,4},{6,7},{7,6},{8,9},{9,8},{10,11... | collective-permute-start | bytes 405512 | tf_op jit(solution)/shard_map/ppermute | solution.py:374
  8.1 1.4 %collective-permute-start.2 = (f32[72,128]{1,0:T(8,128)S(1)}, f32[72,128]{1,0:T(8,128)S(1)}, u32[]{:S(2)}, u32[]{:S(2)}) collective-permute-start(f32[72,128]{1,0:T(8,128)S(1)} %get-tuple-element.19), channel_id=1, source_target_pairs={{0,1},{1,0},{2,3},{3,2},{4,5},{5,4},{6,7},{7,6},{8,9},{9,8},{10,11... | collective-permute-start | bytes 110600 | tf_op jit(solution)/shard_map/ppermute | solution.py:400
  9.5 5.3 %collective-permute-start.5 = (f32[72,128]{1,0:T(8,128)S(1)}, f32[72,128]{1,0:T(8,128)S(1)}, u32[]{:S(2)}, u32[]{:S(2)}) collective-permute-start(f32[72,128]{1,0:T(8,128)S(1)} %add.15), channel_id=1, source_target_pairs={{0,19},{1,18},{2,17},{3,16},{4,23},{5,22},{6,21},{7,20},{8,27},{9,... | collective-permute-start | bytes 110600 | tf_op jit(solution)/shard_map/ppermute | solution.py:400
  13.0 3.4 %collective-permute-start.4 = (f32[72,128]{1,0:T(8,128)S(1)}, f32[72,128]{1,0:T(8,128)S(1)}, u32[]{:S(2)}, u32[]{:S(2)}) collective-permute-start(f32[72,128]{1,0:T(8,128)S(1)} %add.15), channel_id=1, source_target_pairs={{0,3},{1,2},{2,1},{3,0},{4,7},{5,6},{6,5},{7,4},{8,11},{9,10},{10,... | collective-permute-start | bytes 110600 | tf_op jit(solution)/shard_map/ppermute | solution.py:400
  13.0 3.4 %collective-permute-start.3 = (f32[72,128]{1,0:T(8,128)S(1)}, f32[72,128]{1,0:T(8,128)S(1)}, u32[]{:S(2)}, u32[]{:S(2)}) collective-permute-start(f32[72,128]{1,0:T(8,128)S(1)} %add.15), channel_id=1, source_target_pairs={{0,17},{1,16},{2,19},{3,18},{4,21},{5,20},{6,23},{7,22},{8,25},{9,... | collective-permute-start | bytes 110600 | tf_op jit(solution)/shard_map/ppermute | solution.py:400
  16.4 3.4 %collective-permute-start.6 = (f32[72,128]{1,0:T(8,128)S(1)}, f32[72,128]{1,0:T(8,128)S(1)}, u32[]{:S(2)}, u32[]{:S(2)}) collective-permute-start(f32[72,128]{1,0:T(8,128)S(1)} %add_add_fusion), channel_id=1, source_target_pairs={{0,5},{1,4},{2,7},{3,6},{4,1},{5,0},{6,3},{7,2},{8,13},{9,12},{10,... | collective-permute-start | bytes 110600 | tf_op jit(solution)/shard_map/ppermute | solution.py:400
  19.8 4.3 %collective-permute-start.7 = (f32[72,128]{1,0:T(8,128)S(1)}, f32[72,128]{1,0:T(8,128)S(1)}, u32[]{:S(2)}, u32[]{:S(2)}) collective-permute-start(f32[72,128]{1,0:T(8,128)S(1)} %add.19.refs_0_), channel_id=1, source_target_pairs={{0,9},{1,8},{2,11},{3,10},{4,13},{5,12},{6,15},{7,14},{8,1},{9,0},... | collective-permute-start | bytes 110600 | tf_op jit(solution)/shard_map/ppermute | solution.py:400

commit v8 on v7

--- a/solution.py
+++ b/solution.py
@@ -42,14 +42,14 @@
 
 def pack_kernel(basis_ref, state_ref, packed_ref, rows_ref, sems):
     rows = basis_ref.shape[0]
-    state_copy = pltpu.make_async_copy(state_ref, rows_ref, sems.at[0])
-    state_copy.start()
     share = rows // PACK_COPIES
     copies = []
     for part in range(PACK_COPIES):
         at = pl.ds(part * share, share)
         copies.append(pltpu.make_async_copy(basis_ref.at[at], packed_ref.at[at], sems.at[part + 1]))
         copies[-1].start()
+    state_copy = pltpu.make_async_copy(state_ref, rows_ref, sems.at[0])
+    state_copy.start()
     state_copy.wait()
     state = rows_ref[...].astype(F32)
     spare = jnp.zeros((packed_ref.shape[0] - rows - state.shape[0], state.shape[1]), F32)

time: 28.7 us -> 28.7 us (level)
  no operation moved by 1% of the time
where the time goes in v8:
time: 28.7 us; the launch traced here: 28.4 us
  starting transfers between devices  11.9 us (41%)
  Pallas kernels  8.1 us (28%)
  waiting for transfers between devices  7.78 us (27%)
  between operations  0.66 us (2%)
    ppermute x6, starting transfers between devices, sum_parts(): parts.append(lax.ppermute(total, AXES, pairs))  8.74 us
    ppermute x6, waiting for transfers between devices, sum_parts(): parts.append(lax.ppermute(total, AXES, pairs))  7.25 us
    pallas_call x1, Pallas kernels, finish(): pl.pallas_call(functools.partial(finish_kernel, rows_total=rows_total), o...  4.32 us
    ppermute x2, starting transfers between devices, halo(): got.append(lax.ppermute(sent, AXES, swap_pairs(parity, groups, devices)))  3.12 us
    pallas_call x1, Pallas kernels, body(): pl.pallas_call(local_kernel, out_shape=(pltpu.VMEM(prior_basis.shape, F32...  2.36 us
    pallas_call x1, Pallas kernels, pack(): pl.pallas_call(pack_kernel, out_shape=pltpu.VMEM((rows + 16 * pl.cdiv(blo...  0.85 us
  transfers between devices with their start and end apart: 8, of which 6 were waited for; matrix products, arithmetic and copies ran while one was open for 0% of the time, Pallas kernels for 8%

profile of v8, /device:TPU:0, one launch (start us, length us, event | category | flops | bytes accessed | tf_op | source)
XLA Modules:
  0.0 28.4 jit_solution(14256080732741720148)
XLA Ops:
  0.6 0.9 %pack.1.packed_ref.refs_3_ = bf16[528,128]{1,0:T(8,128)(2,1)S(1)} custom-call(bf16[512,128]{1,0:T(8,128)(2,1)} %bitcast.1, bf16[4,128]{1,0:T(4,128)(2,1)} %state_ref.1), custom_call_target="tpu_custom_call" | custom-call | tf_op jit(solution)/shard_map/pack/pallas_call | solution.py:341
  1.5 3.0 %collective-permute-start.1 = (bf16[528,128]{1,0:T(8,128)(2,1)S(1)}, bf16[528,128]{1,0:T(8,128)(2,1)S(1)}, u32[]{:S(2)}, u32[]{:S(2)}) collective-permute-start(bf16[528,128]{1,0:T(8,128)(2,1)S(1)} %pack.1.packed_ref.refs_3_), channel_id=1, source_target_pairs={{0,16},{1,2},{2,1},{3,4},{4,3},{5,6},{6,5},{7,8},{8,7},{9,10},{10,... | collective-permute-start | bytes 405512 | tf_op jit(solution)/shard_map/ppermute | solution.py:374
  4.5 0.1 collective-permute-start
  4.6 2.4 %local_part.1 = (f32[4,128,128]{2,1,0:T(8,128)S(1)}, f32[4,128]{1,0:T(4,128)S(1)}, bf16[4,4,128,128]{3,2,1,0:T(8,128)(2,1)S(1)}, s32[4,4]{1,0:T(4,128)S(4)}, s32[4]{0:T(128)S(4)}, /*index=5*/s32[4]{0:T(128)S(4)}) custom-call(s32[4,4]{1,0:T(4,128)} %index_ref.1, s32[4]{0:T(128)} %count_ref.1, bf16[528,128]{1,0:T(8,128)(2,1)S(1)} %pack.1.packed_ref.refs_3_, ...), custom_call_target="tpu_custom_call" | custom-call | tf_op jit(solution)/shard_map/local_part/pallas_call | solution.py:426
  7.0 0.5 %collective-permute-done.1.outer_ref = bf16[528,128]{1,0:T(8,128)(2,1)S(1)} collective-permute-done((bf16[528,128]{1,0:T(8,128)(2,1)S(1)}, bf16[528,128]{1,0:T(8,128)(2,1)S(1)}, u32[]{:S(2)}, u32[]{:S(2)}) %collective-permute-start.1) | collective-permute-done | bytes 135200 | tf_op jit(solution)/shard_map/ppermute | solution.py:374
  7.5 0.0 collective-permute-done.inner_ref
  7.5 0.6 %shared_part.1 = (f32[4,128,128]{2,1,0:T(8,128)S(1)}, f32[4,128]{1,0:T(4,128)S(1)}, bf16[4,128,128]{2,1,0:T(8,128)(2,1)S(1)}, f32[72,128]{1,0:T(8,128)S(1)}) custom-call(s32[4,4]{1,0:T(4,128)S(4)} %get-tuple-element.13.index_ref, s32[4]{0:T(128)S(4)} %get-tuple-element.14.count_ref, ...), custom_call_target="tpu_custom_call", output_to_operand_aliasing={{0}: (6, {}), {1}: (7, {})} | custom-call | tf_op jit(solution)/shard_map/shared_part/pallas_call | solution.py:442
  8.1 0.6 %collective-permute-start.2 = (f32[72,128]{1,0:T(8,128)S(1)}, f32[72,128]{1,0:T(8,128)S(1)}, u32[]{:S(2)}, u32[]{:S(2)}) collective-permute-start(f32[72,128]{1,0:T(8,128)S(1)} %get-tuple-element.19), channel_id=1, source_target_pairs={{0,1},{1,0},{2,3},{3,2},{4,5},{5,4},{6,7},{7,6},{8,9},{9,8},{10,11... | collective-permute-start | bytes 110600 | tf_op jit(solution)/shard_map/ppermute | solution.py:400
  8.6 0.9 %collective-permute-done.2 = f32[72,128]{1,0:T(8,128)S(1)} collective-permute-done((f32[72,128]{1,0:T(8,128)S(1)}, f32[72,128]{1,0:T(8,128)S(1)}, u32[]{:S(2)}, u32[]{:S(2)}) %collective-permute-start.2) | collective-permute-done | bytes 36896 | tf_op jit(solution)/shard_map/ppermute | solution.py:400
  9.5 3.4 %collective-permute-start.5 = (f32[72,128]{1,0:T(8,128)S(1)}, f32[72,128]{1,0:T(8,128)S(1)}, u32[]{:S(2)}, u32[]{:S(2)}) collective-permute-start(f32[72,128]{1,0:T(8,128)S(1)} %add.15), channel_id=1, source_target_pairs={{0,19},{1,18},{2,17},{3,16},{4,23},{5,22},{6,21},{7,20},{8,27},{9,... | collective-permute-start | bytes 110600 | tf_op jit(solution)/shard_map/ppermute | solution.py:400
  13.0 0.0 collective-permute-start.4
  13.0 0.6 %collective-permute-start.3 = (f32[72,128]{1,0:T(8,128)S(1)}, f32[72,128]{1,0:T(8,128)S(1)}, u32[]{:S(2)}, u32[]{:S(2)}) collective-permute-start(f32[72,128]{1,0:T(8,128)S(1)} %add.15), channel_id=1, source_target_pairs={{0,17},{1,16},{2,19},{3,18},{4,21},{5,20},{6,23},{7,22},{8,25},{9,... | collective-permute-start | bytes 110600 | tf_op jit(solution)/shard_map/ppermute | solution.py:400
  13.5 1.3 %collective-permute-done.5 = f32[72,128]{1,0:T(8,128)S(1)} collective-permute-done((f32[72,128]{1,0:T(8,128)S(1)}, f32[72,128]{1,0:T(8,128)S(1)}, u32[]{:S(2)}, u32[]{:S(2)}) %collective-permute-start.5) | collective-permute-done | bytes 36896 | tf_op jit(solution)/shard_map/ppermute | solution.py:400
  14.8 1.5 %collective-permute-done.4 = f32[72,128]{1,0:T(8,128)S(1)} collective-permute-done((f32[72,128]{1,0:T(8,128)S(1)}, f32[72,128]{1,0:T(8,128)S(1)}, u32[]{:S(2)}, u32[]{:S(2)}) %collective-permute-start.4) | collective-permute-done | bytes 36896 | tf_op jit(solution)/shard_map/ppermute | solution.py:400
  16.3 0.0 collective-permute-done.3
  16.4 1.6 %collective-permute-start.6 = (f32[72,128]{1,0:T(8,128)S(1)}, f32[72,128]{1,0:T(8,128)S(1)}, u32[]{:S(2)}, u32[]{:S(2)}) collective-permute-start(f32[72,128]{1,0:T(8,128)S(1)} %add_add_fusion), channel_id=1, source_target_pairs={{0,5},{1,4},{2,7},{3,6},{4,1},{5,0},{6,3},{7,2},{8,13},{9,12},{10,... | collective-permute-start | bytes 110600 | tf_op jit(solution)/shard_map/ppermute | solution.py:400
  18.0 1.9 %collective-permute-done.6 = f32[72,128]{1,0:T(8,128)S(1)} collective-permute-done((f32[72,128]{1,0:T(8,128)S(1)}, f32[72,128]{1,0:T(8,128)S(1)}, u32[]{:S(2)}, u32[]{:S(2)}) %collective-permute-start.6) | collective-permute-done | bytes 36896 | tf_op jit(solution)/shard_map/ppermute | solution.py:400
  19.8 2.5 %collective-permute-start.7 = (f32[72,128]{1,0:T(8,128)S(1)}, f32[72,128]{1,0:T(8,128)S(1)}, u32[]{:S(2)}, u32[]{:S(2)}) collective-permute-start(f32[72,128]{1,0:T(8,128)S(1)} %add.19.refs_0_), channel_id=1, source_target_pairs={{0,9},{1,8},{2,11},{3,10},{4,13},{5,12},{6,15},{7,14},{8,1},{9,0},... | collective-permute-start | bytes 110600 | tf_op jit(solution)/shard_map/ppermute | solution.py:400
  22.4 1.7 %collective-permute-done.7.refs_1_ = f32[72,128]{1,0:T(8,128)S(1)} collective-permute-done((f32[72,128]{1,0:T(8,128)S(1)}, f32[72,128]{1,0:T(8,128)S(1)}, u32[]{:S(2)}, u32[]{:S(2)}) %collective-permute-start.7) | collective-permute-done | bytes 36896 | tf_op jit(solution)/shard_map/ppermute | solution.py:400
  24.1 4.3 %finish.1 = (bf16[4,128,128]{2,1,0:T(8,128)(2,1)}, bf16[4,128,128]{2,1,0:T(8,128)(2,1)}, f32[4,128]{1,0:T(4,128)}, f32[4,128]{1,0:T(4,128)}) custom-call(f32[72,128]{1,0:T(8,128)S(1)} %add.19.refs_0_, f32[72,128]{1,0:T(8,128)S(1)} %collective-permute-done.7.refs_1_, bf16[4,128,128]{2,1,0:T(8,128)(2,1)S(1)} %get-tuple-element.20.refs_2_, ...), custom_call_target="tpu_custom_call" | custom-call | tf_op jit(solution)/shard_map/finish/pallas_call | solution.py:406
  (3 shorter events, 0.0 us)
Async XLA Ops:
  1.5 6.0 %collective-permute-start.1 = (bf16[528,128]{1,0:T(8,128)(2,1)S(1)}, bf16[528,128]{1,0:T(8,128)(2,1)S(1)}, u32[]{:S(2)}, u32[]{:S(2)}) collective-permute-start(bf16[528,128]{1,0:T(8,128)(2,1)S(1)} %pack.1.packed_ref.refs_3_), channel_id=1, source_target_pairs={{0,16},{1,2},{2,1},{3,4},{4,3},{5,6},{6,5},{7,8},{8,7},{9,10},{10,... | collective-permute-start | bytes 405512 | tf_op jit(solution)/shard_map/ppermute | solution.py:374
  4.5 3.0 %collective-permute-start = (bf16[528,128]{1,0:T(8,128)(2,1)S(1)}, bf16[528,128]{1,0:T(8,128)(2,1)S(1)}, u32[]{:S(2)}, u32[]{:S(2)}) collective-permute-start(bf16[528,128]{1,0:T(8,128)(2,1)S(1)} %pack.1.packed_ref.refs_3_), channel_id=1, source_target_pairs={{0,1},{1,0},{2,3},{3,2},{4,5},{5,4},{6,7},{7,6},{8,9},{9,8},{10,11... | collective-permute-start | bytes 405512 | tf_op jit(solution)/shard_map/ppermute | solution.py:374
  8.1 1.4 %collective-permute-start.2 = (f32[72,128]{1,0:T(8,128)S(1)}, f32[72,128]{1,0:T(8,128)S(1)}, u32[]{:S(2)}, u32[]{:S(2)}) collective-permute-start(f32[72,128]{1,0:T(8,128)S(1)} %get-tuple-element.19), channel_id=1, source_target_pairs={{0,1},{1,0},{2,3},{3,2},{4,5},{5,4},{6,7},{7,6},{8,9},{9,8},{10,11... | collective-permute-start | bytes 110600 | tf_op jit(solution)/shard_map/ppermute | solution.py:400
  9.5 5.3 %collective-permute-start.5 = (f32[72,128]{1,0:T(8,128)S(1)}, f32[72,128]{1,0:T(8,128)S(1)}, u32[]{:S(2)}, u32[]{:S(2)}) collective-permute-start(f32[72,128]{1,0:T(8,128)S(1)} %add.15), channel_id=1, source_target_pairs={{0,19},{1,18},{2,17},{3,16},{4,23},{5,22},{6,21},{7,20},{8,27},{9,... | collective-permute-start | bytes 110600 | tf_op jit(solution)/shard_map/ppermute | solution.py:400
  13.0 3.4 %collective-permute-start.4 = (f32[72,128]{1,0:T(8,128)S(1)}, f32[72,128]{1,0:T(8,128)S(1)}, u32[]{:S(2)}, u32[]{:S(2)}) collective-permute-start(f32[72,128]{1,0:T(8,128)S(1)} %add.15), channel_id=1, source_target_pairs={{0,3},{1,2},{2,1},{3,0},{4,7},{5,6},{6,5},{7,4},{8,11},{9,10},{10,... | collective-permute-start | bytes 110600 | tf_op jit(solution)/shard_map/ppermute | solution.py:400
  13.0 3.4 %collective-permute-start.3 = (f32[72,128]{1,0:T(8,128)S(1)}, f32[72,128]{1,0:T(8,128)S(1)}, u32[]{:S(2)}, u32[]{:S(2)}) collective-permute-start(f32[72,128]{1,0:T(8,128)S(1)} %add.15), channel_id=1, source_target_pairs={{0,17},{1,16},{2,19},{3,18},{4,21},{5,20},{6,23},{7,22},{8,25},{9,... | collective-permute-start | bytes 110600 | tf_op jit(solution)/shard_map/ppermute | solution.py:400
  16.4 3.4 %collective-permute-start.6 = (f32[72,128]{1,0:T(8,128)S(1)}, f32[72,128]{1,0:T(8,128)S(1)}, u32[]{:S(2)}, u32[]{:S(2)}) collective-permute-start(f32[72,128]{1,0:T(8,128)S(1)} %add_add_fusion), channel_id=1, source_target_pairs={{0,5},{1,4},{2,7},{3,6},{4,1},{5,0},{6,3},{7,2},{8,13},{9,12},{10,... | collective-permute-start | bytes 110600 | tf_op jit(solution)/shard_map/ppermute | solution.py:400
  19.8 4.3 %collective-permute-start.7 = (f32[72,128]{1,0:T(8,128)S(1)}, f32[72,128]{1,0:T(8,128)S(1)}, u32[]{:S(2)}, u32[]{:S(2)}) collective-permute-start(f32[72,128]{1,0:T(8,128)S(1)} %add.19.refs_0_), channel_id=1, source_target_pairs={{0,9},{1,8},{2,11},{3,10},{4,13},{5,12},{6,15},{7,14},{8,1},{9,0},... | collective-permute-start | bytes 110600 | tf_op jit(solution)/shard_map/ppermute | solution.py:400
